TPU v7x, 32 devices: a whole 2x2x4 slice. The times are simulated.
32 devices in a mesh: page: 4 (over z), blk: 8 (over y, x, core).
Axes of the slice: x: 2, y: 2, z: 4, core: 2. Of those that a mesh axis runs over, the one named last changes fastest.
Arguments:
- visual: bfloat16 [4, 96, 24, 768], P('page', 'blk'), may hold values from -6 to 6
- query_tokens: bfloat16 [4, 1024, 768], P('page', 'blk'), may hold values from -6 to 6
- answer_len: int32 [4], P('page'), may hold values from 5 to 1024, as said below
- attn_swin: float32 [2359296], P(('page', 'blk')), may hold values from -16 to 16
- attn_self: float32 [2359296], P(('page', 'blk')), may hold values from -16 to 16
- attn_qv: float32 [2359296], P(('page', 'blk')), may hold values from -16 to 16
- attn_vq: float32 [2359296], P(('page', 'blk')), may hold values from -16 to 16
- mlp_up: float32 [2359296], P(('page', 'blk')), may hold values from -0.21875 to 0.21875
- mlp_down: float32 [2359296], P(('page', 'blk')), may hold values from -0.15625 to 0.15625
- norm_gains: float32 [6144], P(('page', 'blk')), may hold values from 0.5 to 1.5
- visual_cot: bfloat16 [4, 96, 24, 768], P('page', 'blk'), may hold values from -6 to 6
- query_cot: bfloat16 [4, 1024, 768], P('page', 'blk'), may hold values from -6 to 6
Outputs:
- visual_out: bfloat16 [4, 96, 24, 768], P('page', 'blk')
- query_out: bfloat16 [4, 1024, 768], P('page', 'blk')
- visual_grad: float32 [4, 96, 24, 768], P('page', 'blk')
- query_grad: float32 [4, 1024, 768], P('page', 'blk')
- swin_grad: float32 [2359296], P(('page', 'blk'))
- self_grad: float32 [2359296], P(('page', 'blk'))
- cross_qv_grad: float32 [2359296], P(('page', 'blk'))
- cross_vq_grad: float32 [2359296], P(('page', 'blk'))
- mlp_up_grad: float32 [2359296], P(('page', 'blk'))
- mlp_down_grad: float32 [2359296], P(('page', 'blk'))
- gains_grad: float32 [6144], P(('page', 'blk'))
Inputs may be any that keep to these rules, and one draw needn't show every extreme that they name: `answer_len`: some page has all 1024 slots live.
All inputs are finite; a program needn't handle non-finite values.
Results may differ from a plain program's by a relative error of at most 0.02.
The roundings to bfloat16 on the way count: a program that leaves them out, or rounds other values in their place, can miss the bound.
Values may be sent and summed in bfloat16 or wider, within the bound.
No kernel may reach another device: no remote copies, remote signals or barrier semaphores. Data moves between devices by JAX's collectives and lax.ppermute only.
A program may use at most 256 MiB of HBM per device.

v0:
```python
import jax
import jax.numpy as jnp
from jax import lax
from jax.sharding import PartitionSpec as P

D = 768
HEADS = 12
HD = 64
FF = 3072


EPS = 1e-05
NEG = -1e30


def extended(value, sides, width):
    for axis, dim in sides:
        count, length = (lax.axis_size(axis), value.shape[dim])
        up = [(i, (i + 1) % count) for i in range(count - 1)]
        down = [(j, i) for i, j in up]
        last = lax.slice_in_dim(value, length - width, length, axis=dim)
        first = lax.slice_in_dim(value, 0, width, axis=dim)
        before = lax.ppermute(last, axis, up)
        after = lax.ppermute(first, axis, down)
        value = jnp.concatenate([before, value, after], axis=dim)
    return value


def merged(value, axis, combine):
    everything = jax.tree.map(
        lambda part, kind: lax.all_gather(part.astype(kind), axis),
        value,
        (jnp.bfloat16, jnp.bfloat16),
    )

    def take(k):
        return jax.tree.map(lambda part, own: part[k].astype(own.dtype), everything, value)

    return lax.fori_loop(
        1, lax.axis_size(axis), lambda k, so_far: combine(so_far, take(k)), take(0)
    )


def layer_norm(rows_in, gain_row):
    centre = jnp.mean(rows_in, axis=-1, keepdims=True)
    centred = rows_in - centre
    spread = jnp.mean(centred * centred, axis=-1, keepdims=True)
    return centred * lax.rsqrt(spread + EPS) * gain_row


def split_block(flat):
    mats = flat.reshape(4, D, D)
    return (jnp.concatenate([mats[0], mats[1], mats[2]], axis=1), mats[3])


def heads_of(matrix):
    return matrix.reshape(matrix.shape[:-1] + (HEADS, HD))


def head_cols(matrix, head_index):
    return lax.dynamic_slice_in_dim(matrix, head_index * HD, HD, 1)


def times_transpose(left, right):
    return lax.dot_general(
        left, right, (((1,), (1,)), ((), ())), preferred_element_type=jnp.float32
    )


def outer_sum(left, right):
    return lax.dot_general(
        left, right, (((0,), (0,)), ((), ())), preferred_element_type=jnp.float32
    )


def scores_of(queries, key_rows, allowed):
    products = jnp.einsum(
        "wqhd,wkhd->whqk", queries, key_rows, preferred_element_type=jnp.float32
    ) * HD ** (-0.5)
    return jnp.where(allowed[:, None], products, NEG)


def attend_forward(queries, key_rows, value_rows, allowed):
    scores = scores_of(queries, key_rows, allowed)
    highest = jnp.max(scores, axis=-1, keepdims=True)
    raised = jnp.exp(scores - highest)
    totals = jnp.sum(raised, axis=-1, keepdims=True)
    chances = (raised / totals).astype(jnp.bfloat16)
    mixed = jnp.einsum("whqk,wkhd->wqhd", chances, value_rows, preferred_element_type=jnp.float32)
    return (mixed, highest + jnp.log(totals))


def attend_backward(queries, key_rows, value_rows, allowed, log_totals, grad_out):
    scores = scores_of(queries, key_rows, allowed)
    chances = jnp.exp(scores - log_totals)
    grad_values = jnp.einsum(
        "whqk,wqhd->wkhd",
        chances.astype(jnp.bfloat16),
        grad_out,
        preferred_element_type=jnp.float32,
    )
    grad_chances = jnp.einsum(
        "wqhd,wkhd->whqk", grad_out, value_rows, preferred_element_type=jnp.float32
    )
    centres = jnp.sum(chances * grad_chances, axis=-1, keepdims=True)
    grad_scores = (chances * (grad_chances - centres)).astype(jnp.bfloat16)
    factor = HD ** (-0.5)
    grad_queries = (
        jnp.einsum("whqk,wkhd->wqhd", grad_scores, key_rows, preferred_element_type=jnp.float32)
        * factor
    )
    grad_keys = (
        jnp.einsum("whqk,wqhd->wkhd", grad_scores, queries, preferred_element_type=jnp.float32)
        * factor
    )
    return (grad_queries, grad_keys, grad_values)


def query_windows(grid_rows, half_rows):
    window = 2 * half_rows
    channels = grid_rows.shape[-1]
    across = grid_rows.shape[1] // window
    rolled = jnp.roll(grid_rows, -half_rows, axis=1)
    shaped = rolled.reshape(2, half_rows, across, window, channels).transpose(0, 2, 1, 3, 4)
    return shaped.reshape(2 * across, half_rows * window, channels)


def key_windows(grid_rows, half_rows):
    window = 2 * half_rows
    channels = grid_rows.shape[-1]
    across = grid_rows.shape[1] // window
    rolled = jnp.roll(grid_rows, -half_rows, axis=1)
    shaped = rolled.reshape(2, window, across, window, channels).transpose(0, 2, 1, 3, 4)
    return shaped.reshape(2 * across, window * window, channels)


def unwindow_queries(windows_in, half_rows):
    window = 2 * half_rows
    across = windows_in.shape[0] // 2
    channels = windows_in.shape[-1]
    shaped = windows_in.reshape(2, across, half_rows, window, channels).transpose(0, 2, 1, 3, 4)
    return jnp.roll(shaped.reshape(window, across * window, channels), half_rows, axis=1)


def unwindow_keys(windows_in, half_rows):
    window = 2 * half_rows
    across = windows_in.shape[0] // 2
    channels = windows_in.shape[-1]
    shaped = windows_in.reshape(2, across, window, window, channels).transpose(0, 2, 1, 3, 4)
    return jnp.roll(shaped.reshape(2 * window, across * window, channels), half_rows, axis=1)


def on_device(
    visual,
    query_tokens,
    answer_len,
    attn_swin,
    attn_self,
    attn_qv,
    attn_vq,
    mlp_up,
    mlp_down,
    norm_gains,
    visual_cot,
    query_cot,
):
    bf16 = jnp.bfloat16
    f32 = jnp.float32
    blk_count = lax.axis_size("blk")
    blk_here = lax.axis_index("blk")
    page_count = lax.axis_size("page")
    gathered = (
        lax.all_gather(attn_swin.astype(bf16), ("page", "blk"), axis=0, tiled=True),
        lax.all_gather(attn_self.astype(bf16), ("page", "blk"), axis=0, tiled=True),
        lax.all_gather(attn_qv.astype(bf16), ("page", "blk"), axis=0, tiled=True),
        lax.all_gather(attn_vq.astype(bf16), ("page", "blk"), axis=0, tiled=True),
        lax.all_gather(mlp_up.astype(bf16), ("page", "blk"), axis=0, tiled=True),
        lax.all_gather(mlp_down.astype(bf16), ("page", "blk"), axis=0, tiled=True),
        lax.all_gather(norm_gains.astype(bf16), ("page", "blk"), axis=0, tiled=True),
    )
    swin_in, swin_out = split_block(gathered[0])
    self_in, self_out = split_block(gathered[1])
    qv_in, qv_out = split_block(gathered[2])
    vq_in, vq_out = split_block(gathered[3])
    w_up = gathered[4].reshape(D, FF)
    w_down = gathered[5].reshape(FF, D)
    gain_rows = gathered[6].astype(f32).reshape(8, D)
    rows_here = visual.shape[1]
    cols_all = visual.shape[2]
    half_rows = rows_here // 2
    tokens = rows_here * cols_all
    vis_in = visual[0].astype(f32).reshape(tokens, D)
    normed, norm_back_one = jax.vjp(layer_norm, vis_in, gain_rows[0])
    normed_low = normed.astype(bf16)
    q_swin = jnp.dot(normed_low, swin_in[:, :D], preferred_element_type=f32).astype(bf16)
    kv_swin = jnp.dot(normed_low, swin_in[:, D:], preferred_element_type=f32).astype(bf16)
    ext_kv = extended(kv_swin.reshape(rows_here, cols_all, 2 * D), (("blk", 0),), half_rows)
    base_tag = (jnp.arange(cols_all) < half_rows).astype(jnp.int32)
    own_flag = (blk_here * rows_here + jnp.arange(rows_here) < half_rows).astype(jnp.int32)
    own_tag = base_tag[None, :] + 2 * own_flag[:, None]
    last_flag = (blk_here == blk_count - 1).astype(jnp.int32)
    top_tag = jnp.broadcast_to(base_tag[None, :], (half_rows, cols_all))
    bottom_tag = jnp.broadcast_to((base_tag + 2 * last_flag)[None, :], (half_rows, cols_all))
    ext_tag = jnp.concatenate([top_tag, own_tag, bottom_tag], axis=0)
    win_q = heads_of(query_windows(q_swin.reshape(rows_here, cols_all, D), half_rows))
    win_kv = key_windows(ext_kv, half_rows)
    win_k = heads_of(win_kv[..., :D])
    win_v = heads_of(win_kv[..., D:])
    q_tags = query_windows(own_tag[..., None], half_rows)[..., 0]
    k_tags = key_windows(ext_tag[..., None], half_rows)[..., 0]
    win_mask = q_tags[:, :, None] == k_tags[:, None, :]
    swin_att, swin_lse = attend_forward(win_q, win_k, win_v, win_mask)
    window_count = swin_att.shape[0]
    swin_low = (
        unwindow_queries(swin_att.reshape(window_count, -1, D), half_rows)
        .reshape(tokens, D)
        .astype(bf16)
    )
    visual_one = vis_in + jnp.dot(swin_low, swin_out, preferred_element_type=f32)
    query_in = query_tokens[0].astype(f32)
    q_rows = query_in.shape[0]
    q_normed, norm_back_two = jax.vjp(layer_norm, query_in, gain_rows[1])
    q_normed_low = q_normed.astype(bf16)
    self_q = jnp.dot(q_normed_low, self_in[:, :D], preferred_element_type=f32).astype(bf16)
    self_kv = jnp.dot(q_normed_low, self_in[:, D:], preferred_element_type=f32).astype(bf16)
    self_kv_all = lax.all_gather(self_kv, "blk", axis=0, tiled=True)
    slots_all = self_kv_all.shape[0]
    slot_rows = blk_here * q_rows + jnp.arange(q_rows)
    slot_keys = jnp.arange(slots_all)
    live_keys = slot_keys < answer_len[0]
    self_mask = ((slot_keys[None, :] <= slot_rows[:, None]) & live_keys[None, :])[None]
    self_heads_q = heads_of(self_q)[None]
    self_heads_k = heads_of(self_kv_all[:, :D])[None]
    self_heads_v = heads_of(self_kv_all[:, D:])[None]
    self_att, self_lse = attend_forward(self_heads_q, self_heads_k, self_heads_v, self_mask)
    self_low = self_att[0].reshape(q_rows, D).astype(bf16)
    query_one = query_in + jnp.dot(self_low, self_out, preferred_element_type=f32)
    vis_normed, norm_back_three = jax.vjp(layer_norm, visual_one, gain_rows[2])
    qry_normed, norm_back_four = jax.vjp(layer_norm, query_one, gain_rows[3])
    vis_low = vis_normed.astype(bf16)
    qry_low = qry_normed.astype(bf16)
    cross_q_a = jnp.dot(qry_low, qv_in[:, :D], preferred_element_type=f32).astype(bf16)
    cross_kv_a = jnp.dot(vis_low, qv_in[:, D:], preferred_element_type=f32).astype(bf16)
    cross_q_b = jnp.dot(vis_low, vq_in[:, :D], preferred_element_type=f32).astype(bf16)
    cross_kv_b = jnp.dot(qry_low, vq_in[:, D:], preferred_element_type=f32).astype(bf16)
    kv_b_all, q_a_all = (
        lax.all_gather(cross_kv_b, "blk", axis=0, tiled=True),
        lax.all_gather(cross_q_a, "blk", axis=0, tiled=True),
    )
    vq_mask = live_keys[None, None, :]
    head_range = jnp.arange(HEADS)

    def vq_head(head_index):
        mixed, log_totals = attend_forward(
            head_cols(cross_q_b, head_index)[None, :, None],
            head_cols(kv_b_all, head_index)[None, :, None],
            head_cols(kv_b_all, HEADS + head_index)[None, :, None],
            vq_mask,
        )
        return (mixed[0, :, 0], log_totals[0, 0, :, 0])

    vq_att, vq_lse = lax.map(vq_head, head_range)
    vq_low = vq_att.transpose(1, 0, 2).reshape(tokens, D).astype(bf16)
    visual_two = visual_one + jnp.dot(vq_low, vq_out, preferred_element_type=f32)
    everything = jnp.ones((1, 1, 1), dtype=jnp.bool_)

    def qv_scores(head_index):
        rows_q = head_cols(q_a_all, head_index)
        return scores_of(
            rows_q[None, :, None], head_cols(cross_kv_a, head_index)[None, :, None], everything
        )[0, 0]

    def qv_stats(head_index):
        scores = qv_scores(head_index)
        highest = jnp.max(scores, axis=-1)
        return (highest, jnp.sum(jnp.exp(scores - highest[:, None]), axis=-1))

    local_peaks, local_totals = lax.map(qv_stats, head_range)

    def merge_stats(earlier, later):
        highest = jnp.maximum(earlier[0], later[0])
        return (
            highest,
            earlier[1] * jnp.exp(earlier[0] - highest) + later[1] * jnp.exp(later[0] - highest),
        )

    peaks, totals = merged((local_peaks, local_totals), "blk", merge_stats)
    qv_lse = peaks + jnp.log(totals)

    def one_head(head_index):
        scores = qv_scores(head_index)
        row_lse = qv_lse[head_index]
        chances = jnp.exp(scores - row_lse[:, None]).astype(bf16)
        return jnp.dot(
            chances, head_cols(cross_kv_a, HEADS + head_index), preferred_element_type=f32
        )

    qv_att = lax.psum_scatter(
        lax.map(one_head, head_range).transpose(1, 0, 2).reshape(lax.axis_size("blk") * q_rows, D),
        "blk",
        scatter_dimension=0,
        tiled=True,
    )
    qv_low = qv_att.astype(bf16)
    query_two = query_one + jnp.dot(qv_low, qv_out, preferred_element_type=f32)
    mlp_normed, norm_back_five = jax.vjp(layer_norm, visual_two, gain_rows[4])
    mlp_low = mlp_normed.astype(bf16)
    hidden_pre = jnp.dot(mlp_low, w_up, preferred_element_type=f32)
    hidden_act, gelu_back = jax.vjp(jax.nn.gelu, hidden_pre)
    act_low = hidden_act.astype(bf16)
    visual_three = visual_two + jnp.dot(act_low, w_down, preferred_element_type=f32)
    grad_three = visual_cot[0].astype(f32).reshape(tokens, D)
    grad_mlp_out = grad_three.astype(bf16)
    grad_act = times_transpose(grad_mlp_out, w_down)
    grad_pre_low = gelu_back(grad_act)[0].astype(bf16)
    grad_vis_two, gain_five_grad = norm_back_five(times_transpose(grad_pre_low, w_up))
    grad_two = grad_three + grad_vis_two
    grad_vq_out = grad_two.astype(bf16)
    grad_vq_att = times_transpose(grad_vq_out, vq_out).astype(bf16)

    def vq_back(head_index):
        grad_q, grad_k, grad_v = attend_backward(
            head_cols(cross_q_b, head_index)[None, :, None],
            head_cols(kv_b_all, head_index)[None, :, None],
            head_cols(kv_b_all, HEADS + head_index)[None, :, None],
            vq_mask,
            vq_lse[head_index][None, None, :, None],
            head_cols(grad_vq_att, head_index)[None, :, None],
        )
        return (grad_q[0, :, 0], grad_k[0, :, 0], grad_v[0, :, 0])

    vq_grad_q, vq_grad_k, vq_grad_v = lax.map(vq_back, head_range)
    grad_q_b = vq_grad_q.transpose(1, 0, 2).reshape(tokens, D).astype(bf16)
    grad_kv_b_all = jnp.concatenate(
        [
            vq_grad_k.transpose(1, 0, 2).reshape(slots_all, D),
            vq_grad_v.transpose(1, 0, 2).reshape(slots_all, D),
        ],
        axis=1,
    )
    query_cot_in = query_cot[0].astype(f32)
    grad_qv_out = query_cot_in.astype(bf16)
    grad_qv_att = times_transpose(grad_qv_out, qv_out).astype(bf16)
    grad_qv_all = lax.all_gather(grad_qv_att, "blk", axis=0, tiled=True)

    def qv_parts(head_index):
        scores = qv_scores(head_index)
        chances = jnp.exp(scores - qv_lse[head_index][:, None])
        grad_chances = times_transpose(
            head_cols(grad_qv_all, head_index), head_cols(cross_kv_a, HEADS + head_index)
        )
        return (chances, grad_chances)

    def qv_centre(head_index):
        chances, grad_chances = qv_parts(head_index)
        return jnp.sum(chances * grad_chances, axis=-1)

    centres = lax.psum(lax.map(qv_centre, head_range), "blk")

    def qv_back(head_index):
        chances, grad_chances = qv_parts(head_index)
        grad_scores = (chances * (grad_chances - centres[head_index][:, None])).astype(bf16)
        factor = HD ** (-0.5)
        grad_q = (
            jnp.dot(grad_scores, head_cols(cross_kv_a, head_index), preferred_element_type=f32)
            * factor
        )
        grad_k = outer_sum(grad_scores, head_cols(q_a_all, head_index)) * factor
        grad_v = outer_sum(chances.astype(bf16), head_cols(grad_qv_all, head_index))
        return (grad_q, grad_k, grad_v)

    qv_grad_q, qv_grad_k, qv_grad_v = lax.map(qv_back, head_range)
    grad_q_a_all = qv_grad_q.transpose(1, 0, 2).reshape(slots_all, D)
    grad_kv_a = jnp.concatenate(
        [
            qv_grad_k.transpose(1, 0, 2).reshape(tokens, D),
            qv_grad_v.transpose(1, 0, 2).reshape(tokens, D),
        ],
        axis=1,
    ).astype(bf16)
    grad_kv_b, grad_q_a = (
        lax.psum_scatter(grad_kv_b_all, "blk", scatter_dimension=0, tiled=True),
        lax.psum_scatter(grad_q_a_all, "blk", scatter_dimension=0, tiled=True),
    )
    grad_kv_b = grad_kv_b.astype(bf16)
    grad_q_a = grad_q_a.astype(bf16)
    grad_vis_norm = times_transpose(grad_kv_a, qv_in[:, D:]) + times_transpose(
        grad_q_b, vq_in[:, :D]
    )
    grad_qry_norm = times_transpose(grad_q_a, qv_in[:, :D]) + times_transpose(
        grad_kv_b, vq_in[:, D:]
    )
    grad_vis_part, gain_three_grad = norm_back_three(grad_vis_norm)
    grad_qry_part, gain_four_grad = norm_back_four(grad_qry_norm)
    grad_one = grad_two + grad_vis_part
    grad_query_one = query_cot_in + grad_qry_part
    grad_self_out = grad_query_one.astype(bf16)
    grad_self_att = times_transpose(grad_self_out, self_out).astype(bf16)
    self_grad_q, self_grad_k, self_grad_v = attend_backward(
        self_heads_q, self_heads_k, self_heads_v, self_mask, self_lse, heads_of(grad_self_att)[None]
    )
    grad_self_kv_all = jnp.concatenate(
        [self_grad_k[0].reshape(slots_all, D), self_grad_v[0].reshape(slots_all, D)], axis=1
    )
    grad_self_kv = lax.psum_scatter(
        grad_self_kv_all, "blk", scatter_dimension=0, tiled=True
    ).astype(bf16)
    grad_self_q = self_grad_q[0].reshape(q_rows, D).astype(bf16)
    grad_q_norm = times_transpose(grad_self_q, self_in[:, :D]) + times_transpose(
        grad_self_kv, self_in[:, D:]
    )
    grad_q_part, gain_two_grad = norm_back_two(grad_q_norm)
    query_grad = grad_query_one + grad_q_part
    grad_swin_out = grad_one.astype(bf16)
    grad_swin_att = (
        times_transpose(grad_swin_out, swin_out).astype(bf16).reshape(rows_here, cols_all, D)
    )
    win_grad = heads_of(query_windows(grad_swin_att, half_rows))
    swin_grad_q, swin_grad_k, swin_grad_v = attend_backward(
        win_q, win_k, win_v, win_mask, swin_lse, win_grad
    )
    grad_q_swin = (
        unwindow_queries(swin_grad_q.reshape(window_count, -1, D), half_rows)
        .reshape(tokens, D)
        .astype(bf16)
    )
    grad_ext = unwindow_keys(
        jnp.concatenate(
            [swin_grad_k.reshape(window_count, -1, D), swin_grad_v.reshape(window_count, -1, D)],
            axis=-1,
        ),
        half_rows,
    )
    rim_rows = jnp.concatenate([grad_ext[:half_rows], grad_ext[rows_here + half_rows :]], axis=0)
    returned = extended(rim_rows.astype(jnp.bfloat16), (("blk", 0),), half_rows).astype(
        rim_rows.dtype
    )
    grad_kv_swin = grad_ext[half_rows : rows_here + half_rows] + jnp.concatenate(
        [returned[:half_rows], returned[rows_here + half_rows :]], axis=0
    )
    grad_kv_swin = grad_kv_swin.reshape(tokens, 2 * D).astype(bf16)
    grad_norm_in = times_transpose(grad_q_swin, swin_in[:, :D]) + times_transpose(
        grad_kv_swin, swin_in[:, D:]
    )
    grad_vis_in, gain_one_grad = norm_back_one(grad_norm_in)
    visual_grad = grad_one + grad_vis_in
    patch_blank = jnp.zeros((tokens, D), bf16)
    slot_blank = jnp.zeros((q_rows, D), bf16)

    def on_patches(rows_in):
        return jnp.concatenate([rows_in, slot_blank], axis=0)

    def on_slots(rows_in):
        return jnp.concatenate([patch_blank, rows_in], axis=0)

    left_mats = [
        [on_patches(normed_low), on_slots(q_normed_low), on_slots(qry_low), on_patches(vis_low)],
        [on_patches(normed_low), on_slots(q_normed_low), on_patches(vis_low), on_slots(qry_low)],
        [on_patches(normed_low), on_slots(q_normed_low), on_patches(vis_low), on_slots(qry_low)],
        [on_patches(swin_low), on_slots(self_low), on_slots(qv_low), on_patches(vq_low)],
    ]
    right_mats = [
        [on_patches(grad_q_swin), on_slots(grad_self_q), on_slots(grad_q_a), on_patches(grad_q_b)],
        [
            on_patches(grad_kv_swin[:, :D]),
            on_slots(grad_self_kv[:, :D]),
            on_patches(grad_kv_a[:, :D]),
            on_slots(grad_kv_b[:, :D]),
        ],
        [
            on_patches(grad_kv_swin[:, D:]),
            on_slots(grad_self_kv[:, D:]),
            on_patches(grad_kv_a[:, D:]),
            on_slots(grad_kv_b[:, D:]),
        ],
        [
            on_patches(grad_swin_out),
            on_slots(grad_self_out),
            on_slots(grad_qv_out),
            on_patches(grad_vq_out),
        ],
    ]
    pair_left = jnp.stack([jnp.concatenate(entry, axis=0) for entry in left_mats], axis=1)
    pair_right = jnp.stack([jnp.concatenate(entry, axis=0) for entry in right_mats], axis=1)
    mlp_cols = mlp_low.reshape(tokens, page_count, D // page_count)
    act_cols = act_low.reshape(tokens, page_count, FF // page_count)
    pre_copies = jnp.broadcast_to(grad_pre_low[:, None, :], (tokens, page_count, FF))
    out_copies = jnp.broadcast_to(grad_mlp_out[:, None, :], (tokens, page_count, D))
    traded = (
        lax.all_to_all(pair_left, "page", split_axis=1, concat_axis=0, tiled=True),
        lax.all_to_all(pair_right, "page", split_axis=1, concat_axis=0, tiled=True),
        lax.all_to_all(mlp_cols, "page", split_axis=1, concat_axis=0, tiled=True),
        lax.all_to_all(act_cols, "page", split_axis=1, concat_axis=0, tiled=True),
        lax.all_to_all(pre_copies, "page", split_axis=1, concat_axis=0, tiled=True),
        lax.all_to_all(out_copies, "page", split_axis=1, concat_axis=0, tiled=True),
    )
    row_span = tokens + q_rows
    left_all = traded[0].reshape(page_count, 4, row_span, D)
    right_all = traded[1].reshape(page_count, 4, row_span, D)
    block_grads = jnp.einsum("pbrd,pbre->bde", left_all, right_all, preferred_element_type=f32)
    up_part = outer_sum(traded[2].reshape(-1, D // page_count), traded[4].reshape(-1, FF))
    down_part = outer_sum(traded[3].reshape(-1, FF // page_count), traded[5].reshape(-1, D))
    shares = (
        lax.psum_scatter(block_grads[0].reshape(-1), "blk", scatter_dimension=0, tiled=True),
        lax.psum_scatter(block_grads[1].reshape(-1), "blk", scatter_dimension=0, tiled=True),
        lax.psum_scatter(block_grads[2].reshape(-1), "blk", scatter_dimension=0, tiled=True),
        lax.psum_scatter(block_grads[3].reshape(-1), "blk", scatter_dimension=0, tiled=True),
        lax.psum_scatter(up_part.reshape(-1), "blk", scatter_dimension=0, tiled=True),
        lax.psum_scatter(down_part.reshape(-1), "blk", scatter_dimension=0, tiled=True),
    )
    gain_block = jnp.concatenate(
        [
            jnp.stack(
                [gain_one_grad, gain_two_grad, gain_three_grad, gain_four_grad, gain_five_grad]
            ),
            jnp.zeros((3, D), f32),
        ],
        axis=0,
    )
    gain_share = lax.psum_scatter(
        gain_block.reshape(-1), ("page", "blk"), scatter_dimension=0, tiled=True
    )
    visual_out = visual_three.reshape(1, rows_here, cols_all, D).astype(bf16)
    query_out = query_two[None].astype(bf16)
    return (
        visual_out,
        query_out,
        visual_grad.reshape(1, rows_here, cols_all, D),
        query_grad[None],
        shares[0],
        shares[1],
        shares[2],
        shares[3],
        shares[4],
        shares[5],
        gain_share,
    )


def solution(mesh):
    placed = (
        P("page", "blk", None, None),
        P("page", "blk", None),
        P("page"),
        P(("page", "blk")),
        P(("page", "blk")),
        P(("page", "blk")),
        P(("page", "blk")),
        P(("page", "blk")),
        P(("page", "blk")),
        P(("page", "blk")),
        P("page", "blk", None, None),
        P("page", "blk", None),
    )
    return jax.shard_map(
        on_device,
        mesh=mesh,
        in_specs=placed,
        out_specs=(
            P("page", "blk", None, None),
            P("page", "blk", None),
            P("page", "blk", None, None),
            P("page", "blk", None),
            P(("page", "blk")),
            P(("page", "blk")),
            P(("page", "blk")),
            P(("page", "blk")),
            P(("page", "blk")),
            P(("page", "blk")),
            P(("page", "blk")),
        ),
        check_vma=False,
    )
```

profile of v0, /device:TPU:0, one launch (start us, length us, event | category | flops | bytes accessed | tf_op | source)
XLA Modules:
  0.0 1992.2 jit_solution(13660361360742526368)
XLA Ops:
  13.2 42.2 %all-reduce = bf16[6144]{0:T(1024)(128)(2,1)S(1)} all-reduce(bf16[6144]{0:T(1024)(128)(2,1)S(1)} %dynamic-update-slice), channel_id=1, replica_groups=mesh['page'=4,'blk'=8] {'page','blk'}, use_global_device_ids=true, to_apply=%add | all-reduce | flops 6144 | bytes 24576
  58.8 19.0 all-gather.17.cloned.1.call-done
  106.5 55.0 %all-gather.15.cloned.1.call-done = bf16[2359296]{0:T(1024)(128)(2,1)} async-done(((bf16[73728]{0:T(1024)(128)(2,1)}), bf16[2359296]{0:T(1024)(128)(2,1)}) %all-gather.15.cloned.1.call-update) | async-done | bytes 4718608 | tf_op jit(solution)/shard_map/all_gather | solution.py:173
  184.6 44.0 %all-gather.29.cloned.1.call-done = bf16[2359296]{0:T(1024)(128)(2,1)} async-done(((bf16[73728]{0:T(1024)(128)(2,1)}), bf16[2359296]{0:T(1024)(128)(2,1)}) %all-gather.29.cloned.1.call-update) | async-done | bytes 4718608 | tf_op jit(solution)/shard_map/all_gather | solution.py:175
  243.2 18.9 all-gather.19.cloned.1.call-done
  279.8 49.4 %all-gather.21.cloned.1.call-done = bf16[2359296]{0:T(1024)(128)(2,1)} async-done(((bf16[73728]{0:T(1024)(128)(2,1)}), bf16[2359296]{0:T(1024)(128)(2,1)}) %all-gather.21.cloned.1.call-update) | async-done | bytes 4718608 | tf_op jit(solution)/shard_map/all_gather | solution.py:176
  373.2 21.7 %all-gather.27.cloned.1.call-done = bf16[2359296]{0:T(1024)(128)(2,1)} async-done(((bf16[73728]{0:T(1024)(128)(2,1)}), bf16[2359296]{0:T(1024)(128)(2,1)}) %all-gather.27.cloned.1.call-update) | async-done | bytes 4718608 | tf_op jit(solution)/shard_map/all_gather | solution.py:178
  394.9 9.2 reshape.908
  404.1 56.7 %all-gather.25.cloned.1.call-done = bf16[2359296]{0:T(1024)(128)(2,1)} async-done(((bf16[73728]{0:T(1024)(128)(2,1)}), bf16[2359296]{0:T(1024)(128)(2,1)}) %all-gather.25.cloned.1.call-update) | async-done | bytes 4718608 | tf_op jit(solution)/shard_map/all_gather | solution.py:177
  525.0 35.9 %while.98 = (s32[]{:T(128)}, bf16[12,1024]{1,0:T(8,128)(2,1)S(1)}, bf16[12,1024]{1,0:T(8,128)(2,1)S(1)}, s32[12]{0:T(128)S(1)}, bf16[1024,768]{1,0:T(8,128)(2,1)}, /*index=5*/bf16[288,1536]{1,0:T(8,128)(2,1)}, s32[1]{0:T(128)}) while((s32[]{:T(128)}, bf16[12,1024]{1,0:T(8,128)(2,1)S(1)}, bf16[12,1024]{1,0:T(8,128)(2,1)S(1)}, ...), condition=%wide.region_21.22_spmd.clone, body=%wide.region_18.21_spmd.sunk.clone | while | flops 38926344 | bytes 2724016 | solution.py:278
  560.9 9.1 all-gather.3
  581.9 75.3 %while.100 = (s32[]{:T(128)}, f32[12,1024,64]{1,2,0:T(8,128)}, s32[12]{0:T(128)S(1)}, bf16[1024,768]{1,0:T(8,128)(2,1)}, bf16[288,1536]{1,0:T(8,128)(2,1)}, /*index=5*/f32[12,1024]{1,0:T(8,128)}) while((s32[]{:T(128)}, f32[12,1024,64]{1,2,0:T(8,128)}, s32[12]{0:T(128)S(1)}, bf16[1024,768]{1,0:T(8,128)(2,1)}, ...), condition=%wide.region_25.26_spmd.clone, body=%wide.region_24.25_spmd.sunk.clone | while | flops 76382224 | bytes 684792 | solution.py:299
  660.8 82.4 %while.101 = (s32[]{:T(128)}, f32[12,1024]{1,0:T(8,128)S(1)}, s32[12]{0:T(128)S(1)}, bf16[1024,768]{1,0:T(8,128)(2,1)}, bf16[288,1536]{1,0:T(8,128)(2,1)}, /*index=5*/f32[12,1024]{1,0:T(8,128)}, bf16[1024,768]{1,0:T(8,128)(2,1)}) while((s32[]{:T(128)}, f32[12,1024]{1,0:T(8,128)S(1)}, s32[12]{0:T(128)S(1)}, ...), condition=%wide.region_31.32_spmd.clone, body=%wide.region_29.31_spmd.sunk.clone | while | flops 76676104 | bytes 3055880 | solution.py:358
  743.2 25.1 %psum.7 = f32[12,1024]{1,0:T(8,128)} all-reduce(f32[12,1024]{1,0:T(8,128)S(1)} %get-tuple-element.398), channel_id=1, replica_groups=mesh['page'=4,'blk'=8] {'blk'}, use_global_device_ids=true, to_apply=%region_32.33 | all-reduce | flops 12288 | bytes 98304 | tf_op jit(solution)/shard_map/psum | solution.py:358
  768.4 87.8 %while.103 = (s32[]{:T(128)}, bf16[12,288,64]{1,2,0:T(8,128)(2,1)S(1)}, f32[12,288]{1,0:T(8,128)}, s32[12]{0:T(128)S(1)}, bf16[1024,1536]{1,0:T(8,128)(2,1)}, /*...) while((s32[]{:T(128)}, bf16[12,288,64]{1,2,0:T(8,128)(2,1)S(1)}, ...), condition=%wide.region_15.16_spmd.clone.clone, body=%wide.region_12.15_spmd.clone.sunk.clone | while | flops 77857512 | bytes 4253694 | solution.py:262
  884.8 9.8 all-to-all-done.2
  903.4 158.7 %while.104 = (s32[]{:T(128)}, bf16[12,288,64]{1,2,0:T(8,128)(2,1)S(1)}, f32[12,1024,64]{1,2,0:T(8,128)}, f32[12,1024,64]{1,2,0:T(8,128)}, s32[12]{0:T(128)S(1)},...) while((s32[]{:T(128)}, ...), condition=%wide.region_37.38_spmd.clone.clone, body=%wide.region_35.37_spmd.clone.sunk.clone | while | flops 191482592 | bytes 10560940 | solution.py:332
  1090.3 154.8 %while.102 = (s32[]{:T(128)}, f32[12,1024,64]{1,2,0:T(8,128)}, bf16[12,288,64]{1,2,0:T(8,128)(2,1)}, bf16[12,288,64]{1,2,0:T(8,128)(2,1)}, s32[12]{0:T(128)S(1)}...) while((s32[]{:T(128)}, f32[12,1024,64]{1,2,0:T(8,128)}, ...), condition=%wide.region_34.35_spmd.clone, body=%wide.region_33.34_spmd.sunk.clone | while | flops 190597120 | bytes 7063336 | solution.py:372
  1280.8 16.2 reduce-scatter.7.cloned.1.call-done
  1443.2 85.0 %all-to-all-done = bf16[1664,4,768]{2,0,1:T(8,128)(2,1)} async-done(((bf16[1664,4,768]{2,0,1:T(8,128)(2,1)}), bf16[1664,4,768]{2,0,1:T(8,128)(2,1)}, u32[]{:S(2)}, u32[]{:S(2)}) %all-to-all-start) | async-done | bytes 10223648 | tf_op jit(solution)/shard_map/all_to_all | solution.py:490
  1546.2 209.8 %all-to-all-done.1 = bf16[1664,4,768]{2,0,1:T(8,128)(2,1)} async-done(((bf16[1664,4,768]{2,0,1:T(8,128)(2,1)}), bf16[1664,4,768]{2,0,1:T(8,128)(2,1)}, u32[]{:S(2)}, u32[]{:S(2)}) %all-to-all-start.1) | async-done | bytes 10223648 | tf_op jit(solution)/shard_map/all_to_all | solution.py:491
  1756.0 13.7 convolution_bitcast_fusion.3
  1800.5 38.6 %all-reduce.7 = f32[6144]{0:T(1024)S(1)} all-reduce(f32[6144]{0:T(1024)S(1)} %reshape.936), channel_id=14, replica_groups=mesh['page'=4,'blk'=8] {'page','blk'}, use_global_device_ids=true, to_apply=%region_62.63.clone | all-reduce | flops 6144 | bytes 49152
  1840.8 134.6 %all-reduce.11.cloned.1.call-done = (f32[589824]{0:T(1024)}, f32[589824]{0:T(1024)}, f32[589824]{0:T(1024)}, f32[589824]{0:T(1024)}, f32[589824]{0:T(1024)}, /*index=5*/f32[589824]{0:T(1024)}) async-done(((f32[589824]{0:T(1024)}, f32[589824]{0:T(1024)}, f32[589824]{0:T(1024)}, f32[589824]{0:T(1024)}, f32[589824]{0:T(1024)}, /*index=5*/f32[589824]{0:T(1024)}), (f32[589824]{0:T(1024)}, f32[589824]{0:T(1024)}, ...) | async-done | bytes 14155792
  (1120 shorter events, 965.5 us)
Async XLA Ops:
  7.2 70.6 %all-gather.17.cloned.1.call-start = ((), (), s32[]{:S(2)}) async-start(), calls=%async_computation.11 | async-start | bytes 4866048 | tf_op jit(solution)/shard_map/all_gather | solution.py:174
  8.9 152.6 %all-gather.15.cloned.1.call-start = ((), (), s32[]{:S(2)}) async-start(), calls=%async_computation.10 | async-start | bytes 4866048 | tf_op jit(solution)/shard_map/all_gather | solution.py:173
  10.6 218.1 %all-gather.29.cloned.1.call-start = ((), (), s32[]{:S(2)}) async-start(), calls=%async_computation.17 | async-start | bytes 4866048 | tf_op jit(solution)/shard_map/all_gather | solution.py:175
  12.3 249.8 %all-gather.19.cloned.1.call-start = ((), (), s32[]{:S(2)}) async-start(), calls=%async_computation.12 | async-start | bytes 3538944 | tf_op jit(solution)/shard_map/all_gather | solution.py:226
  86.9 242.2 %all-gather.21.cloned.1.call-start = ((), (), s32[]{:S(2)}) async-start(), calls=%async_computation.13 | async-start | bytes 4866048 | tf_op jit(solution)/shard_map/all_gather | solution.py:176
  87.7 307.2 %all-gather.27.cloned.1.call-start = ((), (), s32[]{:S(2)}) async-start(), calls=%async_computation.16 | async-start | bytes 4866048 | tf_op jit(solution)/shard_map/all_gather | solution.py:178
  89.8 786.8 %all-to-all-start.5 = ((bf16[288,4,768]{2,0,1:T(8,128)(2,1)}), bf16[288,4,768]{2,0,1:T(8,128)(2,1)}, u32[]{:S(2)}, u32[]{:S(2)}) async-start(bf16[288,4,768]{2,0,1:T(8,128)(2,1)} %broadcast_in_dim.248), calls=%async_computation.9 | async-start | bytes 3538944 | tf_op jit(solution)/shard_map/all_to_all | solution.py:495
  94.4 366.5 %all-gather.25.cloned.1.call-start = ((), (), s32[]{:S(2)}) async-start(), calls=%async_computation.15 | async-start | bytes 4866048 | tf_op jit(solution)/shard_map/all_gather | solution.py:177
  95.2 429.9 %all-gather.31.cloned.1.call-start = ((), (), s32[]{:S(2)}) async-start(), calls=%async_computation.18 | async-start | bytes 1769472 | tf_op jit(solution)/shard_map/all_gather | solution.py:248
  180.2 294.7 %collective-permute-start = (bf16[6,24,1536]{2,1,0:T(8,128)(2,1)}, bf16[6,24,1536]{2,1,0:T(8,128)(2,1)}, u32[]{:S(2)}, u32[]{:S(2)}) collective-permute-start(bf16[6,24,1536]{2,1,0:T(8,128)(2,1)} %bitcast.19), channel_id=1, source_target_pairs={{0,1},{1,2},{2,3},{3,4},{4,5},{5,6},{6,7},{8,9},{9,10},{10,11},{11... | collective-permute-start | bytes 1327112 | tf_op jit(solution)/shard_map/ppermute | solution.py:23
  183.1 291.7 %collective-permute-start.1 = (bf16[6,24,1536]{2,1,0:T(8,128)(2,1)}, bf16[6,24,1536]{2,1,0:T(8,128)(2,1)}, u32[]{:S(2)}, u32[]{:S(2)}) collective-permute-start(bf16[6,24,1536]{2,1,0:T(8,128)(2,1)} %bitcast.21), channel_id=1, source_target_pairs={{1,0},{2,1},{3,2},{4,3},{5,4},{6,5},{7,6},{9,8},{10,9},{11,10},{12... | collective-permute-start | bytes 1327112 | tf_op jit(solution)/shard_map/ppermute | solution.py:24
  279.3 381.5 %all-gather.33.cloned.1.call-start = ((), (), s32[]{:S(2)}) async-start(), calls=%async_computation.20 | async-start | bytes 1769472 | tf_op jit(solution)/shard_map/all_gather | solution.py:344
  373.0 395.3 %all-gather.23.cloned.1.call-start = ((), (), s32[]{:S(2)}) async-start(), calls=%async_computation.14 | async-start | bytes 3538944 | tf_op jit(solution)/shard_map/all_gather | solution.py:247
  524.9 739.6 %reduce-scatter.5.cloned.1.call-start = ((), (), s32[]{:S(2)}) async-start(), calls=%async_computation.19 | async-start | bytes 3538944 | tf_op jit(solution)/shard_map/reduce_scatter | solution.py:298
  876.7 17.9 all-to-all-start.2
  894.6 181.0 %all-to-all-start.4 = ((bf16[288,4,768]{2,0,1:T(8,128)(2,1)}), bf16[288,4,768]{2,0,1:T(8,128)(2,1)}, u32[]{:S(2)}, u32[]{:S(2)}) async-start(bf16[288,4,768]{2,0,1:T(8,128)(2,1)} %bitcast.490), calls=%async_computation.8 | async-start | bytes 3538944 | tf_op jit(solution)/shard_map/all_to_all | solution.py:493
  899.1 377.8 %reduce-scatter.9.cloned.1.call-start = ((), (), s32[]{:S(2)}) async-start(), calls=%async_computation.22 | async-start | bytes 7077888 | tf_op jit(solution)/shard_map/reduce_scatter | solution.py:382
  1080.9 218.5 %all-to-all-start.3 = ((bf16[288,4,3072]{2,0,1:T(8,128)(2,1)}), bf16[288,4,3072]{2,0,1:T(8,128)(2,1)}, u32[]{:S(2)}, u32[]{:S(2)}) async-start(bf16[288,4,3072]{2,0,1:T(8,128)(2,1)} %broadcast_in_dim.247), calls=%async_computation.7 | async-start | bytes 14155776 | tf_op jit(solution)/shard_map/all_to_all | solution.py:494
  1086.4 210.7 %reduce-scatter.7.cloned.1.call-start = ((), (), s32[]{:S(2)}) async-start(), calls=%async_computation.21 | async-start | bytes 3538944 | tf_op jit(solution)/shard_map/reduce_scatter | solution.py:383
  1299.4 228.8 %all-to-all-start = ((bf16[1664,4,768]{2,0,1:T(8,128)(2,1)}), bf16[1664,4,768]{2,0,1:T(8,128)(2,1)}, u32[]{:S(2)}, u32[]{:S(2)}) async-start(bf16[1664,4,768]{2,0,1:T(8,128)(2,1)} %pad_maximum_fusion), calls=%async_computation.4 | async-start | bytes 20447232 | tf_op jit(solution)/shard_map/all_to_all | solution.py:490
  1305.5 122.8 %reduce-scatter.11.cloned.1.call-start = ((), (), s32[]{:S(2)}) async-start(), calls=%async_computation.23 | async-start | bytes 7077888 | tf_op jit(solution)/shard_map/reduce_scatter | solution.py:405
  1408.6 4.9 collective-permute-start.3
  1528.2 227.9 %all-to-all-start.1 = ((bf16[1664,4,768]{2,0,1:T(8,128)(2,1)}), bf16[1664,4,768]{2,0,1:T(8,128)(2,1)}, u32[]{:S(2)}, u32[]{:S(2)}) async-start(bf16[1664,4,768]{2,0,1:T(8,128)(2,1)} %pad_maximum_fusion.1), calls=%async_computation.5 | async-start | bytes 20447232 | tf_op jit(solution)/shard_map/all_to_all | solution.py:491
  1534.1 441.2 %all-reduce.11.cloned.1.call-start = ((), (), s32[]{:S(2)}) async-start(), calls=%async_computation.24 | async-start | bytes 28311552
  (149 other events, 2697.7 us)
Sparse Core Ops, SparseCore 0:
  11.5 66.2 all-gather.16
  81.3 80.1 all-gather.14
  165.0 63.6 all-gather.28
  231.0 31.1 all-gather.18
  265.4 63.6 all-gather.20
  332.5 62.4 all-gather.26
  398.4 62.4 all-gather.24
  463.3 24.4 all-gather.30
  490.3 25.7 all-gather.32
  525.1 31.0 all-gather.22
  768.4 45.1 reduce-scatter.4
  1075.7 63.7 reduce-scatter.8
  1248.8 48.1 reduce-scatter.6
  1334.2 62.1 reduce-scatter.10
  1784.4 190.9 all-reduce.10
where the time goes:
time: 2010 us; the launch traced here: 1990 us
  waiting for transfers between devices  722 us (36%)
  matrix products  438 us (22%)
  local copies, waits for them, and re-layouts  404 us (20%)
  loops' own time  151 us (8%)
  blocking collectives  124 us (6%)
  other arithmetic  97.1 us (5%)
  starting transfers between devices  39.1 us (2%)
    all_to_all x1, waiting for transfers between devices, on_device(): lax.all_to_all(pair_right, 'page', split_axis=1, concat_axis=0, tiled=True)  210 us
    unnamed x16, waiting for transfers between devices  135 us
    dot_general x62, matrix products, scores_of(): jnp.einsum('wqhd,wkhd->whqk', queries, key_rows, preferred_element_type=j...  90 us
    all_to_all x1, waiting for transfers between devices, on_device(): lax.all_to_all(pair_left, 'page', split_axis=1, concat_axis=0, tiled=True)  85 us
    unnamed x2, blocking collectives  80.8 us
    unnamed x347, local copies, waits for them, and re-layouts  64.7 us
    dot_general x38, matrix products, times_transpose(): lax.dot_general(left, right, (((1,), (1,)), ((), ())), preferred_element_...  63.5 us
    dot_general x26, matrix products, outer_sum(): lax.dot_general(left, right, (((0,), (0,)), ((), ())), preferred_element_...  58.9 us
  transfers between devices with their start and end apart: 25, of which 13 were waited for; matrix products, arithmetic and copies ran while one was open for 44% of the time, Pallas kernels for 0%

commit v1 on v0

v1 whole, which is shorter than its diff:
```python
import jax
import jax.numpy as jnp
from jax import lax
from jax.experimental import pallas as pl
from jax.experimental.pallas import tpu as pltpu
from jax.sharding import PartitionSpec as P

D = 768
HEADS = 12
HD = 64
FF = 3072
PAIRS = HEADS // 2
PW = 2 * HD
SCALE = HD ** (-0.5)

EPS = 1e-05
NEG = -1e30

bf16 = jnp.bfloat16
f32 = jnp.float32
VMEM_LIMIT = 56 * 1024 * 1024


def nn(left, right):
    return lax.dot_general(left, right, (((1,), (0,)), ((), ())), preferred_element_type=f32)


def nt(left, right):
    return lax.dot_general(left, right, (((1,), (1,)), ((), ())), preferred_element_type=f32)


def tn(left, right):
    return lax.dot_general(left, right, (((0,), (0,)), ((), ())), preferred_element_type=f32)


def norm_parts(rows):
    centre = jnp.mean(rows, axis=-1, keepdims=True)
    centred = rows - centre
    spread = jnp.mean(centred * centred, axis=-1, keepdims=True)
    inverse = lax.rsqrt(spread + EPS)
    return centred * inverse, inverse


def norm(rows, gain):
    return norm_parts(rows)[0] * gain


def norm_back(rows, gain, grad):
    unit, inverse = norm_parts(rows)
    grad_gain = jnp.sum(grad * unit, axis=0, keepdims=True)
    scaled = grad * gain
    first = jnp.mean(scaled, axis=-1, keepdims=True)
    second = jnp.mean(scaled * unit, axis=-1, keepdims=True)
    return inverse * (scaled - first - unit * second), grad_gain


def mat(ref, index):
    count, rows, _ = ref.shape
    if count >= 4:
        each = count // 4
        return ref[index * each : (index + 1) * each].reshape(D, D)
    return ref[0, index * D : (index + 1) * D]


def lane_half(half, value, dtype):
    lanes = lax.broadcasted_iota(jnp.int32, (1, PW), 1)
    return jnp.where((lanes // HD) == half, value, 0.0).astype(dtype)


def low_half(rows):
    return lax.broadcasted_iota(jnp.int32, (rows, PW), 1) < HD


def column(table, index):
    lanes = lax.broadcasted_iota(jnp.int32, table.shape, 1)
    return jnp.sum(jnp.where(lanes == index, table, 0.0), axis=-1, keepdims=True)


def pair_cols(pair, base=0):
    return pl.ds(pl.multiple_of(base + pair * PW, PW), PW)


def softmax_rows(scores):
    highest = jnp.max(scores, axis=-1, keepdims=True)
    raised = jnp.exp(scores - highest)
    totals = jnp.sum(raised, axis=-1, keepdims=True)
    return raised * (1.0 / totals), highest + jnp.log(totals)


def call(kernel, outs, ins, scratch=(), smem=0, blocks=None, flops=0, name=None):
    def whole(value):
        zeros = (0,) * len(value.shape)
        return pl.BlockSpec(value.shape, lambda i: zeros, pipeline_mode=pl.Buffered(1))

    specs = []
    for index, value in enumerate(ins):
        if index < smem:
            specs.append(pl.BlockSpec(memory_space=pltpu.SMEM))
        elif blocks and index in blocks:
            specs.append(blocks[index])
        else:
            specs.append(whole(value))
    single = not isinstance(outs, list)
    shapes = [outs] if single else outs
    moved = sum(v.size * v.dtype.itemsize for v in list(ins) + shapes)
    result = pl.pallas_call(
        kernel,
        grid=(1,),
        out_shape=shapes,
        in_specs=specs,
        out_specs=[whole(value) for value in shapes],
        scratch_shapes=list(scratch),
        compiler_params=pltpu.CompilerParams(
            vmem_limit_bytes=VMEM_LIMIT, dimension_semantics=("arbitrary",)
        ),
        cost_estimate=pl.CostEstimate(flops=int(flops), bytes_accessed=int(moved), transcendentals=0),
        name=name,
    )(*ins)
    return result[0] if single else result


def sds(shape, dtype):
    return jax.ShapeDtypeStruct(shape, dtype)


def self_bias(bias_ref, first_row, live):
    rows, slots = bias_ref.shape
    keys = lax.broadcasted_iota(jnp.int32, (rows, slots), 1)
    places = lax.broadcasted_iota(jnp.int32, (rows, slots), 0) + first_row
    bias_ref[...] = jnp.where((keys <= places) & (keys < live), 0.0, NEG)


def self_forward_kernel(
    where_ref, y_ref, g_ref, w_ref, b_ref, q_ref, kv_ref, lse_ref, o_ref, y1_ref, c_ref, bias_ref
):
    first_row, live = where_ref[0], where_ref[1]
    slots, own = y_ref.shape[0], q_ref.shape[0]
    tile = 256

    def project(i, carry):
        rows = pl.ds(pl.multiple_of(i * tile, tile), tile)
        normed = norm(y_ref[rows, :].astype(f32), g_ref[1:2, :]).astype(bf16)
        b_ref[rows, :] = normed
        kv_ref[rows, 0:D] = nn(normed, mat(w_ref, 1)).astype(bf16)
        kv_ref[rows, D : 2 * D] = nn(normed, mat(w_ref, 2)).astype(bf16)
        return carry

    lax.fori_loop(0, slots // tile, project, 0)
    mine = pl.ds(pl.multiple_of(first_row, 16), own)
    q_ref[...] = nn(b_ref[mine, :], mat(w_ref, 0)).astype(bf16)
    self_bias(bias_ref, first_row, live)
    lse_ref[...] = jnp.zeros_like(lse_ref)
    lanes = lax.broadcasted_iota(jnp.int32, lse_ref.shape, 1)
    low = low_half(own)

    def attend(pair, carry):
        queries = q_ref[:, pair_cols(pair)]
        keys = kv_ref[:, pair_cols(pair)]
        values = kv_ref[:, pair_cols(pair, D)]
        mixed = []
        table = lse_ref[...]
        for half in range(2):
            scores = nt(queries * lane_half(half, SCALE, bf16), keys) + bias_ref[...]
            chances, log_totals = softmax_rows(scores)
            mixed.append(nn(chances.astype(bf16), values))
            table = jnp.where(lanes == 2 * pair + half, log_totals, table)
        lse_ref[...] = table
        o_ref[:, pair_cols(pair)] = jnp.where(low, mixed[0], mixed[1]).astype(bf16)
        return carry

    lax.fori_loop(0, PAIRS, attend, 0)
    y1 = y_ref[mine, :].astype(f32) + nn(o_ref[...], mat(w_ref, 3))
    y1_ref[...] = y1
    c_ref[...] = norm(y1, g_ref[3:4, :]).astype(bf16)


def window_bias(rows, side, row_split, col_split):
    def flags(shape, dim):
        token = lax.broadcasted_iota(jnp.int32, shape, dim)
        row, col = token // side, token % side
        return jnp.where(row >= side // 2, row_split, 0) + jnp.where(
            col >= side // 2, 2 * col_split, 0
        )

    return jnp.where(flags((rows, rows), 0) == flags((rows, rows), 1), 0.0, NEG)


def swin_forward_kernel(
    side, where_ref, x_ref, g_ref, w_ref, a_ref, qkv_ref, lse_ref, o_ref, v1_ref, e_ref, bias_ref
):
    is_last = where_ref[2]
    tokens = x_ref.shape[0]
    rows = side * side
    windows = tokens // rows
    x = x_ref[...].astype(f32)
    normed = norm(x, g_ref[0:1, :]).astype(bf16)
    a_ref[...] = normed
    for k in range(3):
        qkv_ref[:, k * D : (k + 1) * D] = nn(normed, mat(w_ref, k)).astype(bf16)
    for w in range(windows):
        bias_ref[w] = window_bias(rows, side, is_last, 1 if w == windows - 1 else 0)
    lse_ref[...] = jnp.zeros_like(lse_ref)
    lanes = lax.broadcasted_iota(jnp.int32, (rows, lse_ref.shape[1]), 1)
    low = low_half(rows)

    def attend(pair, carry):
        for w in range(windows):
            at = slice(w * rows, (w + 1) * rows)
            queries = qkv_ref[at, pair_cols(pair)]
            keys = qkv_ref[at, pair_cols(pair, D)]
            values = qkv_ref[at, pair_cols(pair, 2 * D)]
            mixed = []
            table = lse_ref[at, :]
            for half in range(2):
                scores = nt(queries * lane_half(half, SCALE, bf16), keys) + bias_ref[w]
                chances, log_totals = softmax_rows(scores)
                mixed.append(nn(chances.astype(bf16), values))
                table = jnp.where(lanes == 2 * pair + half, log_totals, table)
            lse_ref[at, :] = table
            o_ref[at, pair_cols(pair)] = jnp.where(low, mixed[0], mixed[1]).astype(bf16)
        return carry

    lax.fori_loop(0, PAIRS, attend, 0)
    v1 = x + nn(o_ref[...], mat(w_ref, 3))
    v1_ref[...] = v1
    e_ref[...] = norm(v1, g_ref[2:3, :]).astype(bf16)


def cross_forward_kernel(
    where_ref,
    c_ref,
    cot_ref,
    e_ref,
    wqv_ref,
    wvq_ref,
    qa_ref,
    kvb_ref,
    doa_ref,
    kva_ref,
    qb_ref,
    stats_ref,
    lse_ref,
    ob_ref,
):
    live = where_ref[1]
    slots, tokens = c_ref.shape[0], e_ref.shape[0]
    tile = 256
    normed = e_ref[...]
    for k in range(2):
        kva_ref[:, k * D : (k + 1) * D] = nn(normed, mat(wqv_ref, 1 + k)).astype(bf16)
    qb_ref[...] = nn(normed, mat(wvq_ref, 0)).astype(bf16)

    def project(i, carry):
        rows = pl.ds(pl.multiple_of(i * tile, tile), tile)
        part = c_ref[rows, :]
        qa_ref[rows, :] = nn(part, mat(wqv_ref, 0)).astype(bf16)
        for k in range(2):
            kvb_ref[rows, k * D : (k + 1) * D] = nn(part, mat(wvq_ref, 1 + k)).astype(bf16)
        doa_ref[rows, :] = nt(cot_ref[rows, :], mat(wqv_ref, 3)).astype(bf16)
        return carry

    lax.fori_loop(0, slots // tile, project, 0)
    stats_ref[...] = jnp.zeros_like(stats_ref)

    def page_stats(pair, carry):
        keys = kva_ref[:, pair_cols(pair)]
        values = kva_ref[:, pair_cols(pair, D)]
        for half in range(2):
            head = 2 * pair + half
            keys_h = keys * lane_half(half, SCALE, bf16)
            values_h = values * lane_half(half, 1.0, bf16)
            for i in range(slots // tile):
                rows = slice(i * tile, (i + 1) * tile)
                scores = nt(keys_h, qa_ref[rows, pair_cols(pair)])
                highest = jnp.max(scores, axis=0, keepdims=True)
                raised = jnp.exp(scores - highest)
                grads = nt(values_h, doa_ref[rows, pair_cols(pair)])
                stats_ref[0, pl.ds(head, 1), rows] = highest
                stats_ref[1, pl.ds(head, 1), rows] = jnp.sum(raised, axis=0, keepdims=True)
                stats_ref[2, pl.ds(head, 1), rows] = jnp.sum(raised * grads, axis=0, keepdims=True)
        return carry

    lax.fori_loop(0, PAIRS, page_stats, 0)
    lse_ref[...] = jnp.zeros_like(lse_ref)
    lanes = lax.broadcasted_iota(jnp.int32, lse_ref.shape, 1)
    low = low_half(tokens)
    bias = jnp.where(lax.broadcasted_iota(jnp.int32, (1, slots), 1) < live, 0.0, NEG)

    def attend(pair, carry):
        queries = qb_ref[:, pair_cols(pair)]
        keys = kvb_ref[:, pair_cols(pair)]
        values = kvb_ref[:, pair_cols(pair, D)]
        mixed = []
        table = lse_ref[...]
        for half in range(2):
            scores = nt(queries * lane_half(half, SCALE, bf16), keys) + bias
            chances, log_totals = softmax_rows(scores)
            mixed.append(nn(chances.astype(bf16), values))
            table = jnp.where(lanes == 2 * pair + half, log_totals, table)
        lse_ref[...] = table
        ob_ref[:, pair_cols(pair)] = jnp.where(low, mixed[0], mixed[1]).astype(bf16)
        return carry

    lax.fori_loop(0, PAIRS, attend, 0)


GELU_A = 0.7978845608028654
GELU_B = 0.044715


def mlp_kernel(
    steps,
    v1_ref,
    ob_ref,
    cot_ref,
    g_ref,
    wvq_ref,
    up_ref,
    down_ref,
    v3_ref,
    h_ref,
    act_ref,
    du_ref,
    g2_ref,
    dz_ref,
    dob_ref,
    dg_ref,
    v2_ref,
    sum_ref,
    dh_ref,
):
    step = pl.program_id(0)

    @pl.when(step == 0)
    def _():
        v2 = v1_ref[...] + nn(ob_ref[...], mat(wvq_ref, 3))
        v2_ref[...] = v2
        sum_ref[...] = v2
        h_ref[...] = norm(v2, g_ref[4:5, :]).astype(bf16)
        dh_ref[...] = jnp.zeros_like(dh_ref)

    up, down = up_ref[0], down_ref[0]
    u = nn(h_ref[...], up)
    squared = u * u
    bend = jnp.tanh(GELU_A * (u + GELU_B * u * squared))
    act = (0.5 * u * (1.0 + bend)).astype(bf16)
    act_ref[...] = act
    slope = 0.5 * (1.0 + bend) + 0.5 * u * (1.0 - bend * bend) * GELU_A * (
        1.0 + 3.0 * GELU_B * squared
    )
    du = (nt(cot_ref[...], down) * slope).astype(bf16)
    du_ref[...] = du
    sum_ref[...] += nn(act, down)
    dh_ref[...] += nt(du, up)

    @pl.when(step == steps - 1)
    def _():
        v3_ref[...] = sum_ref[...].astype(bf16)
        part, dg = norm_back(v2_ref[...], g_ref[4:5, :], dh_ref[...])
        dg_ref[...] = dg
        g2 = cot_ref[...].astype(f32) + part
        g2_ref[...] = g2
        dz = g2.astype(bf16)
        dz_ref[...] = dz
        dob_ref[...] = nt(dz, mat(wvq_ref, 3)).astype(bf16)


def mlp(v1, ob, cot, gains, wvq, wvq_spec, up, down):
    tokens = v1.shape[0]
    steps = FF // D
    whole = lambda shape: pl.BlockSpec(shape, lambda i: (0,) * len(shape))
    cols = pl.BlockSpec((tokens, D), lambda i: (0, i))
    weight = pl.BlockSpec((1, D, D), lambda i: (i, 0, 0))
    row = whole((tokens, D))

    def kernel(*refs):
        mlp_kernel(steps, *refs)

    return pl.pallas_call(
        kernel,
        grid=(steps,),
        out_shape=[
            sds((tokens, D), bf16),
            sds((tokens, D), bf16),
            sds((tokens, FF), bf16),
            sds((tokens, FF), bf16),
            sds((tokens, D), f32),
            sds((tokens, D), bf16),
            sds((tokens, D), bf16),
            sds((1, D), f32),
        ],
        in_specs=[
            row,
            row,
            row,
            whole(gains.shape),
            wvq_spec,
            weight,
            weight,
        ],
        out_specs=[row, row, cols, cols, row, row, row, whole((1, D))],
        scratch_shapes=[pltpu.VMEM((tokens, D), f32)] * 3,
        compiler_params=pltpu.CompilerParams(
            vmem_limit_bytes=VMEM_LIMIT, dimension_semantics=("arbitrary",)
        ),
        cost_estimate=pl.CostEstimate(
            flops=2 * tokens * D * D * 18, bytes_accessed=24 * 1024 * 1024, transcendentals=0
        ),
        name="mlp",
    )(v1, ob, cot, gains, wvq, up, down)


def vq_backward_kernel(
    where_ref, qb_ref, kvb_ref, dob_ref, lse_ref, dqb_ref, dkvbt_ref
):
    live = where_ref[1]
    tokens, slots = qb_ref.shape[0], kvb_ref.shape[0]
    bias = jnp.where(lax.broadcasted_iota(jnp.int32, (1, slots), 1) < live, 0.0, NEG)
    low = low_half(tokens)

    def back(pair, carry):
        queries = qb_ref[:, pair_cols(pair)]
        keys = kvb_ref[:, pair_cols(pair)]
        values = kvb_ref[:, pair_cols(pair, D)]
        grads = dob_ref[:, pair_cols(pair)]
        queries_t = (queries * SCALE).astype(f32).T.astype(bf16)
        grads_t = grads.astype(f32).T.astype(bf16)
        parts = []
        for half in range(2):
            own = slice(half * HD, (half + 1) * HD)
            scores = nt(queries * lane_half(half, SCALE, bf16), keys) + bias
            chances = jnp.exp(scores - column(lse_ref[...], 2 * pair + half))
            slopes = nt(grads * lane_half(half, 1.0, bf16), values)
            centre = jnp.sum(chances * slopes, axis=-1, keepdims=True)
            ds = (chances * (slopes - centre)).astype(bf16)
            parts.append(nn(ds, keys))
            at = pair * PW + half * HD
            dkvbt_ref[pl.ds(pl.multiple_of(at, HD), HD), :] = nn(queries_t[own], ds).astype(bf16)
            dkvbt_ref[pl.ds(pl.multiple_of(D + at, HD), HD), :] = nn(
                grads_t[own], chances.astype(bf16)
            ).astype(bf16)
        dqb_ref[:, pair_cols(pair)] = (jnp.where(low, parts[0], parts[1]) * SCALE).astype(bf16)
        return carry

    lax.fori_loop(0, PAIRS, back, 0)


def qv_backward_kernel(qa_ref, kva_ref, doa_ref, lse_ref, centre_ref, oa_ref, dqat_ref, dkva_ref):
    slots, tokens = qa_ref.shape[0], kva_ref.shape[0]
    low = low_half(tokens)
    tile = 512

    def back(pair, carry):
        keys = kva_ref[:, pair_cols(pair)]
        values = kva_ref[:, pair_cols(pair, D)]
        keys_t = (keys * SCALE).astype(f32).T.astype(bf16)
        values_t = values.astype(f32).T.astype(bf16)
        for i in range(slots // tile):
            rows = slice(i * tile, (i + 1) * tile)
            queries = qa_ref[rows, pair_cols(pair)]
            grads = doa_ref[rows, pair_cols(pair)]
            dk, dv, mixed = [], [], []
            for half in range(2):
                head = 2 * pair + half
                own = slice(half * HD, (half + 1) * HD)
                scores = nt(keys * lane_half(half, SCALE, bf16), queries)
                chances = jnp.exp(scores - lse_ref[pl.ds(head, 1), rows])
                slopes = nt(values * lane_half(half, 1.0, bf16), grads)
                ds = (chances * (slopes - centre_ref[pl.ds(head, 1), rows])).astype(bf16)
                rounded = chances.astype(bf16)
                mixed.append(nn(values_t[own], rounded))
                dqat_ref[pl.ds(pl.multiple_of(head * HD, HD), HD), rows] = nn(
                    keys_t[own], ds
                ).astype(bf16)
                dk.append(nn(ds, queries))
                dv.append(nn(rounded, grads))
            oa_ref[rows, pair_cols(pair)] = jnp.concatenate(mixed, axis=0).T.astype(bf16)
            dk_now = jnp.where(low, dk[0], dk[1]) * SCALE
            dv_now = jnp.where(low, dv[0], dv[1])
            if i == 0:
                dk_sum, dv_sum = dk_now, dv_now
            else:
                dk_sum, dv_sum = dk_sum + dk_now, dv_sum + dv_now
        dkva_ref[:, pair_cols(pair)] = dk_sum.astype(bf16)
        dkva_ref[:, pair_cols(pair, D)] = dv_sum.astype(bf16)
        return carry

    lax.fori_loop(0, PAIRS, back, 0)


def slots_back_kernel(dqat_ref, dkvbt_ref, wqv_ref, wvq_ref, dc_ref):
    slots = dqat_ref.shape[1]
    tile = 256
    for i in range(slots // tile):
        cols = slice(i * tile, (i + 1) * tile)
        total = nn(mat(wqv_ref, 0), dqat_ref[:, cols])
        total += nn(mat(wvq_ref, 1), dkvbt_ref[0:D, cols])
        total += nn(mat(wvq_ref, 2), dkvbt_ref[D : 2 * D, cols])
        dc_ref[cols, :] = total.T.astype(bf16)


def swin_backward_kernel(
    side,
    where_ref,
    x_ref,
    v1_ref,
    g2_ref,
    g_ref,
    dkva_ref,
    dqb_ref,
    wqv_ref,
    wvq_ref,
    wsw_ref,
    qkv_ref,
    lse_ref,
    dz_ref,
    dqkv_ref,
    grad_ref,
    dg_ref,
    bias_ref,
    do_ref,
):
    is_last = where_ref[2]
    tokens = x_ref.shape[0]
    rows = side * side
    windows = tokens // rows
    de = nt(dkva_ref[:, 0:D], mat(wqv_ref, 1))
    de += nt(dkva_ref[:, D : 2 * D], mat(wqv_ref, 2))
    de += nt(dqb_ref[...], mat(wvq_ref, 0))
    part, dg3 = norm_back(v1_ref[...], g_ref[2:3, :], de)
    g1 = g2_ref[...] + part
    grad_ref[...] = g1
    dz = g1.astype(bf16)
    dz_ref[...] = dz
    do_ref[...] = nt(dz, mat(wsw_ref, 3)).astype(bf16)
    for w in range(windows):
        bias_ref[w] = window_bias(rows, side, is_last, 1 if w == windows - 1 else 0)
    low = low_half(rows)

    def back(pair, carry):
        for w in range(windows):
            at = slice(w * rows, (w + 1) * rows)
            queries = qkv_ref[at, pair_cols(pair)]
            keys = qkv_ref[at, pair_cols(pair, D)]
            values = qkv_ref[at, pair_cols(pair, 2 * D)]
            grads = do_ref[at, pair_cols(pair)]
            dq, dk, dv = [], [], []
            for half in range(2):
                scores = nt(queries * lane_half(half, SCALE, bf16), keys) + bias_ref[w]
                chances = jnp.exp(scores - column(lse_ref[at, :], 2 * pair + half))
                slopes = nt(grads * lane_half(half, 1.0, bf16), values)
                centre = jnp.sum(chances * slopes, axis=-1, keepdims=True)
                ds = (chances * (slopes - centre)).astype(bf16)
                dq.append(nn(ds, keys))
                dk.append(tn(ds, queries))
                dv.append(tn(chances.astype(bf16), grads))
            for k, (pieces, factor) in enumerate(((dq, SCALE), (dk, SCALE), (dv, 1.0))):
                dqkv_ref[at, pair_cols(pair, k * D)] = (
                    jnp.where(low, pieces[0], pieces[1]) * factor
                ).astype(bf16)
        return carry

    lax.fori_loop(0, PAIRS, back, 0)
    da = nt(dqkv_ref[:, 0:D], mat(wsw_ref, 0))
    da += nt(dqkv_ref[:, D : 2 * D], mat(wsw_ref, 1))
    da += nt(dqkv_ref[:, 2 * D : 3 * D], mat(wsw_ref, 2))
    part, dg1 = norm_back(x_ref[...].astype(f32), g_ref[0:1, :], da)
    grad_ref[...] += part
    dg_ref[...] = jnp.concatenate([dg1, dg3], axis=0)


def self_backward_kernel(
    where_ref,
    dc_ref,
    y1_ref,
    cot_ref,
    g_ref,
    w_ref,
    q_ref,
    kv_ref,
    lse_ref,
    gy1_ref,
    dz_ref,
    dq_ref,
    dkvt_ref,
    db_ref,
    dbq_ref,
    dg_ref,
    bias_ref,
    do_ref,
):
    first_row, live = where_ref[0], where_ref[1]
    own_rows, slots = q_ref.shape[0], kv_ref.shape[0]
    part, dg = norm_back(y1_ref[...], g_ref[3:4, :], dc_ref[...].astype(f32))
    dg_ref[...] = dg
    gy1 = cot_ref[...].astype(f32) + part
    gy1_ref[...] = gy1
    dz = gy1.astype(bf16)
    dz_ref[...] = dz
    do_ref[...] = nt(dz, mat(w_ref, 3)).astype(bf16)
    self_bias(bias_ref, first_row, live)
    low = low_half(own_rows)

    def back(pair, carry):
        queries = q_ref[:, pair_cols(pair)]
        keys = kv_ref[:, pair_cols(pair)]
        values = kv_ref[:, pair_cols(pair, D)]
        grads = do_ref[:, pair_cols(pair)]
        queries_t = (queries * SCALE).astype(f32).T.astype(bf16)
        grads_t = grads.astype(f32).T.astype(bf16)
        parts = []
        for half in range(2):
            own = slice(half * HD, (half + 1) * HD)
            scores = nt(queries * lane_half(half, SCALE, bf16), keys) + bias_ref[...]
            chances = jnp.exp(scores - column(lse_ref[...], 2 * pair + half))
            slopes = nt(grads * lane_half(half, 1.0, bf16), values)
            centre = jnp.sum(chances * slopes, axis=-1, keepdims=True)
            ds = (chances * (slopes - centre)).astype(bf16)
            parts.append(nn(ds, keys))
            at = pair * PW + half * HD
            dkvt_ref[pl.ds(pl.multiple_of(at, HD), HD), :] = nn(queries_t[own], ds).astype(bf16)
            dkvt_ref[pl.ds(pl.multiple_of(D + at, HD), HD), :] = nn(
                grads_t[own], chances.astype(bf16)
            ).astype(bf16)
        dq_ref[:, pair_cols(pair)] = (jnp.where(low, parts[0], parts[1]) * SCALE).astype(bf16)
        return carry

    lax.fori_loop(0, PAIRS, back, 0)
    dbq_ref[...] = nt(dq_ref[...], mat(w_ref, 0))
    tile = 256
    for i in range(slots // tile):
        cols = slice(i * tile, (i + 1) * tile)
        total = nn(mat(w_ref, 1), dkvt_ref[0:D, cols])
        total += nn(mat(w_ref, 2), dkvt_ref[D : 2 * D, cols])
        db_ref[cols, :] = total.T.astype(bf16)


def query_end_kernel(db_ref, dbq_ref, y_ref, gy1_ref, g_ref, grad_ref, dg_ref):
    part, dg = norm_back(
        y_ref[...].astype(f32), g_ref[1:2, :], db_ref[...].astype(f32) + dbq_ref[...]
    )
    grad_ref[...] = gy1_ref[...] + part
    dg_ref[...] = dg


def window_order(grid_rows, half):
    rows, cols, _ = grid_rows.shape
    rolled = jnp.roll(grid_rows, -half, axis=1)
    shaped = rolled.reshape(rows, cols // rows, rows, D).transpose(1, 0, 2, 3)
    return shaped.reshape(rows * cols, D)


def grid_order(tokens_in, rows, cols, half):
    shaped = tokens_in.reshape(cols // rows, rows, rows, D).transpose(1, 0, 2, 3)
    return jnp.roll(shaped.reshape(rows, cols, D), half, axis=1)


def on_device(
    visual,
    query_tokens,
    answer_len,
    attn_swin,
    attn_self,
    attn_qv,
    attn_vq,
    mlp_up,
    mlp_down,
    norm_gains,
    visual_cot,
    query_cot,
):
    everyone = ("page", "blk")
    blk_count = lax.axis_size("blk")
    blk_here = lax.axis_index("blk")
    shards = lax.axis_size("page") * blk_count
    rows_here, cols_all = visual.shape[1], visual.shape[2]
    half = rows_here // 2
    tokens = rows_here * cols_all
    q_rows = query_tokens.shape[1]
    slots = q_rows * blk_count
    share = attn_swin.shape[0] // D
    aligned = share % 16 == 0
    gain_width = norm_gains.shape[0]

    def flat_share(value):
        return value.astype(bf16).reshape(share, D)

    up_share = (
        mlp_up.astype(bf16).reshape(share // 4, 4, D).transpose(1, 0, 2).reshape(share, D)
    )
    gain_row = jnp.pad(norm_gains.astype(bf16)[None], ((0, 15), (0, D - gain_width)))

    def gather(parts):
        joined = lax.all_gather(jnp.concatenate(parts, axis=0), everyone, axis=0, tiled=True)
        return joined.reshape(shards, -1, D)

    first = gather([flat_share(attn_self), flat_share(attn_swin), gain_row])
    second = gather([flat_share(attn_qv), flat_share(attn_vq)])
    third = gather([up_share, flat_share(mlp_down)])
    gains = first[:, 2 * share, :gain_width].reshape(8, D).astype(f32)

    def weight(joined, index):
        if aligned:
            return joined, pl.BlockSpec((shards, share, D), lambda i: (0, index, 0), pipeline_mode=pl.Buffered(1))
        taken = joined[:, index * share : (index + 1) * share].reshape(1, 4 * D, D)
        return taken, pl.BlockSpec((1, 4 * D, D), lambda i: (0, 0, 0), pipeline_mode=pl.Buffered(1))

    w_self, s_self = weight(first, 0)
    w_swin, s_swin = weight(first, 1)
    w_qv, s_qv = weight(second, 0)
    w_vq, s_vq = weight(second, 1)
    w_up = (
        third[:, :share].reshape(shards, 4, share // 4, D).transpose(1, 0, 2, 3).reshape(4, D, D)
    )
    w_down = third[:, share : 2 * share].reshape(4, D, D)

    query_all = lax.all_gather(query_tokens[0], "blk", axis=0, tiled=True)
    cot_all = lax.all_gather(query_cot[0], "blk", axis=0, tiled=True)
    down_one = [(i, (i - 1) % blk_count) for i in range(blk_count)]
    up_one = [(i, (i + 1) % blk_count) for i in range(blk_count)]
    both = jnp.concatenate([visual, visual_cot], axis=0)
    lent = lax.ppermute(both[:, :half], "blk", down_one)
    both = jnp.concatenate([both[:, half:], lent], axis=1)
    vis_in = window_order(both[0], half)
    vis_cot = window_order(both[1], half)

    where = jnp.stack(
        [blk_here * q_rows, answer_len[0], (blk_here == blk_count - 1).astype(jnp.int32)]
    ).astype(jnp.int32)

    b_all, q_self, kv_self, lse_self, o_self, y1, c_own = call(
        self_forward_kernel,
        [
            sds((slots, D), bf16),
            sds((q_rows, D), bf16),
            sds((slots, 2 * D), bf16),
            sds((q_rows, 128), f32),
            sds((q_rows, D), bf16),
            sds((q_rows, D), f32),
            sds((q_rows, D), bf16),
        ],
        [where, query_all, gains, w_self],
        scratch=[pltpu.VMEM((q_rows, slots), f32)],
        smem=1,
        blocks={3: s_self},
        flops=2 * slots * D * 2 * D,
        name="self_forward",
    )
    c_all = lax.all_gather(c_own, "blk", axis=0, tiled=True)

    def swin_forward(*refs):
        swin_forward_kernel(rows_here, *refs)

    a_low, qkv_swin, lse_swin, o_swin, v1, e_low = call(
        swin_forward,
        [
            sds((tokens, D), bf16),
            sds((tokens, 3 * D), bf16),
            sds((tokens, 128), f32),
            sds((tokens, D), bf16),
            sds((tokens, D), f32),
            sds((tokens, D), bf16),
        ],
        [where, vis_in, gains, w_swin],
        scratch=[pltpu.VMEM((cols_all // rows_here, rows_here**2, rows_here**2), f32)],
        smem=1,
        blocks={3: s_swin},
        flops=2 * tokens * D * 4 * D,
        name="swin_forward",
    )

    qa, kvb, doa, kva, qb, stats, lse_vq, o_vq = call(
        cross_forward_kernel,
        [
            sds((slots, D), bf16),
            sds((slots, 2 * D), bf16),
            sds((slots, D), bf16),
            sds((tokens, 2 * D), bf16),
            sds((tokens, D), bf16),
            sds((3, 16, slots), f32),
            sds((tokens, 128), f32),
            sds((tokens, D), bf16),
        ],
        [where, c_all, cot_all, e_low, w_qv, w_vq],
        smem=1,
        blocks={4: s_qv, 5: s_vq},
        flops=2 * slots * D * 4 * D + 2 * tokens * slots * D * 4,
        name="cross_forward",
    )

    all_stats = lax.all_gather(stats, "blk", axis=0)
    peaks = jnp.max(all_stats[:, 0], axis=0)
    weights = jnp.exp(all_stats[:, 0] - peaks[None])
    totals = jnp.sum(all_stats[:, 1] * weights, axis=0)
    lse_qv = peaks + jnp.log(totals)
    centre_qv = jnp.sum(all_stats[:, 2] * weights, axis=0) / totals

    v3, h_low, act_low, du_low, g2, dz_vq, dob, dg5 = mlp(
        v1, o_vq, vis_cot, gains, w_vq, s_vq, w_up, w_down
    )

    dqb, dkvbt = call(
        vq_backward_kernel,
        [sds((tokens, D), bf16), sds((2 * D, slots), bf16)],
        [where, qb, kvb, dob, lse_vq],
        smem=1,
        flops=2 * tokens * slots * D * 5,
        name="vq_backward",
    )
    oa_part, dqat, dkva = call(
        qv_backward_kernel,
        [sds((slots, D), bf16), sds((D, slots), bf16), sds((tokens, 2 * D), bf16)],
        [qa, kva, doa, lse_qv, centre_qv],
        flops=2 * tokens * slots * D * 6,
        name="qv_backward",
    )
    dc_part = call(
        slots_back_kernel,
        sds((slots, D), bf16),
        [dqat, dkvbt, w_qv, w_vq],
        blocks={2: s_qv, 3: s_vq},
        flops=2 * slots * D * D * 3,
        name="slots_back",
    )
    merged = lax.psum_scatter(
        jnp.concatenate([oa_part, dc_part], axis=1), "blk", scatter_dimension=0, tiled=True
    )
    oa_low, dc_low = merged[:, :D], merged[:, D:]

    def swin_backward(*refs):
        swin_backward_kernel(rows_here, *refs)

    dz_swin, dqkv_swin, visual_grad, dg_visual = call(
        swin_backward,
        [
            sds((tokens, D), bf16),
            sds((tokens, 3 * D), bf16),
            sds((tokens, D), f32),
            sds((2, D), f32),
        ],
        [where, vis_in, v1, g2, gains, dkva, dqb, w_qv, w_vq, w_swin, qkv_swin, lse_swin],
        scratch=[
            pltpu.VMEM((cols_all // rows_here, rows_here**2, rows_here**2), f32),
            pltpu.VMEM((tokens, D), bf16),
        ],
        smem=1,
        blocks={7: s_qv, 8: s_vq, 9: s_swin},
        flops=2 * tokens * D * 7 * D,
        name="swin_backward",
    )

    gy1, dz_self, dq_self, dkvt_self, db_part, dbq, dg4 = call(
        self_backward_kernel,
        [
            sds((q_rows, D), f32),
            sds((q_rows, D), bf16),
            sds((q_rows, D), bf16),
            sds((2 * D, slots), bf16),
            sds((slots, D), bf16),
            sds((q_rows, D), f32),
            sds((1, D), f32),
        ],
        [where, dc_low, y1, query_cot[0], gains, w_self, q_self, kv_self, lse_self],
        scratch=[pltpu.VMEM((q_rows, slots), f32), pltpu.VMEM((q_rows, D), bf16)],
        smem=1,
        blocks={5: s_self},
        flops=2 * slots * D * 2 * D,
        name="self_backward",
    )
    db = lax.psum_scatter(db_part, "blk", scatter_dimension=0, tiled=True)
    query_grad, dg2 = call(
        query_end_kernel,
        [sds((q_rows, D), f32), sds((1, D), f32)],
        [db, dbq, query_tokens[0], gy1, gains],
        name="query_end",
    )
    query_out = (y1 + jnp.dot(oa_low, w_out(first=w_qv, share=share, shards=shards, aligned=aligned),
                              preferred_element_type=f32)).astype(bf16)

    def outer(left, right):
        return tn(left, right).astype(bf16)

    def outer_t(left, right_t):
        return lax.dot_general(
            left, right_t, (((0,), (1,)), ((), ())), preferred_element_type=f32
        ).astype(bf16)

    def as_shares(mats):
        return jnp.concatenate(mats, axis=0).reshape(shards, share, D)

    def summed(parts):
        joined = jnp.concatenate(parts, axis=1)
        width = joined.shape[1]
        return lax.psum_scatter(
            joined.reshape(shards * width, D), everyone, scatter_dimension=0, tiled=True
        )

    up_mats = jnp.stack([outer(h_low, du_low[:, k * D : (k + 1) * D]) for k in range(4)])
    up_part = (
        up_mats.reshape(4, shards, share // 4, D).transpose(1, 0, 2, 3).reshape(shards, share, D)
    )
    down_part = outer(act_low, vis_cot).reshape(shards, share, D)
    mlp_sum = summed([up_part, down_part])

    qv_part = as_shares(
        [
            outer_t(c_all, dqat),
            outer(e_low, dkva[:, :D]),
            outer(e_low, dkva[:, D:]),
            outer(oa_low, query_cot[0]),
        ]
    )
    vq_part = as_shares(
        [
            outer(e_low, dqb),
            outer_t(c_all, dkvbt[:D]),
            outer_t(c_all, dkvbt[D:]),
            outer(o_vq, dz_vq),
        ]
    )
    cross_sum = summed([qv_part, vq_part])

    swin_part = as_shares(
        [outer(a_low, dqkv_swin[:, k * D : (k + 1) * D]) for k in range(3)]
        + [outer(o_swin, dz_swin)]
    )
    b_own = lax.dynamic_slice_in_dim(b_all, blk_here * q_rows, q_rows, 0)
    self_part = as_shares(
        [
            outer(b_own, dq_self),
            outer_t(b_all, dkvt_self[:D]),
            outer_t(b_all, dkvt_self[D:]),
            outer(o_self, dz_self),
        ]
    )
    gain_block = jnp.concatenate(
        [dg_visual[0:1], dg2, dg_visual[1:2], dg4, dg5, jnp.zeros((3, D), f32)], axis=0
    )
    gain_part = jnp.pad(
        gain_block.astype(bf16).reshape(shards, 1, gain_width),
        ((0, 0), (0, 15), (0, D - gain_width)),
    )
    last_sum = summed([swin_part, self_part, gain_part])

    def flat(value):
        return value.astype(f32).reshape(-1)

    up_grad = flat(mlp_sum[:share].reshape(4, share // 4, D).transpose(1, 0, 2))

    def back_to_grid(value):
        grid = grid_order(value, rows_here, cols_all, half)
        returned = lax.ppermute(grid[half:], "blk", up_one)
        return jnp.concatenate([returned, grid[:half]], axis=0)[None]

    return (
        back_to_grid(v3),
        query_out[None],
        back_to_grid(visual_grad),
        query_grad[None],
        flat(last_sum[:share]),
        flat(last_sum[share : 2 * share]),
        flat(cross_sum[:share]),
        flat(cross_sum[share : 2 * share]),
        up_grad,
        flat(mlp_sum[share : 2 * share]),
        flat(last_sum[2 * share, :gain_width]),
    )


def w_out(first, share, shards, aligned):
    if aligned:
        return first[3 * shards // 4 :, :share].reshape(D, D)
    return first[0, 3 * D :]


def solution(mesh):
    placed = (
        P("page", "blk", None, None),
        P("page", "blk", None),
        P("page"),
        P(("page", "blk")),
        P(("page", "blk")),
        P(("page", "blk")),
        P(("page", "blk")),
        P(("page", "blk")),
        P(("page", "blk")),
        P(("page", "blk")),
        P("page", "blk", None, None),
        P("page", "blk", None),
    )
    return jax.shard_map(
        on_device,
        mesh=mesh,
        in_specs=placed,
        out_specs=(
            P("page", "blk", None, None),
            P("page", "blk", None),
            P("page", "blk", None, None),
            P("page", "blk", None),
            P(("page", "blk")),
            P(("page", "blk")),
            P(("page", "blk")),
            P(("page", "blk")),
            P(("page", "blk")),
            P(("page", "blk")),
            P(("page", "blk")),
        ),
        check_vma=False,
    )
```

time: 2010 us -> 976 us (0.49)
  matrix products: 438 us -> 27.3 us
  local copies, waits for them, and re-layouts: 404 us -> 27.3 us
  Pallas kernels: 0 us -> 153 us
  loops' own time: 151 us -> 0 us
  blocking collectives: 124 us -> 0 us
  other arithmetic: 97.1 us -> 45.2 us
  starting transfers between devices: 39.1 us -> 4.18 us
  waiting for transfers between devices: 722 us -> 695 us
    dot_general x235 -> x22, matrix products: 438 us -> 27.3 us  [the longest x16 17.6 us: tn(): lax.dot_general(left, right, (((0,), (0,)), ((), ())), preferred_element_...]
    reduce_scatter x4 -> x5, waiting for transfers between devices: 16.2 us -> 409 us  [the longest x3 364 us: summed(): lax.psum_scatter(joined.reshape(shards * width, D), everyone, scatter_dim...]
    all_to_all x6 -> x0, waiting for transfers between devices: 305 us -> none  [the longest x1 210 us: on_device(): lax.all_to_all(pair_right, 'page', split_axis=1, concat_axis=0, tiled=True)]
    pallas_call x0 -> x10, Pallas kernels: none -> 153 us  [the longest x9 138 us: call(): pl.pallas_call(kernel, grid=(1,), out_shape=shapes, in_specs=specs, out_s...]
    another operation x7 -> x0, loops' own time: 151 us -> none  [the longest x1 32 us: on_device(): vq_grad_q, vq_grad_k, vq_grad_v = lax.map(vq_back, head_range)]
    unnamed x16 -> x12, waiting for transfers between devices: 135 us -> 1.54 us
    unnamed x2 -> x0, blocking collectives: 80.8 us -> none
    dynamic_slice x120 -> x0, local copies, waits for them, and re-layouts: 78.8 us -> none  [the longest x72 42.1 us: on_device(): vq_att, vq_lse = lax.map(vq_head, head_range)]
  transfers between devices with their start and end apart: 25 -> 15, of which waited for: 13 -> 11; matrix products, arithmetic and copies ran while one was open for 44% -> 8% of each run, Pallas kernels for 0% -> 11%
where the time goes in v1:
time: 976 us; the launch traced here: 967 us
  waiting for transfers between devices  695 us (71%)
  Pallas kernels  153 us (16%)
  other arithmetic  45.2 us (5%)
  local copies, waits for them, and re-layouts  27.3 us (3%)
  matrix products  27.3 us (3%)
  between operations  16.1 us (2%)
    reduce_scatter x3, waiting for transfers between devices, summed(): lax.psum_scatter(joined.reshape(shards * width, D), everyone, scatter_dim...  364 us
    all_gather x3, waiting for transfers between devices, gather(): lax.all_gather(jnp.concatenate(parts, axis=0), everyone, axis=0, tiled=True)  215 us
    pallas_call x9, Pallas kernels, call(): pl.pallas_call(kernel, grid=(1,), out_shape=shapes, in_specs=specs, out_s...  138 us
    reduce_scatter x1, waiting for transfers between devices, on_device(): lax.psum_scatter(jnp.concatenate([oa_part, dc_part], axis=1), 'blk', scat...  45 us
    all_gather x1, waiting for transfers between devices, on_device(): c_all = lax.all_gather(c_own, 'blk', axis=0, tiled=True)  26.6 us
    all_gather x1, waiting for transfers between devices, on_device(): query_all = lax.all_gather(query_tokens[0], 'blk', axis=0, tiled=True)  24.4 us
  transfers between devices with their start and end apart: 15, of which 11 were waited for; matrix products, arithmetic and copies ran while one was open for 8% of the time, Pallas kernels for 11%

profile of v1, /device:TPU:0, one launch (start us, length us, event | category | flops | bytes accessed | tf_op | source)
XLA Modules:
  0.0 967.3 jit_solution(9469197225712634573)
XLA Ops:
  15.0 84.9 %all-gather.11.cloned.1.call-done = bf16[6656,768]{1,0:T(8,128)(2,1)} async-done(((bf16[208,768]{1,0:T(8,128)(2,1)}), bf16[6656,768]{1,0:T(8,128)(2,1)}) %all-gather.11.cloned.1.call-update) | async-done | bytes 10223632 | tf_op jit(solution)/shard_map/all_gather | solution.py:694
  101.6 24.4 %all-gather.19.cloned.1.call-done = bf16[1,1024,768]{2,1,0:T(8,128)(2,1)} async-done(((bf16[1,128,768]{2,1,0:T(8,128)(2,1)}), bf16[1,1024,768]{2,1,0:T(8,128)(2,1)}) %all-gather.19.cloned.1.call-update) | async-done | bytes 1572880 | tf_op jit(solution)/shard_map/all_gather | solution.py:717
  126.0 15.5 %self_forward.1 = (bf16[1024,768]{1,0:T(8,128)(2,1)}, bf16[128,768]{1,0:T(8,128)(2,1)}, bf16[1024,1536]{1,0:T(8,128)(2,1)}, f32[128,128]{1,0:T(8,128)}, bf16[128...) custom-call(s32[3]{0:T(128)} %pad_add_fusion.refs_0_.where_ref, bf16[1024,768]{1,0:T(8,128)(2,1)} %bitcast.155, ...), custom_call_target="tpu_custom_call" | custom-call | flops 2415919104 | bytes 17588236 | tf_op jit(solution)/shard_map/self_forward/pallas_call | solution.py:106
  144.3 10.1 %collective-permute-done = bf16[2,6,24,768]{3,2,1,0:T(8,128)(2,1)S(1)} collective-permute-done((bf16[2,6,24,768]{3,2,1,0:T(8,128)(2,1)S(1)}, bf16[2,6,24,768]{3,2,1,0:T(8,128)(2,1)S(1)}, u32[]{:S(2)}, u32[]{:S(2)}) %collective-permute-start) | collective-permute-done | bytes 442400 | tf_op jit(solution)/shard_map/ppermute | solution.py:722
  155.7 11.0 %swin_forward.1 = (bf16[288,768]{1,0:T(8,128)(2,1)}, bf16[288,2304]{1,0:T(8,128)(2,1)}, f32[288,128]{1,0:T(8,128)}, bf16[288,768]{1,0:T(8,128)(2,1)}, f32[288,768]{1,0:T(8,128)}, /*index=5*/bf16[288,768]{1,0:T(8,128)(2,1)}) custom-call(s32[3]{0:T(128)} %pad_add_fusion.refs_0_.where_ref, bf16[288,768]{1,0:T(8,128)(2,1)} %reshape.181.refs_1_, ...), custom_call_target="tpu_custom_call" | custom-call | flops 1358954496 | bytes 14376972 | tf_op jit(solution)/shard_map/swin_forward/pallas_call | solution.py:106
  166.7 74.5 %all-gather.15.cloned.1.call-done = bf16[6144,768]{1,0:T(8,128)(2,1)} async-done(((bf16[192,768]{1,0:T(8,128)(2,1)}), bf16[6144,768]{1,0:T(8,128)(2,1)}) %all-gather.15.cloned.1.call-update) | async-done | bytes 9437200 | tf_op jit(solution)/shard_map/all_gather | solution.py:694
  241.2 26.6 %all-gather.13.cloned.1.call-done.c_ref = bf16[1024,768]{1,0:T(8,128)(2,1)} async-done(((bf16[128,768]{1,0:T(8,128)(2,1)}), bf16[1024,768]{1,0:T(8,128)(2,1)}) %all-gather.13.cloned.1.call-update) | async-done | bytes 1572880 | tf_op jit(solution)/shard_map/all_gather | solution.py:749
  267.8 28.3 %cross_forward.1 = (bf16[1024,768]{1,0:T(8,128)(2,1)}, bf16[1024,1536]{1,0:T(8,128)(2,1)}, bf16[1024,768]{1,0:T(8,128)(2,1)}, bf16[288,1536]{1,0:T(8,128)(2,1)},...) custom-call(s32[3]{0:T(128)} %pad_add_fusion.refs_0_.where_ref, ...), custom_call_target="tpu_custom_call" | custom-call | flops 6643777536 | bytes 30867468 | tf_op jit(solution)/shard_map/cross_forward/pallas_call | solution.py:106
  297.9 55.3 %all-gather.17.cloned.1.call-done = bf16[6144,768]{1,0:T(8,128)(2,1)} async-done(((bf16[192,768]{1,0:T(8,128)(2,1)}), bf16[6144,768]{1,0:T(8,128)(2,1)}) %all-gather.17.cloned.1.call-update) | async-done | bytes 9437200 | tf_op jit(solution)/shard_map/all_gather | solution.py:694
  353.2 6.5 fusion.55
  362.1 14.5 %mlp.1 = (bf16[288,768]{1,0:T(8,128)(2,1)}, bf16[288,768]{1,0:T(8,128)(2,1)}, bf16[288,3072]{1,0:T(8,128)(2,1)}, bf16[288,3072]{1,0:T(8,128)(2,1)}, f32[288,768]...) custom-call(f32[288,768]{1,0:T(8,128)} %get-tuple-element.58.refs_0_.refs_2_, ...), custom_call_target="tpu_custom_call" | custom-call | flops 6115295232 | bytes 25165824 | tf_op jit(solution)/shard_map/mlp/pallas_call | solution.py:379
  376.6 15.9 %vq_backward.1 = (bf16[288,768]{1,0:T(8,128)(2,1)}, bf16[1536,1024]{1,0:T(8,128)(2,1)}) custom-call(s32[3]{0:T(128)} %pad_add_fusion.refs_0_.where_ref, bf16[288,768]{1,0:T(8,128)(2,1)} %get-tuple-element.70.qb_ref, bf16[1024,1536]{1,0:T(8,128)(2,1)} %get-tuple-element.71.kvb_ref, bf16[288,768]{1,0:T(8,128)(2,1)} %get-tuple-element.72.dob_ref, ...), custom_call_target="tpu_custom_call" | custom-call | flops 2264924160 | bytes 7766028 | tf_op jit(solution)/shard_map/vq_backward/pallas_call | solution.py:106
  395.7 17.5 %qv_backward.1 = (bf16[1024,768]{1,0:T(8,128)(2,1)}, bf16[768,1024]{1,0:T(8,128)(2,1)}, bf16[288,1536]{1,0:T(8,128)(2,1)}) custom-call(bf16[1024,768]{1,0:T(8,128)(2,1)} %get-tuple-element.64.qa_ref, bf16[288,1536]{1,0:T(8,128)(2,1)} %get-tuple-element.65.kva_ref, bf16[1024,768]{1,0:T(8,128)(2,1)} %get-tuple-element.66.doa_ref, ...), custom_call_target="tpu_custom_call" | custom-call | flops 2717908992 | bytes 8192000 | tf_op jit(solution)/shard_map/qv_backward/pallas_call | solution.py:106
  413.3 10.3 %slots_back.1 = bf16[1024,768]{1,0:T(8,128)(2,1)} custom-call(bf16[768,1024]{1,0:T(8,128)(2,1)} %get-tuple-element.69.dqat_ref, bf16[1536,1024]{1,0:T(8,128)(2,1)} %get-tuple-element.74.dkvbt_ref, bf16[32,192,768]{2,1,0:T(8,128)(2,1)} %bitcast.125, bf16[32,192,768]{2,1,0:T(8,128)(2,1)} %bitcast.126), custom_call_target="tpu_custom_call" | custom-call | flops 3623878656 | bytes 25165824 | tf_op jit(solution)/shard_map/slots_back/pallas_call | solution.py:106
  427.1 45.0 %reduce-scatter.6.cloned.1.call-done = bf16[128,1536]{1,0:T(8,128)(2,1)} async-done(((bf16[1024,1536]{1,0:T(8,128)(2,1)}), bf16[128,1536]{1,0:T(8,128)(2,1)}) %reduce-scatter.6.cloned.1.call-update) | async-done | bytes 393232 | tf_op jit(solution)/shard_map/reduce_scatter | solution.py:825
  473.7 15.8 %self_backward.1 = (f32[128,768]{1,0:T(8,128)}, bf16[128,768]{1,0:T(8,128)(2,1)}, bf16[128,768]{1,0:T(8,128)(2,1)}, bf16[1536,1024]{1,0:T(8,128)(2,1)}, bf16[102...) custom-call(s32[3]{0:T(128)} %pad_add_fusion.refs_0_.where_ref, bf16[128,768]{1,0:T(8,128)(2,1)} %slice.221.dc_ref, ...), custom_call_target="tpu_custom_call" | custom-call | flops 2415919104 | bytes 20343820 | tf_op jit(solution)/shard_map/self_backward/pallas_call | solution.py:106
  496.5 4.0 pad_maximum_fusion.1
  515.0 3.9 pad_maximum_fusion
  519.5 21.4 %swin_backward.1 = (bf16[288,768]{1,0:T(8,128)(2,1)}, bf16[288,2304]{1,0:T(8,128)(2,1)}, f32[288,768]{1,0:T(8,128)}, f32[2,768]{1,0:T(2,128)}) custom-call(s32[3]{0:T(128)} %pad_add_fusion.refs_0_.where_ref, bf16[288,768]{1,0:T(8,128)(2,1)} %reshape.181.refs_1_, f32[288,768]{1,0:T(8,128)} %get-tuple-element.58.refs_0_.refs_2_, ...), custom_call_target="tpu_custom_call" | custom-call | flops 2378170368 | bytes 36796428 | tf_op jit(solution)/shard_map/swin_backward/pallas_call | solution.py:106
  559.4 9.5 fusion.1
  576.0 8.1 collective-permute-done.1
  586.9 83.8 %reduce-scatter.14.cloned.1.call-done = bf16[192,768]{1,0:T(8,128)(2,1)} async-done(((bf16[6144,768]{1,0:T(8,128)(2,1)}), bf16[192,768]{1,0:T(8,128)(2,1)}) %reduce-scatter.14.cloned.1.call-update) | async-done | bytes 294928 | tf_op jit(solution)/shard_map/reduce_scatter | solution.py:894
  673.5 137.3 %reduce-scatter.12.cloned.1.call-done = bf16[192,768]{1,0:T(8,128)(2,1)} async-done(((bf16[6144,768]{1,0:T(8,128)(2,1)}), bf16[192,768]{1,0:T(8,128)(2,1)}) %reduce-scatter.12.cloned.1.call-update) | async-done | bytes 294928 | tf_op jit(solution)/shard_map/reduce_scatter | solution.py:894
  813.2 143.1 %reduce-scatter.10.cloned.1.call-done = bf16[208,768]{1,0:T(8,128)(2,1)} async-done(((bf16[6656,768]{1,0:T(8,128)(2,1)}), bf16[208,768]{1,0:T(8,128)(2,1)}) %reduce-scatter.10.cloned.1.call-update) | async-done | bytes 319504 | tf_op jit(solution)/shard_map/reduce_scatter | solution.py:894
  (201 shorter events, 84.0 us)
Async XLA Ops:
  7.2 5.6 copy-start.14
  7.2 92.7 %all-gather.11.cloned.1.call-start = ((), (), s32[]{:S(2)}) async-start(), calls=%async_computation.5 | async-start | bytes 10543104 | tf_op jit(solution)/shard_map/all_gather | solution.py:694
  11.0 115.0 %all-gather.19.cloned.1.call-start = ((), (), s32[]{:S(2)}) async-start(), calls=%async_computation.14 | async-start | bytes 1769472 | tf_op jit(solution)/shard_map/all_gather | solution.py:717
  11.8 155.0 %all-gather.21.cloned.1.call-start = ((), (), s32[]{:S(2)}) async-start(), calls=%async_computation.15 | async-start | bytes 1769472 | tf_op jit(solution)/shard_map/all_gather | solution.py:718
  12.5 228.7 %all-gather.15.cloned.1.call-start = ((), (), s32[]{:S(2)}) async-start(), calls=%async_computation.7 | async-start | bytes 9732096 | tf_op jit(solution)/shard_map/all_gather | solution.py:694
  13.7 254.1 %all-gather.13.cloned.1.call-start = ((), (), s32[]{:S(2)}) async-start(), calls=%async_computation.6 | async-start | bytes 1769472 | tf_op jit(solution)/shard_map/all_gather | solution.py:749
  126.0 15.6 %copy-start.15 = (f32[73728]{0:T(1024)S(1)}, f32[73728]{0:T(1024)}, u32[]{:S(2)}) copy-start(f32[73728]{0:T(1024)} %param.19) | copy-start | bytes 884740
  126.0 15.7 %copy-start.16 = (f32[73728]{0:T(1024)S(1)}, f32[73728]{0:T(1024)}, u32[]{:S(2)}) copy-start(f32[73728]{0:T(1024)} %param.20) | copy-start | bytes 884740
  141.6 211.6 %all-gather.17.cloned.1.call-start = ((), (), s32[]{:S(2)}) async-start(), calls=%async_computation.8 | async-start | bytes 9732096 | tf_op jit(solution)/shard_map/all_gather | solution.py:694
  142.7 249.8 %all-gather.23.cloned.1.call-start = ((), (), s32[]{:S(2)}) async-start(), calls=%async_computation.16 | async-start | bytes 1769472 | tf_op jit(solution)/shard_map/all_gather | solution.py:791
  142.9 11.5 %collective-permute-start = (bf16[2,6,24,768]{3,2,1,0:T(8,128)(2,1)S(1)}, bf16[2,6,24,768]{3,2,1,0:T(8,128)(2,1)S(1)}, u32[]{:S(2)}, u32[]{:S(2)}) collective-permute-start(bf16[2,6,24,768]{3,2,1,0:T(8,128)(2,1)S(1)} %get-tuple-element.111), channel_id=1, source_target_pairs={{0,7},{1,0},{2,1},{3,2},{4,3},{5,4},{6,5},{7,6},{8,15},{9,8},{10,9... | collective-permute-start | bytes 1327112 | tf_op jit(solution)/shard_map/ppermute | solution.py:722
  296.1 176.0 %reduce-scatter.6.cloned.1.call-start = ((), (), s32[]{:S(2)}) async-start(), calls=%async_computation.9 | async-start | bytes 3538944 | tf_op jit(solution)/shard_map/reduce_scatter | solution.py:825
  413.3 10.3 %copy-start.3 = (bf16[1024,768]{1,0:T(8,128)(2,1)S(1)}, bf16[1024,768]{1,0:T(8,128)(2,1)}, u32[]{:S(2)}) copy-start(bf16[1024,768]{1,0:T(8,128)(2,1)} %get-tuple-element.68) | copy-start | bytes 4718596
  426.9 129.2 %reduce-scatter.8.cloned.1.call-start = ((), (), s32[]{:S(2)}) async-start(), calls=%async_computation.10 | async-start | bytes 1769472 | tf_op jit(solution)/shard_map/reduce_scatter | solution.py:870
  473.7 15.9 %copy-start.30 = (bf16[288,3072]{1,0:T(8,128)(2,1)S(1)}, bf16[288,3072]{1,0:T(8,128)(2,1)}, u32[]{:S(2)}) copy-start(bf16[288,3072]{1,0:T(8,128)(2,1)} %get-tuple-element.103) | copy-start | bytes 5308420
  473.7 15.9 %copy-start.31 = (bf16[288,768]{1,0:T(8,128)(2,1)S(1)}, bf16[288,768]{1,0:T(8,128)(2,1)}, u32[]{:S(2)}) copy-start(bf16[288,768]{1,0:T(8,128)(2,1)} %get-tuple-element.102) | copy-start | bytes 1327108
  489.6 181.1 %reduce-scatter.14.cloned.1.call-start = ((), (), s32[]{:S(2)}) async-start(), calls=%async_computation.13 | async-start | bytes 9732096 | tf_op jit(solution)/shard_map/reduce_scatter | solution.py:894
  500.5 310.2 %reduce-scatter.12.cloned.1.call-start = ((), (), s32[]{:S(2)}) async-start(), calls=%async_computation.12 | async-start | bytes 9732096 | tf_op jit(solution)/shard_map/reduce_scatter | solution.py:894
  518.9 437.4 %reduce-scatter.10.cloned.1.call-start = ((), (), s32[]{:S(2)}) async-start(), calls=%async_computation.11 | async-start | bytes 10543104 | tf_op jit(solution)/shard_map/reduce_scatter | solution.py:894
  519.5 22.2 %copy-start.27 = (bf16[288,768]{1,0:T(8,128)(2,1)S(1)}, bf16[288,768]{1,0:T(8,128)(2,1)}, u32[]{:S(2)}) copy-start(bf16[288,768]{1,0:T(8,128)(2,1)} %get-tuple-element.88) | copy-start | bytes 1327108
  573.0 11.9 %collective-permute-start.2 = (f32[6,24,768]{2,1,0:T(8,128)S(1)}, f32[6,24,768]{2,1,0:T(8,128)S(1)}, u32[]{:S(2)}, u32[]{:S(2)}) collective-permute-start(f32[6,24,768]{2,1,0:T(8,128)S(1)} %fusion.32), channel_id=1, source_target_pairs={{0,1},{1,2},{2,3},{3,4},{4,5},{5,6},{6,7},{7,0},{8,9},{9,10},{10,1... | collective-permute-start | bytes 1327112 | tf_op jit(solution)/shard_map/ppermute | solution.py:952
  573.2 10.9 %collective-permute-start.1 = (bf16[6,24,768]{2,1,0:T(8,128)(2,1)S(1)}, bf16[6,24,768]{2,1,0:T(8,128)(2,1)S(1)}, u32[]{:S(2)}, u32[]{:S(2)}) collective-permute-start(bf16[6,24,768]{2,1,0:T(8,128)(2,1)S(1)} %fusion.48), channel_id=1, source_target_pairs={{0,1},{1,2},{2,3},{3,4},{4,5},{5,6},{6,7},{7,0},{8,9},{9,10},{10,1... | collective-permute-start | bytes 663560 | tf_op jit(solution)/shard_map/ppermute | solution.py:952
  576.0 9.9 %copy-start.4 = (f32[128,768]{1,0:T(8,128)S(1)}, f32[128,768]{1,0:T(8,128)}, u32[]{:S(2)}) copy-start(f32[128,768]{1,0:T(8,128)} %get-tuple-element.63.y1_ref) | copy-start | bytes 1179652
  576.0 9.9 %copy-start.7 = (bf16[128,1536]{1,0:T(8,128)(2,1)S(1)}, bf16[128,1536]{1,0:T(8,128)(2,1)}, u32[]{:S(2)}) copy-start(bf16[128,1536]{1,0:T(8,128)(2,1)} %reduce-scatter.6.cloned.1.call-done) | copy-start | bytes 1179652
  (24 other events, 51.0 us)
Sparse Core Ops, SparseCore 0:
  11.5 88.3 all-gather.10
  101.8 24.1 all-gather.18
  127.9 27.8 all-gather.20
  159.1 82.0 all-gather.14
  243.5 24.2 all-gather.12
  271.1 82.0 all-gather.16
  355.7 24.3 all-gather.22
  427.0 45.0 reduce-scatter.5
  489.7 38.4 reduce-scatter.7
  535.0 135.7 reduce-scatter.13
  676.6 134.0 reduce-scatter.11
  817.6 138.6 reduce-scatter.9

commit v2 on v1

v2 whole, which is shorter than its diff:
```python
import jax
import jax.numpy as jnp
from jax import lax
from jax.experimental import pallas as pl
from jax.experimental.pallas import tpu as pltpu
from jax.sharding import PartitionSpec as P

D = 768
HEADS = 12
HD = 64
FF = 3072
PAIRS = HEADS // 2
PW = 2 * HD
SCALE = HD ** (-0.5)

EPS = 1e-05
NEG = -1e30

bf16 = jnp.bfloat16
f32 = jnp.float32
VMEM_LIMIT = 56 * 1024 * 1024


def nn(left, right):
    return lax.dot_general(left, right, (((1,), (0,)), ((), ())), preferred_element_type=f32)


def nt(left, right):
    return lax.dot_general(left, right, (((1,), (1,)), ((), ())), preferred_element_type=f32)


def tn(left, right):
    return lax.dot_general(left, right, (((0,), (0,)), ((), ())), preferred_element_type=f32)


def norm_parts(rows):
    centre = jnp.mean(rows, axis=-1, keepdims=True)
    centred = rows - centre
    spread = jnp.mean(centred * centred, axis=-1, keepdims=True)
    inverse = lax.rsqrt(spread + EPS)
    return centred * inverse, inverse


def norm(rows, gain):
    return norm_parts(rows)[0] * gain


def norm_back(rows, gain, grad):
    unit, inverse = norm_parts(rows)
    grad_gain = jnp.sum(grad * unit, axis=0, keepdims=True)
    scaled = grad * gain
    first = jnp.mean(scaled, axis=-1, keepdims=True)
    second = jnp.mean(scaled * unit, axis=-1, keepdims=True)
    return inverse * (scaled - first - unit * second), grad_gain


def lane_half(half, value, dtype):
    lanes = lax.broadcasted_iota(jnp.int32, (1, PW), 1)
    return jnp.where((lanes // HD) == half, value, 0.0).astype(dtype)


def low_half(rows):
    return lax.broadcasted_iota(jnp.int32, (rows, PW), 1) < HD


def column(table, index):
    lanes = lax.broadcasted_iota(jnp.int32, table.shape, 1)
    return jnp.sum(jnp.where(lanes == index, table, 0.0), axis=-1, keepdims=True)


def pair_cols(pair, base=0):
    return pl.ds(pl.multiple_of(base + pair * PW, PW), PW)


def softmax_rows(scores):
    highest = jnp.max(scores, axis=-1, keepdims=True)
    raised = jnp.exp(scores - highest)
    totals = jnp.sum(raised, axis=-1, keepdims=True)
    return raised * (1.0 / totals), highest + jnp.log(totals)


class Stored:
    def __init__(self, arrays, lanes=(), joint=None):
        self.arrays = list(arrays)
        self.lanes = tuple(lanes)
        self.joint = joint


def stage_bits(lane):
    return (1, 2) if lane == 0 else (2, 1)


def relative(lane, core, first, second):
    bit_one, bit_two = stage_bits(lane)
    return core | (first << bit_one) | (second << bit_two)


def local_copy(source, target, sem):
    pltpu.make_async_copy(source, target, sem).start()


def fetch(where_ref, stored, refs, index, target, sem):
    if stored.joint is not None:
        first, rows = stored.joint
        count = D // rows
        for k in range(count):
            piece = refs[0].at[index * count + k, first : first + rows]
            local_copy(piece, target.at[k * rows : (k + 1) * rows], sem)
        return
    if len(refs) == 1:
        local_copy(refs[0].at[index], target, sem)
        return
    page, blk = where_ref[3], where_ref[4]
    count = len(stored.lanes)
    for number, lane in enumerate(stored.lanes):
        for core in range(2):
            for second in range(2):
                for first in range(2):
                    ref = refs[4 * number + 2 * core + second]
                    piece = ref.at[(index ^ page) + 4 * first]
                    rows = piece.shape[0]
                    owner = blk ^ relative(lane, core, first, second)
                    start = pl.multiple_of((owner * count + number) * rows, rows)
                    local_copy(piece, target.at[pl.ds(start, rows)], sem)


def fetch_up(where_ref, stored, refs, target, sem):
    if len(refs) == 1:
        local_copy(refs[0], target, sem)
        return
    page, blk = where_ref[3], where_ref[4]
    for core in range(2):
        for second in range(2):
            for first in range(2):
                ref = refs[2 * core + second]
                near = (blk ^ relative(stored.lanes[0], 0, first, second)) >> 1
                for origin in range(4):
                    piece = ref.at[(origin ^ page) + 4 * first]
                    rows = piece.shape[0] // 2
                    spot = pl.ds(pl.multiple_of((origin * 4 + near) * rows, rows), rows)
                    for k in range(2):
                        group = 2 * ((blk & 1) ^ core) + k
                        local_copy(piece.at[k * rows : (k + 1) * rows], target.at[group, spot], sem)


class Loads:
    def __init__(self, held, sems, plan):
        self.held, self.sems, self.plan, self.done = held, sems, plan, set()

    def ready(self, *places):
        for place in places:
            if place not in self.done:
                self.done.add(place)
                start, count = self.plan[place]
                span = self.held.at[start : start + count]
                pltpu.make_async_copy(span, span, self.sems.at[place]).wait()

    def __getitem__(self, place):
        self.ready(place)
        return self.held[self.plan[place][0]]

    def part(self, place, k):
        return self.held[self.plan[place][0] + k]


def call(kernel, outs, ins, scratch=(), smem=1, loads=(), slots=None, flops=0, name=None):
    def whole(value):
        zeros = (0,) * len(value.shape)
        return pl.BlockSpec(value.shape, lambda i: zeros, pipeline_mode=pl.Buffered(1))

    specs = []
    for index, value in enumerate(ins):
        if index < smem:
            specs.append(pl.BlockSpec(memory_space=pltpu.SMEM))
        else:
            specs.append(whole(value))
    single = not isinstance(outs, list)
    shapes = [outs] if single else outs
    count_in, count_out = len(ins), len(shapes)
    unique, plan, size = [], [], 0
    for stored, which in loads:
        if stored not in unique:
            unique.append(stored)
        width = 4 if which is None else 1
        plan.append((size, width))
        size += width
    arrays = [array for stored in unique for array in stored.arrays]
    gathered, slot_scratch = [], []
    if slots:
        gathered, part, own = slots
        blocks = len(gathered) if len(gathered) > 1 else gathered[0].shape[0]
        slot_scratch = [pltpu.VMEM((blocks, own, D), bf16), pltpu.SemaphoreType.DMA]
    held = [pltpu.VMEM((size, D, D), bf16), pltpu.SemaphoreType.DMA((len(plan),))] if loads else []

    def body(*refs):
        inner = list(refs[:count_in])
        at = count_in
        taken = {}
        for stored in unique:
            taken[id(stored)] = refs[at : at + len(stored.arrays)]
            at += len(stored.arrays)
        pieces = refs[at : at + len(gathered)]
        at += len(gathered)
        results = list(refs[at : at + count_out])
        rest = list(refs[at + count_out :])
        if slots:
            together, slot_sem = rest[:2]
            rest = rest[2:]
            rows = slice(part * own, (part + 1) * own)
            if len(pieces) == 1:
                local_copy(pieces[0].at[:, rows], together, slot_sem)
            for k, piece in enumerate(pieces if len(pieces) > 1 else ()):
                local_copy(piece.at[rows], together.at[inner[0][4] ^ k], slot_sem)
            inner.append(together)
        if not loads:
            kernel(*inner, *results, *rest)
            return
        kept, sems = rest[-2], rest[-1]
        for place, (stored, which) in enumerate(loads):
            mine, (start, width) = taken[id(stored)], plan[place]
            if which is None:
                fetch_up(inner[0], stored, mine, kept.at[start : start + width], sems.at[place])
            else:
                fetch(inner[0], stored, mine, which, kept.at[start], sems.at[place])
        if slots:
            pltpu.make_async_copy(together, together, slot_sem).wait()
        weights = Loads(kept, sems, plan)
        kernel(*inner, weights, *results, *rest[:-2])
        weights.ready(*range(len(plan)))

    moved = sum(v.size * v.dtype.itemsize for v in list(ins) + shapes) + size * D * D * 2
    result = pl.pallas_call(
        body,
        grid=(1,),
        out_shape=shapes,
        in_specs=specs + [pl.BlockSpec(memory_space=pl.ANY)] * (len(arrays) + len(gathered)),
        out_specs=[whole(value) for value in shapes],
        scratch_shapes=slot_scratch + list(scratch) + held,
        compiler_params=pltpu.CompilerParams(
            vmem_limit_bytes=VMEM_LIMIT, dimension_semantics=("arbitrary",)
        ),
        cost_estimate=pl.CostEstimate(flops=int(flops), bytes_accessed=int(moved), transcendentals=0),
        name=name,
    )(*ins, *arrays, *gathered)
    return result[0] if single else result


def sds(shape, dtype):
    return jax.ShapeDtypeStruct(shape, dtype)


def self_bias(bias_ref, first_row, live):
    rows, slots = bias_ref.shape
    keys = lax.broadcasted_iota(jnp.int32, (rows, slots), 1)
    places = lax.broadcasted_iota(jnp.int32, (rows, slots), 0) + first_row
    bias_ref[...] = jnp.where((keys <= places) & (keys < live), 0.0, NEG)


def self_forward_kernel(
    where_ref, g_ref, y_ref, w, b_ref, q_ref, kv_ref, lse_ref, o_ref, y1_ref, c_ref, bias_ref
):
    first_row, live = where_ref[0], where_ref[1]
    slots, own = b_ref.shape[0], q_ref.shape[0]
    tile = 256
    group = tile // own
    w.ready(0, 1)

    def project(i, carry):
        rows = pl.ds(pl.multiple_of(i * tile, tile), tile)
        part = y_ref[pl.ds(i * group, group)].reshape(tile, D)
        normed = norm(part.astype(f32), g_ref[1:2, :]).astype(bf16)
        b_ref[rows, :] = normed
        kv_ref[rows, 0:D] = nn(normed, w[0]).astype(bf16)
        kv_ref[rows, D : 2 * D] = nn(normed, w[1]).astype(bf16)
        return carry

    lax.fori_loop(0, slots // tile, project, 0)
    mine = pl.ds(pl.multiple_of(first_row, 16), own)
    q_ref[...] = nn(b_ref[mine, :], w[2]).astype(bf16)
    self_bias(bias_ref, first_row, live)
    lse_ref[...] = jnp.zeros_like(lse_ref)
    lanes = lax.broadcasted_iota(jnp.int32, lse_ref.shape, 1)
    low = low_half(own)

    def attend(pair, carry):
        queries = q_ref[:, pair_cols(pair)]
        keys = kv_ref[:, pair_cols(pair)]
        values = kv_ref[:, pair_cols(pair, D)]
        mixed = []
        table = lse_ref[...]
        for half in range(2):
            scores = nt(queries * lane_half(half, SCALE, bf16), keys) + bias_ref[...]
            chances, log_totals = softmax_rows(scores)
            mixed.append(nn(chances.astype(bf16), values))
            table = jnp.where(lanes == 2 * pair + half, log_totals, table)
        lse_ref[...] = table
        o_ref[:, pair_cols(pair)] = jnp.where(low, mixed[0], mixed[1]).astype(bf16)
        return carry

    lax.fori_loop(0, PAIRS, attend, 0)
    y1 = y_ref[where_ref[4]].astype(f32) + nn(o_ref[...], w[3])
    y1_ref[...] = y1
    c_ref[...] = norm(y1, g_ref[3:4, :]).astype(bf16)


def window_bias(rows, side, row_split, col_split):
    def flags(shape, dim):
        token = lax.broadcasted_iota(jnp.int32, shape, dim)
        row, col = token // side, token % side
        return jnp.where(row >= side // 2, row_split, 0) + jnp.where(
            col >= side // 2, 2 * col_split, 0
        )

    return jnp.where(flags((rows, rows), 0) == flags((rows, rows), 1), 0.0, NEG)


def swin_forward_kernel(
    side, where_ref, x_ref, g_ref, w, a_ref, qkv_ref, lse_ref, o_ref, v1_ref, e_ref, bias_ref
):
    is_last = where_ref[2]
    tokens = x_ref.shape[0]
    rows = side * side
    windows = tokens // rows
    x = x_ref[...].astype(f32)
    normed = norm(x, g_ref[0:1, :]).astype(bf16)
    a_ref[...] = normed
    for k in range(3):
        qkv_ref[:, k * D : (k + 1) * D] = nn(normed, w[k]).astype(bf16)
    for win in range(windows):
        bias_ref[win] = window_bias(rows, side, is_last, 1 if win == windows - 1 else 0)
    lse_ref[...] = jnp.zeros_like(lse_ref)
    lanes = lax.broadcasted_iota(jnp.int32, (rows, lse_ref.shape[1]), 1)
    low = low_half(rows)

    def attend(pair, carry):
        for win in range(windows):
            at = slice(win * rows, (win + 1) * rows)
            queries = qkv_ref[at, pair_cols(pair)]
            keys = qkv_ref[at, pair_cols(pair, D)]
            values = qkv_ref[at, pair_cols(pair, 2 * D)]
            mixed = []
            table = lse_ref[at, :]
            for half in range(2):
                scores = nt(queries * lane_half(half, SCALE, bf16), keys) + bias_ref[win]
                chances, log_totals = softmax_rows(scores)
                mixed.append(nn(chances.astype(bf16), values))
                table = jnp.where(lanes == 2 * pair + half, log_totals, table)
            lse_ref[at, :] = table
            o_ref[at, pair_cols(pair)] = jnp.where(low, mixed[0], mixed[1]).astype(bf16)
        return carry

    lax.fori_loop(0, PAIRS, attend, 0)
    v1 = x + nn(o_ref[...], w[3])
    v1_ref[...] = v1
    e_ref[...] = norm(v1, g_ref[2:3, :]).astype(bf16)


def cross_forward_kernel(
    where_ref,
    c_ref,
    e_ref,
    cot_ref,
    w,
    qa_ref,
    kvb_ref,
    doa_ref,
    kva_ref,
    qb_ref,
    stats_ref,
):
    slots, tokens = qa_ref.shape[0], e_ref.shape[0]
    tile = 256
    normed = e_ref[...]
    for k in range(2):
        kva_ref[:, k * D : (k + 1) * D] = nn(normed, w[k]).astype(bf16)
    qb_ref[...] = nn(normed, w[2]).astype(bf16)
    w.ready(3, 4, 5, 6)
    group = tile // cot_ref.shape[1]

    def project(i, carry):
        rows = pl.ds(pl.multiple_of(i * tile, tile), tile)
        part = c_ref[rows, :]
        qa_ref[rows, :] = nn(part, w[3]).astype(bf16)
        for k in range(2):
            kvb_ref[rows, k * D : (k + 1) * D] = nn(part, w[4 + k]).astype(bf16)
        cot = cot_ref[pl.ds(i * group, group)].reshape(tile, D)
        doa_ref[rows, :] = nt(cot, w[6]).astype(bf16)
        return carry

    lax.fori_loop(0, slots // tile, project, 0)
    stats_ref[...] = jnp.zeros_like(stats_ref)

    def page_stats(pair, carry):
        keys = kva_ref[:, pair_cols(pair)]
        values = kva_ref[:, pair_cols(pair, D)]
        for half in range(2):
            head = 2 * pair + half
            keys_h = keys * lane_half(half, SCALE, bf16)
            values_h = values * lane_half(half, 1.0, bf16)
            for i in range(slots // tile):
                rows = slice(i * tile, (i + 1) * tile)
                scores = nt(keys_h, qa_ref[rows, pair_cols(pair)])
                highest = jnp.max(scores, axis=0, keepdims=True)
                raised = jnp.exp(scores - highest)
                grads = nt(values_h, doa_ref[rows, pair_cols(pair)])
                stats_ref[0, pl.ds(head, 1), rows] = highest
                stats_ref[1, pl.ds(head, 1), rows] = jnp.sum(raised, axis=0, keepdims=True)
                stats_ref[2, pl.ds(head, 1), rows] = jnp.sum(raised * grads, axis=0, keepdims=True)
        return carry

    lax.fori_loop(0, PAIRS, page_stats, 0)


def vq_forward_kernel(where_ref, qb_ref, kvb_ref, lse_ref, ob_ref):
    live = where_ref[1]
    tokens, slots = qb_ref.shape[0], kvb_ref.shape[0]
    lse_ref[...] = jnp.zeros_like(lse_ref)
    lanes = lax.broadcasted_iota(jnp.int32, lse_ref.shape, 1)
    low = low_half(tokens)
    bias = jnp.where(lax.broadcasted_iota(jnp.int32, (1, slots), 1) < live, 0.0, NEG)

    def attend(pair, carry):
        queries = qb_ref[:, pair_cols(pair)]
        keys = kvb_ref[:, pair_cols(pair)]
        values = kvb_ref[:, pair_cols(pair, D)]
        mixed = []
        table = lse_ref[...]
        for half in range(2):
            scores = nt(queries * lane_half(half, SCALE, bf16), keys) + bias
            chances, log_totals = softmax_rows(scores)
            mixed.append(nn(chances.astype(bf16), values))
            table = jnp.where(lanes == 2 * pair + half, log_totals, table)
        lse_ref[...] = table
        ob_ref[:, pair_cols(pair)] = jnp.where(low, mixed[0], mixed[1]).astype(bf16)
        return carry

    lax.fori_loop(0, PAIRS, attend, 0)


GELU_A = 0.7978845608028654
GELU_B = 0.044715


def mlp_kernel(
    where_ref,
    v1_ref,
    ob_ref,
    cot_ref,
    g_ref,
    w,
    v3_ref,
    h_ref,
    act_ref,
    du_ref,
    g2_ref,
    dz_ref,
    dob_ref,
    dg_ref,
    v2_ref,
    sum_ref,
    dh_ref,
):
    v2 = v1_ref[...] + nn(ob_ref[...], w[0])
    v2_ref[...] = v2
    sum_ref[...] = v2
    h_ref[...] = norm(v2, g_ref[4:5, :]).astype(bf16)
    dh_ref[...] = jnp.zeros_like(dh_ref)
    w.ready(1, 2, 3, 4, 5)

    def chunk(k, carry):
        up, down = w.part(1, k), w.part(2, k)
        at = pl.ds(pl.multiple_of(k * D, D), D)
        u = nn(h_ref[...], up)
        squared = u * u
        bend = jnp.tanh(GELU_A * (u + GELU_B * u * squared))
        act = (0.5 * u * (1.0 + bend)).astype(bf16)
        act_ref[:, at] = act
        slope = 0.5 * (1.0 + bend) + 0.5 * u * (1.0 - bend * bend) * GELU_A * (
            1.0 + 3.0 * GELU_B * squared
        )
        du = (nt(cot_ref[...], down) * slope).astype(bf16)
        du_ref[:, at] = du
        sum_ref[...] += nn(act, down)
        dh_ref[...] += nt(du, up)
        return carry

    lax.fori_loop(0, FF // D, chunk, 0)
    v3_ref[...] = sum_ref[...].astype(bf16)
    part, dg = norm_back(v2_ref[...], g_ref[4:5, :], dh_ref[...])
    dg_ref[...] = dg
    g2 = cot_ref[...].astype(f32) + part
    g2_ref[...] = g2
    dz = g2.astype(bf16)
    dz_ref[...] = dz
    dob_ref[...] = nt(dz, w[0]).astype(bf16)


def vq_backward_kernel(
    where_ref, qb_ref, kvb_ref, dob_ref, lse_ref, dqb_ref, dkvbt_ref
):
    live = where_ref[1]
    tokens, slots = qb_ref.shape[0], kvb_ref.shape[0]
    bias = jnp.where(lax.broadcasted_iota(jnp.int32, (1, slots), 1) < live, 0.0, NEG)
    low = low_half(tokens)

    def back(pair, carry):
        queries = qb_ref[:, pair_cols(pair)]
        keys = kvb_ref[:, pair_cols(pair)]
        values = kvb_ref[:, pair_cols(pair, D)]
        grads = dob_ref[:, pair_cols(pair)]
        queries_t = (queries * SCALE).astype(f32).T.astype(bf16)
        grads_t = grads.astype(f32).T.astype(bf16)
        parts = []
        for half in range(2):
            own = slice(half * HD, (half + 1) * HD)
            scores = nt(queries * lane_half(half, SCALE, bf16), keys) + bias
            chances = jnp.exp(scores - column(lse_ref[...], 2 * pair + half))
            slopes = nt(grads * lane_half(half, 1.0, bf16), values)
            centre = jnp.sum(chances * slopes, axis=-1, keepdims=True)
            ds = (chances * (slopes - centre)).astype(bf16)
            parts.append(nn(ds, keys))
            at = pair * PW + half * HD
            dkvbt_ref[pl.ds(pl.multiple_of(at, HD), HD), :] = nn(queries_t[own], ds).astype(bf16)
            dkvbt_ref[pl.ds(pl.multiple_of(D + at, HD), HD), :] = nn(
                grads_t[own], chances.astype(bf16)
            ).astype(bf16)
        dqb_ref[:, pair_cols(pair)] = (jnp.where(low, parts[0], parts[1]) * SCALE).astype(bf16)
        return carry

    lax.fori_loop(0, PAIRS, back, 0)


def hand_out(where_ref, held, outs):
    if len(outs) == 1:
        outs[0][...] = held[...]
        return
    rows = outs[0].shape[1]
    for core, out in enumerate(outs):
        for k in range(4):
            start = pl.multiple_of((where_ref[4] ^ (2 * k + core)) * rows, rows)
            out[k] = held[pl.ds(start, rows), :]


def qv_backward_kernel(
    where_ref,
    qa_ref,
    kva_ref,
    doa_ref,
    lse_ref,
    centre_ref,
    dkvbt_ref,
    w,
    dqat_ref,
    dkva_ref,
    *rest,
):
    dc_refs, held = rest[:-1], rest[-1]
    slots, tokens = qa_ref.shape[0], kva_ref.shape[0]
    low = low_half(tokens)
    tile = 512

    def back(pair, carry):
        keys = kva_ref[:, pair_cols(pair)]
        values = kva_ref[:, pair_cols(pair, D)]
        keys_t = (keys * SCALE).astype(f32).T.astype(bf16)
        values_t = values.astype(f32).T.astype(bf16)
        for i in range(slots // tile):
            rows = slice(i * tile, (i + 1) * tile)
            queries = qa_ref[rows, pair_cols(pair)]
            grads = doa_ref[rows, pair_cols(pair)]
            dk, dv, mixed = [], [], []
            for half in range(2):
                head = 2 * pair + half
                own = slice(half * HD, (half + 1) * HD)
                scores = nt(keys * lane_half(half, SCALE, bf16), queries)
                chances = jnp.exp(scores - lse_ref[pl.ds(head, 1), rows])
                slopes = nt(values * lane_half(half, 1.0, bf16), grads)
                ds = (chances * (slopes - centre_ref[pl.ds(head, 1), rows])).astype(bf16)
                rounded = chances.astype(bf16)
                mixed.append(nn(values_t[own], rounded))
                dqat_ref[pl.ds(pl.multiple_of(head * HD, HD), HD), rows] = nn(
                    keys_t[own], ds
                ).astype(bf16)
                dk.append(nn(ds, queries))
                dv.append(nn(rounded, grads))
            held[rows, pair_cols(pair, D)] = jnp.concatenate(mixed, axis=0).T.astype(bf16)
            dk_now = jnp.where(low, dk[0], dk[1]) * SCALE
            dv_now = jnp.where(low, dv[0], dv[1])
            if i == 0:
                dk_sum, dv_sum = dk_now, dv_now
            else:
                dk_sum, dv_sum = dk_sum + dk_now, dv_sum + dv_now
        dkva_ref[:, pair_cols(pair)] = dk_sum.astype(bf16)
        dkva_ref[:, pair_cols(pair, D)] = dv_sum.astype(bf16)
        return carry

    lax.fori_loop(0, PAIRS, back, 0)
    for i in range(slots // tile):
        cols = slice(i * tile, (i + 1) * tile)
        total = nn(w[0], dqat_ref[:, cols])
        total += nn(w[1], dkvbt_ref[0:D, cols])
        total += nn(w[2], dkvbt_ref[D : 2 * D, cols])
        held[cols, 0:D] = total.T.astype(bf16)
    hand_out(where_ref, held, dc_refs)


def swin_backward_kernel(
    side,
    where_ref,
    x_ref,
    v1_ref,
    g2_ref,
    g_ref,
    dkva_ref,
    dqb_ref,
    qkv_ref,
    lse_ref,
    w,
    dz_ref,
    dqkv_ref,
    grad_ref,
    dg_ref,
    bias_ref,
    do_ref,
):
    is_last = where_ref[2]
    tokens = x_ref.shape[0]
    rows = side * side
    windows = tokens // rows
    de = nt(dkva_ref[:, 0:D], w[0])
    de += nt(dkva_ref[:, D : 2 * D], w[1])
    de += nt(dqb_ref[...], w[2])
    part, dg3 = norm_back(v1_ref[...], g_ref[2:3, :], de)
    g1 = g2_ref[...] + part
    grad_ref[...] = g1
    dz = g1.astype(bf16)
    dz_ref[...] = dz
    do_ref[...] = nt(dz, w[3]).astype(bf16)
    for win in range(windows):
        bias_ref[win] = window_bias(rows, side, is_last, 1 if win == windows - 1 else 0)
    low = low_half(rows)

    def back(pair, carry):
        for win in range(windows):
            at = slice(win * rows, (win + 1) * rows)
            queries = qkv_ref[at, pair_cols(pair)]
            keys = qkv_ref[at, pair_cols(pair, D)]
            values = qkv_ref[at, pair_cols(pair, 2 * D)]
            grads = do_ref[at, pair_cols(pair)]
            dq, dk, dv = [], [], []
            for half in range(2):
                scores = nt(queries * lane_half(half, SCALE, bf16), keys) + bias_ref[win]
                chances = jnp.exp(scores - column(lse_ref[at, :], 2 * pair + half))
                slopes = nt(grads * lane_half(half, 1.0, bf16), values)
                centre = jnp.sum(chances * slopes, axis=-1, keepdims=True)
                ds = (chances * (slopes - centre)).astype(bf16)
                dq.append(nn(ds, keys))
                dk.append(tn(ds, queries))
                dv.append(tn(chances.astype(bf16), grads))
            for k, (pieces, factor) in enumerate(((dq, SCALE), (dk, SCALE), (dv, 1.0))):
                dqkv_ref[at, pair_cols(pair, k * D)] = (
                    jnp.where(low, pieces[0], pieces[1]) * factor
                ).astype(bf16)
        return carry

    lax.fori_loop(0, PAIRS, back, 0)
    da = nt(dqkv_ref[:, 0:D], w[4])
    da += nt(dqkv_ref[:, D : 2 * D], w[5])
    da += nt(dqkv_ref[:, 2 * D : 3 * D], w[6])
    part, dg1 = norm_back(x_ref[...].astype(f32), g_ref[0:1, :], da)
    grad_ref[...] += part
    dg_ref[...] = jnp.concatenate([dg1, dg3], axis=0)


def self_backward_kernel(
    where_ref,
    dc_ref,
    y1_ref,
    cot_ref,
    g_ref,
    q_ref,
    kv_ref,
    lse_ref,
    w,
    gy1_ref,
    dz_ref,
    dq_ref,
    dkvt_ref,
    dbq_ref,
    dg_ref,
    *rest,
):
    db_refs, (bias_ref, do_ref, db_held) = rest[:-3], rest[-3:]
    first_row, live = where_ref[0], where_ref[1]
    own_rows, slots = q_ref.shape[0], kv_ref.shape[0]
    part, dg = norm_back(y1_ref[...], g_ref[3:4, :], dc_ref[...].astype(f32))
    dg_ref[...] = dg
    gy1 = cot_ref[...].astype(f32) + part
    gy1_ref[...] = gy1
    dz = gy1.astype(bf16)
    dz_ref[...] = dz
    do_ref[...] = nt(dz, w[0]).astype(bf16)
    self_bias(bias_ref, first_row, live)
    low = low_half(own_rows)

    def back(pair, carry):
        queries = q_ref[:, pair_cols(pair)]
        keys = kv_ref[:, pair_cols(pair)]
        values = kv_ref[:, pair_cols(pair, D)]
        grads = do_ref[:, pair_cols(pair)]
        queries_t = (queries * SCALE).astype(f32).T.astype(bf16)
        grads_t = grads.astype(f32).T.astype(bf16)
        parts = []
        for half in range(2):
            own = slice(half * HD, (half + 1) * HD)
            scores = nt(queries * lane_half(half, SCALE, bf16), keys) + bias_ref[...]
            chances = jnp.exp(scores - column(lse_ref[...], 2 * pair + half))
            slopes = nt(grads * lane_half(half, 1.0, bf16), values)
            centre = jnp.sum(chances * slopes, axis=-1, keepdims=True)
            ds = (chances * (slopes - centre)).astype(bf16)
            parts.append(nn(ds, keys))
            at = pair * PW + half * HD
            dkvt_ref[pl.ds(pl.multiple_of(at, HD), HD), :] = nn(queries_t[own], ds).astype(bf16)
            dkvt_ref[pl.ds(pl.multiple_of(D + at, HD), HD), :] = nn(
                grads_t[own], chances.astype(bf16)
            ).astype(bf16)
        dq_ref[:, pair_cols(pair)] = (jnp.where(low, parts[0], parts[1]) * SCALE).astype(bf16)
        return carry

    lax.fori_loop(0, PAIRS, back, 0)
    dbq_ref[...] = nt(dq_ref[...], w[1])
    tile = 256
    for i in range(slots // tile):
        cols = slice(i * tile, (i + 1) * tile)
        total = nn(w[2], dkvt_ref[0:D, cols])
        total += nn(w[3], dkvt_ref[D : 2 * D, cols])
        db_held[cols, :] = total.T.astype(bf16)
    hand_out(where_ref, db_held, db_refs)


def query_end_kernel(
    where_ref, db_ref, dbq_ref, y_ref, gy1_ref, g_ref, y1_ref, oa_ref, w, grad_ref, dg_ref, out_ref
):
    part, dg = norm_back(
        y_ref[...].astype(f32), g_ref[1:2, :], db_ref[...].astype(f32) + dbq_ref[...]
    )
    grad_ref[...] = gy1_ref[...] + part
    dg_ref[...] = dg
    out_ref[...] = (y1_ref[...] + nn(oa_ref[...], w[0])).astype(bf16)


def weight_grad_call(where, weights, name, shards=0):
    arrays, items = [], []

    def place(value):
        for index, known in enumerate(arrays):
            if known is value:
                return index
        arrays.append(value)
        return len(arrays) - 1

    for lanes, kind, entries in weights:
        for index, (left, left_at, right, right_at, form) in enumerate(entries):
            items.append((lanes, kind, index, place(left), left_at, place(right), right_at, form))
    count = len(arrays)
    rows = D // 8 // len(weights[0][0])

    def body(*refs):
        where_ref = refs[0]
        ins = refs[1 : 1 + count]
        *outs, held, sems = refs[1 + count :]
        keep, send = outs[0], outs[-1]
        page, blk = where_ref[3], where_ref[4]

        def place_natural(slot, lane, kind, index):
            out, width = outs[0], 4 * D // shards
            each = width // 2
            for k in range(2 * D // width if kind == "up" else D // width):
                if kind == "up":
                    piece = held.at[slot, k * each : (k + 1) * each]
                    first = lane * width + (index % 2) * each
                    local_copy(
                        piece, out.at[2 * k + index // 2, first : first + each], sems.at[slot]
                    )
                else:
                    piece = held.at[slot, k * width : (k + 1) * width]
                    owner = index * (D // width) + k
                    spot = slice(lane * width, (lane + 1) * width)
                    local_copy(piece, out.at[owner, spot], sems.at[slot])

        def finish(slot):
            pltpu.make_async_copy(held.at[slot], held.at[slot], sems.at[slot]).wait()

        def place_up(slot, lane, index, core, first, second):
            near = (blk ^ relative(lane, 0, first, second)) >> 1
            group, k = index // 2, index % 2
            out = send if core else keep

            @pl.when(((blk & 1) ^ core) == group)
            def _():
                half = rows // 2
                for origin in range(4):
                    spot = first * 8 + second * 4 + (origin ^ page)
                    take = pl.ds(pl.multiple_of((origin * 4 + near) * half, half), half)
                    local_copy(
                        held.at[slot, take],
                        out.at[lane, spot, k * half : (k + 1) * half],
                        sems.at[slot],
                    )

        def place_rows(slot, lanes, index, core, first, second):
            out = send if core else keep
            for number, lane in enumerate(lanes):
                owner = blk ^ relative(lane, core, first, second)
                spot = first * 8 + second * 4 + (index ^ page)
                start = pl.multiple_of((owner * len(lanes) + number) * rows, rows)
                local_copy(held.at[slot, pl.ds(start, rows)], out.at[lane, spot], sems.at[slot])

        for step, (lanes, kind, index, left, left_at, right, right_at, form) in enumerate(items):
            slot = step % 2
            if step >= 2:
                finish(slot)
            lhs = ins[left][:, left_at * D : (left_at + 1) * D]
            if form == "tt":
                rhs = ins[right][right_at * D : (right_at + 1) * D, :]
                product = nt(lhs.astype(f32).T.astype(bf16), rhs)
            else:
                product = tn(lhs, ins[right][:, right_at * D : (right_at + 1) * D])
            held[slot] = product.astype(bf16)
            if shards:
                place_natural(slot, lanes[0], kind, index)
                continue
            for core in range(2):
                for first in range(2):
                    for second in range(2):
                        if kind == "up":
                            place_up(slot, lanes[0], index, core, first, second)
                        else:
                            place_rows(slot, lanes, index, core, first, second)
        for step in range(max(0, len(items) - 2), len(items)):
            finish(step % 2)

    shapes = [sds((2, 16, rows, D), bf16)] * 2
    if shards:
        shapes = [sds((shards, len(weights) * 4 * D // shards, D), bf16)]
    moved = 2 * len(items) * D * D + sum(v.size * 2 for v in arrays)
    return pl.pallas_call(
        body,
        grid=(1,),
        out_shape=shapes,
        in_specs=[pl.BlockSpec(memory_space=pltpu.SMEM)]
        + [
            pl.BlockSpec(v.shape, lambda i: (0, 0), pipeline_mode=pl.Buffered(1)) for v in arrays
        ],
        out_specs=[pl.BlockSpec(memory_space=pl.ANY)] * len(shapes),
        scratch_shapes=[pltpu.VMEM((2, D, D), bf16), pltpu.SemaphoreType.DMA((2,))],
        compiler_params=pltpu.CompilerParams(
            vmem_limit_bytes=VMEM_LIMIT, dimension_semantics=("arbitrary",)
        ),
        cost_estimate=pl.CostEstimate(
            flops=int(len(items) * 1.6e-6 * 1.1e15), bytes_accessed=int(moved), transcendentals=0
        ),
        name=name,
    )(where, *arrays)


def window_order(grid_rows, half):
    rows, cols, _ = grid_rows.shape
    rolled = jnp.roll(grid_rows, -half, axis=1)
    shaped = rolled.reshape(rows, cols // rows, rows, D).transpose(1, 0, 2, 3)
    return shaped.reshape(rows * cols, D)


def grid_order(tokens_in, rows, cols, half):
    shaped = tokens_in.reshape(cols // rows, rows, rows, D).transpose(1, 0, 2, 3)
    return jnp.roll(shaped.reshape(rows, cols, D), half, axis=1)


def after(value, *others):
    return lax.optimization_barrier((value, others))[0]


def swapped(value, axis, flip):
    count = lax.axis_size(axis)
    return lax.ppermute(value, axis, [(i, i ^ flip) for i in range(count)])


def from_pages(value):
    pages = lax.axis_size("page")
    return [value] + [swapped(value, "page", k) for k in range(1, pages)]


def spread_first(shares):
    parts = from_pages(jnp.stack(shares))
    return [jnp.stack([part[k] for part in parts]) for k in range(2)]


def spread_second(held):
    return [
        jnp.concatenate([held[0], swapped(held[0], "blk", 2)]),
        jnp.concatenate([held[1], swapped(held[1], "blk", 4)]),
    ]


def spread_third(near):
    return [swapped(near[0], "blk", 4), swapped(near[1], "blk", 2)]


def spread_core(held):
    return [swapped(value, "blk", 1) for value in held]


def lane_arrays(near, far, near_core, far_core, lane):
    return [near[lane], far[lane], near_core[lane], far_core[lane]]


def added(left, right):
    return (left.astype(f32) + right.astype(f32)).astype(bf16)


def collect_first(keep, send, *gate):
    got = swapped(send, "blk", 1)
    keep = after(keep, *gate)
    return [[added(keep[k, i : i + 8], got[k, i : i + 8]) for i in (0, 8)] for k in range(2)]


def collect_second(held, *gate):
    got = swapped(held[0][1], "blk", 2), swapped(held[1][1], "blk", 4)
    kept = after([held[0][0], held[1][0]], *gate)
    return [[added(kept[k][i : i + 4], got[k][i : i + 4]) for i in (0, 4)] for k in range(2)]


def collect_third(held, *gate):
    got = swapped(held[0][1], "blk", 4), swapped(held[1][1], "blk", 2)
    kept = after([held[0][0], held[1][0]], *gate)
    sums = [added(kept[k], got[k]) for k in range(2)]
    return [jnp.stack([sums[k][i] for k in range(2)]) for i in range(4)]


def collect_last(held, *gate):
    total = after(held[0], *gate).astype(f32)
    for k in range(1, 4):
        total = total + swapped(held[k], "page", k).astype(f32)
    return total


def collect_blocks(parts):
    if len(parts) == 1:
        return lax.psum_scatter(parts[0], "blk", scatter_dimension=0, tiled=True)
    keep, send = parts
    got = swapped(send, "blk", 1)
    chips = [added(keep[k], got[k]) for k in range(4)]
    total = chips[0].astype(f32)
    for k in range(1, 4):
        total = total + swapped(chips[k], "blk", 2 * k).astype(f32)
    return total.astype(bf16)


def summed_everywhere(value):
    for axis in ("blk", "page"):
        flip = 1
        while flip < lax.axis_size(axis):
            value = value + swapped(value, axis, flip)
            flip *= 2
    return value


def on_device(
    visual,
    query_tokens,
    answer_len,
    attn_swin,
    attn_self,
    attn_qv,
    attn_vq,
    mlp_up,
    mlp_down,
    norm_gains,
    visual_cot,
    query_cot,
):
    everyone = ("page", "blk")
    pages = lax.axis_size("page")
    page_here = lax.axis_index("page")
    blk_count = lax.axis_size("blk")
    blk_here = lax.axis_index("blk")
    shards = pages * blk_count
    rows_here, cols_all = visual.shape[1], visual.shape[2]
    half = rows_here // 2
    tokens = rows_here * cols_all
    q_rows = query_tokens.shape[1]
    slots = q_rows * blk_count
    share = attn_swin.shape[0] // D
    staged = pages == 4 and blk_count == 8 and share % 32 == 0
    gain_width = norm_gains.shape[0]
    core_here = blk_here % 2

    where = jnp.stack(
        [
            blk_here * q_rows,
            answer_len[0],
            (blk_here == blk_count - 1).astype(jnp.int32),
            page_here,
            blk_here,
        ]
    ).astype(jnp.int32)

    def flat_share(value):
        return value.astype(bf16).reshape(share, D)

    gain_pages = jnp.concatenate(from_pages(norm_gains.astype(bf16)))[None]
    gain_rows = jnp.pad(gain_pages, ((0, 15), (0, D - pages * gain_width)))
    slot_own = jnp.concatenate([query_tokens[0], query_cot[0], gain_rows], axis=0)
    slots_joined = lax.all_gather(slot_own, "blk", axis=0)
    slot_arrays = [slots_joined]
    gain_parts = slots_joined[:, 2 * q_rows, : pages * gain_width]
    gain_parts = gain_parts.reshape(blk_count, pages, gain_width)
    gains = jnp.take(gain_parts, jnp.arange(pages) ^ page_here, axis=1)
    gains = gains.transpose(1, 0, 2).reshape(8, D).astype(f32)
    if staged:
        a_z = spread_first([flat_share(attn_self), flat_share(attn_swin)])
        a_near = spread_second(a_z)
        c_z = spread_first(after([flat_share(attn_qv), flat_share(attn_vq)], a_z))
        a_far = spread_third(a_near)
        a_near_core, a_far_core = spread_core(a_near), spread_core(a_far)
        w_self, w_swin = [
            Stored(lane_arrays(a_near, a_far, a_near_core, a_far_core, k), (k,)) for k in range(2)
        ]
        up_groups = after(mlp_up, a_near).astype(bf16)
        up_groups = up_groups.reshape(share // 4, 2, 2, D).transpose(1, 2, 0, 3)
        mine = jnp.where(core_here == 0, up_groups[0], up_groups[1])
        other = swapped(jnp.where(core_here == 0, up_groups[1], up_groups[0]), "blk", 1)
        up_share = jnp.where(
            core_here == 0,
            jnp.concatenate([mine, other], axis=1),
            jnp.concatenate([other, mine], axis=1),
        ).reshape(share, D)
        d_z = spread_first(after([up_share, flat_share(mlp_down)], c_z))
        c_near = spread_second(after(c_z, a_far))
        c_far = spread_third(c_near)
        c_near_core, c_far_core = spread_core(c_near), spread_core(c_far)
        w_qv, w_vq = [
            Stored(lane_arrays(c_near, c_far, c_near_core, c_far_core, k), (k,)) for k in range(2)
        ]
        d_near = spread_second(after(d_z, c_far))
        d_far = spread_third(d_near)
        d_near_core, d_far_core = spread_core(d_near), spread_core(d_far)
        w_up, w_down = [
            Stored(lane_arrays(d_near, d_far, d_near_core, d_far_core, k), (k,)) for k in range(2)
        ]
    else:
        up_share = (
            mlp_up.astype(bf16).reshape(share // 4, 4, D).transpose(1, 0, 2).reshape(share, D)
        )
        joined = lax.all_gather(
            jnp.concatenate(
                [flat_share(v) for v in (attn_self, attn_swin, attn_qv, attn_vq, mlp_down)]
                + [up_share],
                axis=0,
            ),
            everyone,
            axis=0,
            tiled=True,
        ).reshape(shards, -1, D)
        w_self, w_swin, w_qv, w_vq, w_down = [
            Stored([joined[:, k * share : (k + 1) * share].reshape(4, D, D)]) for k in range(5)
        ]
        up_all = joined[:, 5 * share : 6 * share].reshape(shards, 4, share // 4, D)
        w_up = Stored([up_all.transpose(1, 0, 2, 3).reshape(4, D, D)])

    down_one = [(i, (i - 1) % blk_count) for i in range(blk_count)]
    up_one = [(i, (i + 1) % blk_count) for i in range(blk_count)]
    both = jnp.concatenate([visual, visual_cot], axis=0)
    if staged:
        both = after(both, a_near)
    lent = lax.ppermute(both[:, :half], "blk", down_one)
    both = jnp.concatenate([both[:, half:], lent], axis=1)
    vis_in = window_order(both[0], half)
    vis_cot = window_order(both[1], half)

    b_all, q_self, kv_self, lse_self, o_self, y1, c_own = call(
        self_forward_kernel,
        [
            sds((slots, D), bf16),
            sds((q_rows, D), bf16),
            sds((slots, 2 * D), bf16),
            sds((q_rows, 128), f32),
            sds((q_rows, D), bf16),
            sds((q_rows, D), f32),
            sds((q_rows, D), bf16),
        ],
        [where, gains],
        slots=(slot_arrays, 0, q_rows),
        scratch=[pltpu.VMEM((q_rows, slots), f32)],
        loads=[(w_self, 1), (w_self, 2), (w_self, 0), (w_self, 3)],
        flops=15e-6 * 1.1e15,
        name="self_forward",
    )
    c_all = lax.all_gather(c_own, "blk", axis=0, tiled=True)

    def swin_forward(*refs):
        swin_forward_kernel(rows_here, *refs)

    a_low, qkv_swin, lse_swin, o_swin, v1, e_low = call(
        swin_forward,
        [
            sds((tokens, D), bf16),
            sds((tokens, 3 * D), bf16),
            sds((tokens, 128), f32),
            sds((tokens, D), bf16),
            sds((tokens, D), f32),
            sds((tokens, D), bf16),
        ],
        [where, vis_in, gains],
        scratch=[pltpu.VMEM((cols_all // rows_here, rows_here**2, rows_here**2), f32)],
        loads=[(w_swin, k) for k in range(4)],
        flops=11e-6 * 1.1e15,
        name="swin_forward",
    )

    qa, kvb, doa, kva, qb, stats = call(
        cross_forward_kernel,
        [
            sds((slots, D), bf16),
            sds((slots, 2 * D), bf16),
            sds((slots, D), bf16),
            sds((tokens, 2 * D), bf16),
            sds((tokens, D), bf16),
            sds((3, 16, slots), f32),
        ],
        [where, c_all, e_low],
        slots=(slot_arrays, 1, q_rows),
        loads=[(w_qv, 1), (w_qv, 2), (w_vq, 0), (w_qv, 0), (w_vq, 1), (w_vq, 2), (w_qv, 3)],
        flops=18e-6 * 1.1e15,
        name="cross_forward",
    )
    lse_vq, o_vq = call(
        vq_forward_kernel,
        [sds((tokens, 128), f32), sds((tokens, D), bf16)],
        [where, qb, kvb],
        flops=11e-6 * 1.1e15,
        name="vq_forward",
    )

    all_stats = lax.all_gather(stats, "blk", axis=0)
    peaks = jnp.max(all_stats[:, 0], axis=0)
    weights = jnp.exp(all_stats[:, 0] - peaks[None])
    totals = jnp.sum(all_stats[:, 1] * weights, axis=0)
    lse_qv = peaks + jnp.log(totals)
    centre_qv = jnp.sum(all_stats[:, 2] * weights, axis=0) / totals

    v3, h_low, act_low, du_low, g2, dz_vq, dob, dg5 = call(
        mlp_kernel,
        [
            sds((tokens, D), bf16),
            sds((tokens, D), bf16),
            sds((tokens, FF), bf16),
            sds((tokens, FF), bf16),
            sds((tokens, D), f32),
            sds((tokens, D), bf16),
            sds((tokens, D), bf16),
            sds((1, D), f32),
        ],
        [where, v1, o_vq, vis_cot, gains],
        scratch=[pltpu.VMEM((tokens, D), f32)] * 3,
        loads=[(w_vq, 3), (w_up, None)] + [(w_down, k) for k in range(4)],
        flops=14e-6 * 1.1e15,
        name="mlp",
    )

    up_entries = [(h_low, 0, du_low, k, "tn") for k in range(4)]
    down_entries = [(act_low, k, vis_cot, 0, "tn") for k in range(4)]
    where_vq_back = where
    if staged:
        m_keep, m_send = weight_grad_call(
            where, [((0,), "up", up_entries), ((1,), "rows", down_entries)], "mlp_grads"
        )
        where_vq_back = after(where, m_keep)

    dqb, dkvbt = call(
        vq_backward_kernel,
        [sds((tokens, D), bf16), sds((2 * D, slots), bf16)],
        [where_vq_back, qb, kvb, dob, lse_vq],
        flops=16e-6 * 1.1e15,
        name="vq_backward",
    )
    dqat, dkva, *merged_parts = call(
        qv_backward_kernel,
        [sds((D, slots), bf16), sds((tokens, 2 * D), bf16)] + [sds((slots, 2 * D), bf16)],
        [where, qa, kva, doa, lse_qv, centre_qv, dkvbt],
        scratch=[pltpu.VMEM((slots, 2 * D), bf16)],
        loads=[(w_qv, 0), (w_vq, 1), (w_vq, 2)],
        flops=23e-6 * 1.1e15,
        name="qv_backward",
    )
    merged = collect_blocks(merged_parts)
    dc, oa_low = merged[:, :D], merged[:, D:]

    def swin_backward(*refs):
        swin_backward_kernel(rows_here, *refs)

    dz_swin, dqkv_swin, visual_grad, dg_visual = call(
        swin_backward,
        [
            sds((tokens, D), bf16),
            sds((tokens, 3 * D), bf16),
            sds((tokens, D), f32),
            sds((2, D), f32),
        ],
        [where, vis_in, v1, g2, gains, dkva, dqb, qkv_swin, lse_swin],
        scratch=[
            pltpu.VMEM((cols_all // rows_here, rows_here**2, rows_here**2), f32),
            pltpu.VMEM((tokens, D), bf16),
        ],
        loads=[(w_qv, 1), (w_qv, 2), (w_vq, 0), (w_swin, 3)] + [(w_swin, k) for k in range(3)],
        flops=20e-6 * 1.1e15,
        name="swin_backward",
    )

    swin_entries = [(a_low, 0, dqkv_swin, k, "tn") for k in range(3)]
    swin_entries.append((o_swin, 0, dz_swin, 0, "tn"))
    vq_entries = [
        (e_low, 0, dqb, 0, "tn"),
        (c_all, 0, dkvbt, 0, "tt"),
        (c_all, 0, dkvbt, 1, "tt"),
        (o_vq, 0, dz_vq, 0, "tn"),
    ]
    qv_entries = [
        (c_all, 0, dqat, 0, "tt"),
        (e_low, 0, dkva, 0, "tn"),
        (e_low, 0, dkva, 1, "tn"),
        (oa_low, 0, query_cot[0], 0, "tn"),
    ]
    if staged:
        p_keep, p_send = weight_grad_call(
            where, [((0,), "rows", vq_entries), ((1,), "rows", swin_entries)], "patch_grads"
        )

    gy1, dz_self, dq_self, dkvt_self, dbq, dg4, *db_parts = call(
        self_backward_kernel,
        [
            sds((q_rows, D), f32),
            sds((q_rows, D), bf16),
            sds((q_rows, D), bf16),
            sds((2 * D, slots), bf16),
            sds((q_rows, D), f32),
            sds((1, D), f32),
        ]
        + ([sds((4, q_rows, D), bf16)] * 2 if staged else [sds((slots, D), bf16)]),
        [where, dc, y1, query_cot[0], gains, q_self, kv_self, lse_self],
        scratch=[
            pltpu.VMEM((q_rows, slots), f32),
            pltpu.VMEM((q_rows, D), bf16),
            pltpu.VMEM((slots, D), bf16),
        ],
        loads=[(w_self, 3), (w_self, 0), (w_self, 1), (w_self, 2)],
        flops=15e-6 * 1.1e15,
        name="self_backward",
    )
    b_own = lax.dynamic_slice_in_dim(b_all, blk_here * q_rows, q_rows, 0)
    self_entries = [
        (b_own, 0, dq_self, 0, "tn"),
        (b_all, 0, dkvt_self, 0, "tt"),
        (b_all, 0, dkvt_self, 1, "tt"),
        (o_self, 0, dz_self, 0, "tn"),
    ]
    db = collect_blocks(db_parts)
    where_end = where
    if staged:
        z_keep, z_send = weight_grad_call(
            where, [((0,), "rows", qv_entries), ((1,), "rows", self_entries)], "slot_grads"
        )
        m_one = collect_first(m_keep, m_send, dqb)
        m_two = collect_second(m_one, dz_swin)
        m_three = collect_third(m_two, gy1)
        mlp_sum = collect_last(m_three, z_keep)
        p_one = collect_first(p_keep, p_send, gy1)
        p_two = collect_second(p_one, z_keep)
        p_three = collect_third(p_two)
        z_one = collect_first(z_keep, z_send)
        where_end = after(where, z_keep)
    query_grad, dg2, query_out = call(
        query_end_kernel,
        [sds((q_rows, D), f32), sds((1, D), f32), sds((q_rows, D), bf16)],
        [where_end, db, dbq, query_tokens[0], gy1, gains, y1, oa_low],
        loads=[(w_qv, 3)],
        name="query_end",
    )

    gain_block = jnp.concatenate(
        [dg_visual[0:1], dg2, dg_visual[1:2], dg4, dg5, jnp.zeros((3, D), f32)], axis=0
    )
    gain_sum = summed_everywhere(gain_block)
    gain_grad = lax.dynamic_slice_in_dim(
        gain_sum.reshape(-1), (page_here * blk_count + blk_here) * gain_width, gain_width, 0
    )

    def flat(value):
        return value.astype(f32).reshape(-1)

    if staged:
        patch_sum = collect_last(p_three)
        slot_sum = collect_last(collect_third(collect_second(z_one)))
        up_sum = mlp_sum[0].reshape(2, 2, share // 4, D)
        up_mine = jnp.where(core_here == 0, up_sum[:, 0], up_sum[:, 1])
        up_other = swapped(jnp.where(core_here == 0, up_sum[:, 1], up_sum[:, 0]), "blk", 1)
        up_grad = jnp.where(
            core_here == 0,
            jnp.concatenate([up_mine, up_other], axis=0),
            jnp.concatenate([up_other, up_mine], axis=0),
        )
        up_grad = flat(up_grad.transpose(1, 0, 2))
        swin_grad, self_grad = flat(patch_sum[1]), flat(slot_sum[1])
        qv_grad, vq_grad = flat(slot_sum[0]), flat(patch_sum[0])
        down_grad = flat(mlp_sum[1])
    else:

        def outer(left, right):
            return tn(left, right).astype(bf16)

        def outer_t(left, right_t):
            return lax.dot_general(
                left, right_t, (((0,), (1,)), ((), ())), preferred_element_type=f32
            ).astype(bf16)

        def as_shares(mats):
            return jnp.concatenate(mats, axis=0).reshape(shards, share, D)

        def summed(parts):
            joined = jnp.concatenate(parts, axis=1)
            width = joined.shape[1]
            return lax.psum_scatter(
                joined.reshape(shards * width, D), everyone, scatter_dimension=0, tiled=True
            )

        up_mats = jnp.stack([outer(h_low, du_low[:, k * D : (k + 1) * D]) for k in range(4)])
        up_part = (
            up_mats.reshape(4, shards, share // 4, D)
            .transpose(1, 0, 2, 3)
            .reshape(shards, share, D)
        )
        down_part = outer(act_low, vis_cot).reshape(shards, share, D)
        mlp_sum = summed([up_part, down_part])
        qv_part = as_shares(
            [
                outer_t(c_all, dqat),
                outer(e_low, dkva[:, :D]),
                outer(e_low, dkva[:, D:]),
                outer(oa_low, query_cot[0]),
            ]
        )
        vq_part = as_shares(
            [
                outer(e_low, dqb),
                outer_t(c_all, dkvbt[:D]),
                outer_t(c_all, dkvbt[D:]),
                outer(o_vq, dz_vq),
            ]
        )
        cross_sum = summed([qv_part, vq_part])
        swin_part = as_shares(
            [outer(a_low, dqkv_swin[:, k * D : (k + 1) * D]) for k in range(3)]
            + [outer(o_swin, dz_swin)]
        )
        self_part = as_shares(
            [
                outer(b_own, dq_self),
                outer_t(b_all, dkvt_self[:D]),
                outer_t(b_all, dkvt_self[D:]),
                outer(o_self, dz_self),
            ]
        )
        last_sum = summed([swin_part, self_part])
        up_grad = flat(mlp_sum[:share].reshape(4, share // 4, D).transpose(1, 0, 2))
        down_grad = flat(mlp_sum[share:])
        qv_grad, vq_grad = flat(cross_sum[:share]), flat(cross_sum[share:])
        swin_grad, self_grad = flat(last_sum[:share]), flat(last_sum[share:])

    def back_to_grid(value):
        grid = grid_order(value, rows_here, cols_all, half)
        returned = lax.ppermute(grid[half:], "blk", up_one)
        return jnp.concatenate([returned, grid[:half]], axis=0)[None]

    return (
        back_to_grid(v3),
        query_out[None],
        back_to_grid(visual_grad),
        query_grad[None],
        swin_grad,
        self_grad,
        qv_grad,
        vq_grad,
        up_grad,
        down_grad,
        gain_grad,
    )


def solution(mesh):
    placed = (
        P("page", "blk", None, None),
        P("page", "blk", None),
        P("page"),
        P(("page", "blk")),
        P(("page", "blk")),
        P(("page", "blk")),
        P(("page", "blk")),
        P(("page", "blk")),
        P(("page", "blk")),
        P(("page", "blk")),
        P("page", "blk", None, None),
        P("page", "blk", None),
    )
    return jax.shard_map(
        on_device,
        mesh=mesh,
        in_specs=placed,
        out_specs=(
            P("page", "blk", None, None),
            P("page", "blk", None),
            P("page", "blk", None, None),
            P("page", "blk", None),
            P(("page", "blk")),
            P(("page", "blk")),
            P(("page", "blk")),
            P(("page", "blk")),
            P(("page", "blk")),
            P(("page", "blk")),
            P(("page", "blk")),
        ),
        check_vma=False,
    )
```

time: 976 us -> 607 us (0.62)
  waiting for transfers between devices: 695 us -> 238 us
  starting transfers between devices: 4.18 us -> 70.6 us
  Pallas kernels: 153 us -> 194 us
  matrix products: 27.3 us -> 0 us
    reduce_scatter x5 -> x1, waiting for transfers between devices: 409 us -> 0.01 us  [collect_blocks(): return lax.psum_scatter(parts[0], 'blk', scatter_dimension=0, tiled=True)]
    all_gather x5 -> x1, waiting for transfers between devices: 239 us -> 0.02 us  [on_device(): slots_joined = lax.all_gather(slot_own, 'blk', axis=0)]
    ppermute x0 -> x71, waiting for transfers between devices: none -> 235 us  [swapped(): return lax.ppermute(value, axis, [(i, i ^ flip) for i in range(count)])]
    ppermute x0 -> x71, starting transfers between devices: none -> 68.3 us  [swapped(): return lax.ppermute(value, axis, [(i, i ^ flip) for i in range(count)])]
    pallas_call x10 -> x13, Pallas kernels: 153 us -> 194 us  [the longest x10 154 us: call(): pl.pallas_call(body, grid=(1,), out_shape=shapes, in_specs=specs + [pl.Bl...]
    dot_general x22 -> x0, matrix products: 27.3 us -> none  [the longest x16 17.6 us: tn(): lax.dot_general(left, right, (((0,), (0,)), ((), ())), preferred_element_...]
    concatenate x11 -> x3, other arithmetic: 29 us -> 1.97 us  [the longest x1 1.81 us: on_device(): jnp.concatenate([query_tokens[0], query_cot[0], gain_rows], axis=0)]
    all_gather x1, waiting for transfers between devices: 26.6 us -> 0.01 us  [on_device(): c_all = lax.all_gather(c_own, 'blk', axis=0, tiled=True)]
  transfers between devices with their start and end apart: 15 -> 78, of which waited for: 11 -> 33; matrix products, arithmetic and copies ran while one was open for 8% -> 12% of each run, Pallas kernels for 11% -> 32%
where the time goes in v2:
time: 607 us; the launch traced here: 600 us
  waiting for transfers between devices  238 us (39%)
  Pallas kernels  194 us (32%)
  starting transfers between devices  70.6 us (12%)
  other arithmetic  43.8 us (7%)
  local copies, waits for them, and re-layouts  36.7 us (6%)
  between operations  15.7 us (3%)
    ppermute x71, waiting for transfers between devices, swapped(): return lax.ppermute(value, axis, [(i, i ^ flip) for i in range(count)])  235 us
    pallas_call x10, Pallas kernels, call(): pl.pallas_call(body, grid=(1,), out_shape=shapes, in_specs=specs + [pl.Bl...  154 us
    ppermute x71, starting transfers between devices, swapped(): return lax.ppermute(value, axis, [(i, i ^ flip) for i in range(count)])  68.3 us
    pallas_call x3, Pallas kernels, weight_grad_call(): pl.pallas_call(body, grid=(1,), out_shape=shapes, in_specs=[pl.BlockSpec(...  40.4 us
    convert_element_type x16, other arithmetic, added(): return (left.astype(f32) + right.astype(f32)).astype(bf16)  24.4 us
  transfers between devices with their start and end apart: 78, of which 33 were waited for; matrix products, arithmetic and copies ran while one was open for 12% of the time, Pallas kernels for 32%

profile of v2, /device:TPU:0, one launch (start us, length us, event | category | flops | bytes accessed | tf_op | source)
XLA Modules:
  0.0 599.5 jit_solution(14361581300799366973)
XLA Ops:
  36.2 9.3 %collective-permute-done.1 = bf16[2,96,768]{2,1,0:T(8,128)(2,1)S(1)} collective-permute-done((bf16[2,96,768]{2,1,0:T(8,128)(2,1)S(1)}, bf16[2,96,768]{2,1,0:T(8,128)(2,1)S(1)}, u32[]{:S(2)}, u32[]{:S(2)}) %collective-permute-start.1) | collective-permute-done | bytes 294944 | tf_op jit(solution)/shard_map/ppermute | solution.py:885
  59.7 16.1 %collective-permute-done.16 = bf16[2,96,768]{2,1,0:T(8,128)(2,1)S(1)} collective-permute-done((bf16[2,96,768]{2,1,0:T(8,128)(2,1)}, bf16[2,96,768]{2,1,0:T(8,128)(2,1)S(1)}, u32[]{:S(2)}, u32[]{:S(2)}) %collective-permute-start.16) | collective-permute-done | bytes 294944 | tf_op jit(solution)/shard_map/ppermute | solution.py:885
  86.2 16.1 %collective-permute-done.9.refs_4_.refs_18_ = bf16[8,96,768]{2,1,0:T(8,128)(2,1)} collective-permute-done((bf16[8,96,768]{2,1,0:T(8,128)(2,1)}, bf16[8,96,768]{2,1,0:T(8,128)(2,1)}, u32[]{:S(2)}, u32[]{:S(2)}) %collective-permute-start.9) | collective-permute-done | bytes 1179680 | tf_op jit(solution)/shard_map/ppermute | solution.py:885
  128.1 16.1 %self_forward.1 = (bf16[1024,768]{1,0:T(8,128)(2,1)}, bf16[128,768]{1,0:T(8,128)(2,1)}, bf16[1024,1536]{1,0:T(8,128)(2,1)}, f32[128,128]{1,0:T(8,128)}, bf16[128...) custom-call(s32[5]{0:T(128)} %stack.98.refs_0_, ...), custom_call_target="tpu_custom_call" | custom-call | flops 16499999744 | bytes 10510356 | tf_op jit(solution)/shard_map/self_forward/pallas_call | solution.py:232
  171.2 9.2 %collective-permute-done.30 = bf16[4,96,768]{2,1,0:T(8,128)(2,1)S(1)} collective-permute-done((bf16[4,96,768]{2,1,0:T(8,128)(2,1)S(1)}, bf16[4,96,768]{2,1,0:T(8,128)(2,1)S(1)}, u32[]{:S(2)}, u32[]{:S(2)}) %collective-permute-start.30) | collective-permute-done | bytes 589856 | tf_op jit(solution)/shard_map/ppermute | solution.py:885
  186.2 11.5 %swin_forward.1 = (bf16[288,768]{1,0:T(8,128)(2,1)}, bf16[288,2304]{1,0:T(8,128)(2,1)}, f32[288,128]{1,0:T(8,128)}, bf16[288,768]{1,0:T(8,128)(2,1)}, f32[288,768]{1,0:T(8,128)}, /*index=5*/bf16[288,768]{1,0:T(8,128)(2,1)}) custom-call(s32[5]{0:T(128)} %stack.98.refs_0_, bf16[288,768]{1,0:T(8,128)(2,1)} %reshape.169.refs_1_, ...), custom_call_target="tpu_custom_call" | custom-call | flops 12099999744 | bytes 8871956 | tf_op jit(solution)/shard_map/swin_forward/pallas_call | solution.py:232
  198.3 11.8 %collective-permute-done.35.refs_14_ = bf16[8,96,768]{2,1,0:T(8,128)(2,1)} collective-permute-done((bf16[8,96,768]{2,1,0:T(8,128)(2,1)}, bf16[8,96,768]{2,1,0:T(8,128)(2,1)}, u32[]{:S(2)}, u32[]{:S(2)}) %collective-permute-start.35) | collective-permute-done | bytes 1179680 | tf_op jit(solution)/shard_map/ppermute | solution.py:885
  211.0 21.1 %cross_forward.1 = (bf16[1024,768]{1,0:T(8,128)(2,1)}, bf16[1024,1536]{1,0:T(8,128)(2,1)}, bf16[1024,768]{1,0:T(8,128)(2,1)}, bf16[288,1536]{1,0:T(8,128)(2,1)},...) custom-call(s32[5]{0:T(128)} %stack.98.refs_0_, bf16[1024,768]{1,0:T(8,128)(2,1)} %all-gather.6.cloned.1.call-done.refs_1_.refs_3_, ...), custom_call_target="tpu_custom_call" | custom-call | flops 19800000512 | bytes 18087956 | tf_op jit(solution)/shard_map/cross_forward/pallas_call | solution.py:232
  232.7 11.7 %vq_forward.1 = (f32[288,128]{1,0:T(8,128)}, bf16[288,768]{1,0:T(8,128)(2,1)}) custom-call(s32[5]{0:T(128)} %stack.98.refs_0_, bf16[288,768]{1,0:T(8,128)(2,1)} %get-tuple-element.101.refs_1_, bf16[1024,1536]{1,0:T(8,128)(2,1)} %get-tuple-element.102.refs_2_), custom_call_target="tpu_custom_call" | custom-call | flops 12099999744 | bytes 4177940 | tf_op jit(solution)/shard_map/vq_forward/pallas_call | solution.py:232
  246.3 14.8 %mlp.1 = (bf16[288,768]{1,0:T(8,128)(2,1)}, bf16[288,768]{1,0:T(8,128)(2,1)}, bf16[288,3072]{1,0:T(8,128)(2,1)}, bf16[288,3072]{1,0:T(8,128)(2,1)}, f32[288,768]...) custom-call(s32[5]{0:T(128)} %stack.98.refs_0_, ...), custom_call_target="tpu_custom_call" | custom-call | flops 15399999488 | bytes 18607124 | tf_op jit(solution)/shard_map/mlp/pallas_call | solution.py:232
  261.0 11.5 %mlp_grads.1 = (bf16[2,16,96,768]{3,2,1,0:T(8,128)(2,1)}, bf16[2,16,96,768]{3,2,1,0:T(8,128)(2,1)}) custom-call(s32[5]{0:T(128)} %stack.98.refs_0_, bf16[288,768]{1,0:T(8,128)(2,1)} %get-tuple-element.114.refs_1_, bf16[288,3072]{1,0:T(8,128)(2,1)} %get-tuple-element.115.refs_2_, bf16[288,3072]{1,0:T(8,128)(2,1)} %get-tuple-element.116.refs_3_, ...), custom_call_target="tpu_custom_call" | custom-call | flops 14080000000 | bytes 13860864 | tf_op jit(solution)/shard_map/mlp_grads/pallas_call | solution.py:847
  273.1 16.1 %vq_backward.1 = (bf16[288,768]{1,0:T(8,128)(2,1)}, bf16[1536,1024]{1,0:T(8,128)(2,1)}) custom-call(s32[5]{0:T(128)} %stack.98.refs_0_, bf16[288,768]{1,0:T(8,128)(2,1)} %get-tuple-element.101.refs_1_, bf16[1024,1536]{1,0:T(8,128)(2,1)} %get-tuple-element.102.refs_2_, bf16[288,768]{1,0:T(8,128)(2,1)} %get-tuple-element.119.refs_3_, ...), custom_call_target="tpu_custom_call" | custom-call | flops 17600000000 | bytes 7766036 | tf_op jit(solution)/shard_map/vq_backward/pallas_call | solution.py:232
  292.5 22.6 %qv_backward.1 = (bf16[768,1024]{1,0:T(8,128)(2,1)}, bf16[288,1536]{1,0:T(8,128)(2,1)}, bf16[1024,1536]{1,0:T(8,128)(2,1)}) custom-call(s32[5]{0:T(128)} %stack.98.refs_0_, bf16[1024,768]{1,0:T(8,128)(2,1)} %get-tuple-element.110.refs_1_, bf16[288,1536]{1,0:T(8,128)(2,1)} %get-tuple-element.111.refs_2_, bf16[1024,768]{1,0:T(8,128)(2,1)} %get-tuple-element.112.refs_3_, ...), custom_call_target="tpu_custom_call" | custom-call | flops 25300000768 | bytes 16449556 | tf_op jit(solution)/shard_map/qv_backward/pallas_call | solution.py:232
  317.9 19.5 %swin_backward.1 = (bf16[288,768]{1,0:T(8,128)(2,1)}, bf16[288,2304]{1,0:T(8,128)(2,1)}, f32[288,768]{1,0:T(8,128)}, f32[2,768]{1,0:T(2,128)}) custom-call(s32[5]{0:T(128)} %stack.98.refs_0_, bf16[288,768]{1,0:T(8,128)(2,1)} %reshape.169.refs_1_, f32[288,768]{1,0:T(8,128)} %get-tuple-element.94.refs_1_.refs_2_, f32[288,768]{1,0:T(8,128)} %get-tuple-element.141.refs_3_, ...), custom_call_target="tpu_custom_call" | custom-call | flops 22000001024 | bytes 15955988 | tf_op jit(solution)/shard_map/swin_backward/pallas_call | solution.py:232
  344.6 14.1 %patch_grads.1 = (bf16[2,16,96,768]{3,2,1,0:T(8,128)(2,1)}, bf16[2,16,96,768]{3,2,1,0:T(8,128)(2,1)}) custom-call(s32[5]{0:T(128)} %stack.98.refs_0_, bf16[288,768]{1,0:T(8,128)(2,1)} %get-tuple-element.96.refs_2_.refs_3_.refs_1_, bf16[288,768]{1,0:T(8,128)(2,1)} %get-tuple-element.142.refs_6_.refs_2_, ...), custom_call_target="tpu_custom_call" | custom-call | flops 14080000000 | bytes 18579456 | tf_op jit(solution)/shard_map/patch_grads/pallas_call | solution.py:847
  365.0 12.5 %collective-permute-done.61 = bf16[8,96,768]{2,1,0:T(8,128)(2,1)} collective-permute-done((bf16[8,96,768]{2,1,0:T(8,128)(2,1)}, bf16[8,96,768]{2,1,0:T(8,128)(2,1)}, u32[]{:S(2)}, u32[]{:S(2)}) %collective-permute-start.61) | collective-permute-done | bytes 1179680 | tf_op jit(solution)/shard_map/ppermute | solution.py:885
  383.4 16.6 %self_backward.1 = (f32[128,768]{1,0:T(8,128)}, bf16[128,768]{1,0:T(8,128)(2,1)}, bf16[128,768]{1,0:T(8,128)(2,1)}, bf16[1536,1024]{1,0:T(8,128)(2,1)}, f32[128,...) custom-call(s32[5]{0:T(128)} %stack.98.refs_0_, ...), custom_call_target="tpu_custom_call" | custom-call | flops 16499999744 | bytes 14838804 | tf_op jit(solution)/shard_map/self_backward/pallas_call | solution.py:232
  400.1 14.8 %slot_grads.1 = (bf16[2,16,96,768]{3,2,1,0:T(8,128)(2,1)}, bf16[2,16,96,768]{3,2,1,0:T(8,128)(2,1)}) custom-call(s32[5]{0:T(128)} %stack.98.refs_0_, bf16[1024,768]{1,0:T(8,128)(2,1)} %all-gather.6.cloned.1.call-done.refs_1_.refs_3_, bf16[768,1024]{1,0:T(8,128)(2,1)} %get-tuple-element.122.refs_2_, ...), custom_call_target="tpu_custom_call" | custom-call | flops 14080000000 | bytes 19808256 | tf_op jit(solution)/shard_map/slot_grads/pallas_call | solution.py:847
  419.4 12.9 %collective-permute-done.64 = bf16[4,96,768]{2,1,0:T(8,128)(2,1)S(1)} collective-permute-done((bf16[4,96,768]{2,1,0:T(8,128)(2,1)S(1)}, bf16[4,96,768]{2,1,0:T(8,128)(2,1)S(1)}, u32[]{:S(2)}, u32[]{:S(2)}) %collective-permute-start.64) | collective-permute-done | bytes 589856 | tf_op jit(solution)/shard_map/ppermute | solution.py:885
  469.0 17.9 %collective-permute-done.70 = f32[8,768]{1,0:T(8,128)S(1)} collective-permute-done((f32[8,768]{1,0:T(8,128)S(1)}, f32[8,768]{1,0:T(8,128)S(1)}, u32[]{:S(2)}, u32[]{:S(2)}) %collective-permute-start.70) | collective-permute-done | bytes 24608 | tf_op jit(solution)/shard_map/ppermute | solution.py:885
  488.0 11.9 %collective-permute-done.71 = f32[8,768]{1,0:T(8,128)S(1)} collective-permute-done((f32[8,768]{1,0:T(8,128)S(1)}, f32[8,768]{1,0:T(8,128)S(1)}, u32[]{:S(2)}, u32[]{:S(2)}) %collective-permute-start.71) | collective-permute-done | bytes 24608 | tf_op jit(solution)/shard_map/ppermute | solution.py:885
  537.4 15.7 %collective-permute-done.53 = bf16[8,96,768]{2,1,0:T(8,128)(2,1)S(1)} collective-permute-done((bf16[8,96,768]{2,1,0:T(8,128)(2,1)S(1)}, bf16[8,96,768]{2,1,0:T(8,128)(2,1)S(1)}, u32[]{:S(2)}, u32[]{:S(2)}) %collective-permute-start.53) | collective-permute-done | bytes 1179680 | tf_op jit(solution)/shard_map/ppermute | solution.py:885
  555.9 9.9 %collective-permute-done.55 = bf16[4,96,768]{2,1,0:T(8,128)(2,1)S(1)} collective-permute-done((bf16[4,96,768]{2,1,0:T(8,128)(2,1)S(1)}, bf16[4,96,768]{2,1,0:T(8,128)(2,1)S(1)}, u32[]{:S(2)}, u32[]{:S(2)}) %collective-permute-start.55) | collective-permute-done | bytes 589856 | tf_op jit(solution)/shard_map/ppermute | solution.py:885
  577.4 13.8 %collective-permute-done.58 = bf16[2,96,768]{2,1,0:T(8,128)(2,1)S(1)} collective-permute-done((bf16[2,96,768]{2,1,0:T(8,128)(2,1)S(1)}, bf16[2,96,768]{2,1,0:T(8,128)(2,1)S(1)}, u32[]{:S(2)}, u32[]{:S(2)}) %collective-permute-start.58) | collective-permute-done | bytes 294944 | tf_op jit(solution)/shard_map/ppermute | solution.py:885
  (350 shorter events, 236.4 us)
Async XLA Ops:
  7.2 116.5 %all-gather.8.cloned.1.call-start = ((), (), s32[]{:S(2)}) async-start(), calls=%async_computation.3 | async-start | bytes 3760128 | tf_op jit(solution)/shard_map/all_gather | solution.py:1014
  20.9 190.1 %all-gather.6.cloned.1.call-start = ((), (), s32[]{:S(2)}) async-start(), calls=%async_computation.1 | async-start | bytes 1769472 | tf_op jit(solution)/shard_map/all_gather | solution.py:1099
  85.6 40.6 %collective-permute-start.13 = (bf16[8,96,768]{2,1,0:T(8,128)(2,1)}, bf16[8,96,768]{2,1,0:T(8,128)(2,1)}, u32[]{:S(2)}, u32[]{:S(2)}) collective-permute-start(bf16[8,96,768]{2,1,0:T(8,128)(2,1)} %constant_dynamic-update-slice_fusion.2.refs_2_.refs_8_), channel_id=1, source_target_pairs={{0,1},{1,0},{2,3},{3,2},{4,5},{5,4},{6,7},{7,6},{8,9},{9,8},{10,11... | collective-permute-start | bytes 3538952 | tf_op jit(solution)/shard_map/ppermute | solution.py:885
  85.7 95.6 %collective-permute-start.10 = (bf16[8,96,768]{2,1,0:T(8,128)(2,1)}, bf16[8,96,768]{2,1,0:T(8,128)(2,1)}, u32[]{:S(2)}, u32[]{:S(2)}) collective-permute-start(bf16[8,96,768]{2,1,0:T(8,128)(2,1)} %constant_dynamic-update-slice_fusion.7.refs_3_.refs_17_), channel_id=1, source_target_pairs={{0,1},{1,0},{2,3},{3,2},{4,5},{5,4},{6,7},{7,6},{8,9},{9,8},{10,11... | collective-permute-start | bytes 3538952 | tf_op jit(solution)/shard_map/ppermute | solution.py:885
  144.3 144.9 %all-gather.10.cloned.1.call-start = ((), (), s32[]{:S(2)}) async-start(), calls=%async_computation.4 | async-start | bytes 1769472 | tf_op jit(solution)/shard_map/all_gather | solution.py:1145
  145.0 36.8 %collective-permute-start.11 = (bf16[8,96,768]{2,1,0:T(8,128)(2,1)}, bf16[8,96,768]{2,1,0:T(8,128)(2,1)S(1)}, u32[]{:S(2)}, u32[]{:S(2)}) collective-permute-start(bf16[8,96,768]{2,1,0:T(8,128)(2,1)} %collective-permute-done.9.refs_4_.refs_18_), channel_id=1, source_target_pairs={{0,1},{1,0},{2,3},{3,2},{4,5},{5,4},{6,7},{7,6},{8,9},{9,8},{10,11... | collective-permute-start | bytes 3538952 | tf_op jit(solution)/shard_map/ppermute | solution.py:885
  154.1 28.9 %collective-permute-start.24 = (bf16[8,96,768]{2,1,0:T(8,128)(2,1)}, bf16[8,96,768]{2,1,0:T(8,128)(2,1)S(1)}, u32[]{:S(2)}, u32[]{:S(2)}) collective-permute-start(bf16[8,96,768]{2,1,0:T(8,128)(2,1)} %constant_dynamic-update-slice_fusion.14.refs_7_.refs_5_.refs_11_.refs_13_), channel_id=1, source_target_pairs={{0,1},{1,0},{2,3},{3,2},{4,5},{5,4},{6,7},{7,6},{8,9},{9,8},{10,11... | collective-permute-start | bytes 3538952 | tf_op jit(solution)/shard_map/ppermute | solution.py:885
  181.3 29.7 %collective-permute-start.21 = (bf16[8,96,768]{2,1,0:T(8,128)(2,1)}, bf16[8,96,768]{2,1,0:T(8,128)(2,1)}, u32[]{:S(2)}, u32[]{:S(2)}) collective-permute-start(bf16[8,96,768]{2,1,0:T(8,128)(2,1)} %collective-permute-done.19.refs_4_.refs_8_.refs_9_.refs_10_), channel_id=1, source_target_pairs={{0,1},{1,0},{2,3},{3,2},{4,5},{5,4},{6,7},{7,6},{8,9},{9,8},{10,11... | collective-permute-start | bytes 3538952 | tf_op jit(solution)/shard_map/ppermute | solution.py:885
  181.8 28.3 %collective-permute-start.35 = (bf16[8,96,768]{2,1,0:T(8,128)(2,1)}, bf16[8,96,768]{2,1,0:T(8,128)(2,1)}, u32[]{:S(2)}, u32[]{:S(2)}) collective-permute-start(bf16[8,96,768]{2,1,0:T(8,128)(2,1)} %constant_dynamic-update-slice_fusion.18.refs_13_), channel_id=1, source_target_pairs={{0,2},{1,3},{2,0},{3,1},{4,6},{5,7},{6,4},{7,5},{8,10},{9,11},{10,... | collective-permute-start | bytes 3538952 | tf_op jit(solution)/shard_map/ppermute | solution.py:885
  197.7 46.7 %collective-permute-start.36 = (bf16[8,96,768]{2,1,0:T(8,128)(2,1)}, bf16[8,96,768]{2,1,0:T(8,128)(2,1)S(1)}, u32[]{:S(2)}, u32[]{:S(2)}) collective-permute-start(bf16[8,96,768]{2,1,0:T(8,128)(2,1)} %constant_dynamic-update-slice_fusion.18.refs_13_), channel_id=1, source_target_pairs={{0,1},{1,0},{2,3},{3,2},{4,5},{5,4},{6,7},{7,6},{8,9},{9,8},{10,11... | collective-permute-start | bytes 3538952 | tf_op jit(solution)/shard_map/ppermute | solution.py:885
  197.8 46.6 %collective-permute-start.32 = (bf16[8,96,768]{2,1,0:T(8,128)(2,1)}, bf16[8,96,768]{2,1,0:T(8,128)(2,1)S(1)}, u32[]{:S(2)}, u32[]{:S(2)}) collective-permute-start(bf16[8,96,768]{2,1,0:T(8,128)(2,1)} %constant_dynamic-update-slice_fusion.16.refs_9_), channel_id=1, source_target_pairs={{0,1},{1,0},{2,3},{3,2},{4,5},{5,4},{6,7},{7,6},{8,9},{9,8},{10,11... | collective-permute-start | bytes 3538952 | tf_op jit(solution)/shard_map/ppermute | solution.py:885
  210.1 34.4 %collective-permute-start.37 = (bf16[8,96,768]{2,1,0:T(8,128)(2,1)}, bf16[8,96,768]{2,1,0:T(8,128)(2,1)S(1)}, u32[]{:S(2)}, u32[]{:S(2)}) collective-permute-start(bf16[8,96,768]{2,1,0:T(8,128)(2,1)} %collective-permute-done.35.refs_14_), channel_id=1, source_target_pairs={{0,1},{1,0},{2,3},{3,2},{4,5},{5,4},{6,7},{7,6},{8,9},{9,8},{10,11... | collective-permute-start | bytes 3538952 | tf_op jit(solution)/shard_map/ppermute | solution.py:885
  211.0 33.5 %collective-permute-start.33 = (bf16[8,96,768]{2,1,0:T(8,128)(2,1)}, bf16[8,96,768]{2,1,0:T(8,128)(2,1)}, u32[]{:S(2)}, u32[]{:S(2)}) collective-permute-start(bf16[8,96,768]{2,1,0:T(8,128)(2,1)} %collective-permute-done.31.refs_10_), channel_id=1, source_target_pairs={{0,1},{1,0},{2,3},{3,2},{4,5},{5,4},{6,7},{7,6},{8,9},{9,8},{10,11... | collective-permute-start | bytes 3538952 | tf_op jit(solution)/shard_map/ppermute | solution.py:885
  232.1 149.5 %reduce-scatter.2.cloned.1.call-start = ((), (), s32[]{:S(2)}) async-start(), calls=%async_computation.2 | async-start | bytes 3538944 | tf_op jit(solution)/shard_map/reduce_scatter | solution.py:949
  272.6 64.8 %collective-permute-start.60 = (bf16[2,16,96,768]{3,2,1,0:T(8,128)(2,1)}, bf16[2,16,96,768]{3,2,1,0:T(8,128)(2,1)}, u32[]{:S(2)}, u32[]{:S(2)}) collective-permute-start(bf16[2,16,96,768]{3,2,1,0:T(8,128)(2,1)} %get-tuple-element.165), channel_id=1, source_target_pairs={{0,1},{1,0},{2,3},{3,2},{4,5},{5,4},{6,7},{7,6},{8,9},{9,8},{10,11... | collective-permute-start | bytes 14155784 | tf_op jit(solution)/shard_map/ppermute | solution.py:885
  343.4 34.1 %collective-permute-start.61 = (bf16[8,96,768]{2,1,0:T(8,128)(2,1)}, bf16[8,96,768]{2,1,0:T(8,128)(2,1)}, u32[]{:S(2)}, u32[]{:S(2)}) collective-permute-start(bf16[8,96,768]{2,1,0:T(8,128)(2,1)} %get-tuple-element.177), channel_id=1, source_target_pairs={{0,2},{1,3},{2,0},{3,1},{4,6},{5,7},{6,4},{7,5},{8,10},{9,11},{10,... | collective-permute-start | bytes 3538952 | tf_op jit(solution)/shard_map/ppermute | solution.py:885
  358.7 76.1 %collective-permute-start.44 = (bf16[2,16,96,768]{3,2,1,0:T(8,128)(2,1)}, bf16[2,16,96,768]{3,2,1,0:T(8,128)(2,1)}, u32[]{:S(2)}, u32[]{:S(2)}) collective-permute-start(bf16[2,16,96,768]{3,2,1,0:T(8,128)(2,1)} %get-tuple-element.154), channel_id=1, source_target_pairs={{0,1},{1,0},{2,3},{3,2},{4,5},{5,4},{6,7},{7,6},{8,9},{9,8},{10,11... | collective-permute-start | bytes 14155784 | tf_op jit(solution)/shard_map/ppermute | solution.py:885
  363.7 51.3 %collective-permute-start.62 = (bf16[8,96,768]{2,1,0:T(8,128)(2,1)}, bf16[8,96,768]{2,1,0:T(8,128)(2,1)}, u32[]{:S(2)}, u32[]{:S(2)}) collective-permute-start(bf16[8,96,768]{2,1,0:T(8,128)(2,1)} %get-tuple-element.178), channel_id=1, source_target_pairs={{0,4},{1,5},{2,6},{3,7},{4,0},{5,1},{6,2},{7,3},{8,12},{9,13},{10,... | collective-permute-start | bytes 3538952 | tf_op jit(solution)/shard_map/ppermute | solution.py:885
  380.2 38.0 %collective-permute-start.63 = (bf16[4,96,768]{2,1,0:T(8,128)(2,1)}, bf16[4,96,768]{2,1,0:T(8,128)(2,1)}, u32[]{:S(2)}, u32[]{:S(2)}) collective-permute-start(bf16[4,96,768]{2,1,0:T(8,128)(2,1)} %get-tuple-element.189), channel_id=1, source_target_pairs={{0,4},{1,5},{2,6},{3,7},{4,0},{5,1},{6,2},{7,3},{8,12},{9,13},{10,... | collective-permute-start | bytes 1769480 | tf_op jit(solution)/shard_map/ppermute | solution.py:885
  414.9 99.8 %collective-permute-start.52 = (bf16[2,16,96,768]{3,2,1,0:T(8,128)(2,1)}, bf16[2,16,96,768]{3,2,1,0:T(8,128)(2,1)}, u32[]{:S(2)}, u32[]{:S(2)}) collective-permute-start(bf16[2,16,96,768]{3,2,1,0:T(8,128)(2,1)} %get-tuple-element.159), channel_id=1, source_target_pairs={{0,1},{1,0},{2,3},{3,2},{4,5},{5,4},{6,7},{7,6},{8,9},{9,8},{10,11... | collective-permute-start | bytes 14155784 | tf_op jit(solution)/shard_map/ppermute | solution.py:885
  452.2 35.5 %collective-permute-start.38 = (bf16[6,24,768]{2,1,0:T(8,128)(2,1)}, bf16[6,24,768]{2,1,0:T(8,128)(2,1)}, u32[]{:S(2)}, u32[]{:S(2)}) collective-permute-start(bf16[6,24,768]{2,1,0:T(8,128)(2,1)} %fusion.31), channel_id=1, source_target_pairs={{0,1},{1,2},{2,3},{3,4},{4,5},{5,6},{6,7},{7,0},{8,9},{9,10},{10,1... | collective-permute-start | bytes 663560 | tf_op jit(solution)/shard_map/ppermute | solution.py:1381
  457.8 53.1 %collective-permute-start.45 = (bf16[8,96,768]{2,1,0:T(8,128)(2,1)}, bf16[8,96,768]{2,1,0:T(8,128)(2,1)}, u32[]{:S(2)}, u32[]{:S(2)}) collective-permute-start(bf16[8,96,768]{2,1,0:T(8,128)(2,1)} %get-tuple-element.185), channel_id=1, source_target_pairs={{0,2},{1,3},{2,0},{3,1},{4,6},{5,7},{6,4},{7,5},{8,10},{9,11},{10,... | collective-permute-start | bytes 3538952 | tf_op jit(solution)/shard_map/ppermute | solution.py:885
  466.6 46.5 %collective-permute-start.46 = (bf16[8,96,768]{2,1,0:T(8,128)(2,1)}, bf16[8,96,768]{2,1,0:T(8,128)(2,1)}, u32[]{:S(2)}, u32[]{:S(2)}) collective-permute-start(bf16[8,96,768]{2,1,0:T(8,128)(2,1)} %get-tuple-element.186), channel_id=1, source_target_pairs={{0,4},{1,5},{2,6},{3,7},{4,0},{5,1},{6,2},{7,3},{8,12},{9,13},{10,... | collective-permute-start | bytes 3538952 | tf_op jit(solution)/shard_map/ppermute | solution.py:885
  519.1 34.0 %collective-permute-start.53 = (bf16[8,96,768]{2,1,0:T(8,128)(2,1)S(1)}, bf16[8,96,768]{2,1,0:T(8,128)(2,1)S(1)}, u32[]{:S(2)}, u32[]{:S(2)}) collective-permute-start(bf16[8,96,768]{2,1,0:T(8,128)(2,1)S(1)} %get-tuple-element.181), channel_id=1, source_target_pairs={{0,2},{1,3},{2,0},{3,1},{4,6},{5,7},{6,4},{7,5},{8,10},{9,11},{10,... | collective-permute-start | bytes 3538952 | tf_op jit(solution)/shard_map/ppermute | solution.py:885
  (79 other events, 1173.9 us)
Sparse Core Ops, SparseCore 0:
  21.0 31.3 all-gather.7
  144.4 35.8 all-gather.5
  232.3 26.2 all-gather.9
  315.2 55.6 reduce-scatter.1

commit v3 on v2

--- a/solution.py
+++ b/solution.py
@@ -681,6 +681,7 @@
     q_ref,
     kv_ref,
     lse_ref,
+    y_ref,
     w,
     gy1_ref,
     dz_ref,
@@ -691,10 +692,10 @@
     *rest,
 ):
     db_refs, (bias_ref, do_ref, db_held) = rest[:-3], rest[-3:]
+    group = 256 // q_ref.shape[0]
     first_row, live = where_ref[0], where_ref[1]
     own_rows, slots = q_ref.shape[0], kv_ref.shape[0]
     part, dg = norm_back(y1_ref[...], g_ref[3:4, :], dc_ref[...].astype(f32))
-    dg_ref[...] = dg
     gy1 = cot_ref[...].astype(f32) + part
     gy1_ref[...] = gy1
     dz = gy1.astype(bf16)
@@ -728,24 +729,31 @@
         return carry
 
     lax.fori_loop(0, PAIRS, back, 0)
-    dbq_ref[...] = nt(dq_ref[...], w[1])
+    dbq = nt(dq_ref[...], w[1])
+    dbq_ref[...] = dbq
+    unit = norm_parts(y_ref[where_ref[4]].astype(f32))[0]
+    dg2 = jnp.sum(dbq * unit, axis=0, keepdims=True)
     tile = 256
     for i in range(slots // tile):
         cols = slice(i * tile, (i + 1) * tile)
         total = nn(w[2], dkvt_ref[0:D, cols])
         total += nn(w[3], dkvt_ref[D : 2 * D, cols])
-        db_held[cols, :] = total.T.astype(bf16)
+        back = total.T
+        db_held[cols, :] = back.astype(bf16)
+        part = y_ref[i * group : (i + 1) * group].reshape(tile, D)
+        unit = norm_parts(part.astype(f32))[0]
+        dg2 += jnp.sum(back * unit, axis=0, keepdims=True)
+    dg_ref[...] = jnp.concatenate([dg2, dg], axis=0)
     hand_out(where_ref, db_held, db_refs)
 
 
 def query_end_kernel(
-    where_ref, db_ref, dbq_ref, y_ref, gy1_ref, g_ref, y1_ref, oa_ref, w, grad_ref, dg_ref, out_ref
+    where_ref, db_ref, dbq_ref, y_ref, gy1_ref, g_ref, y1_ref, oa_ref, w, grad_ref, out_ref
 ):
-    part, dg = norm_back(
+    part, _ = norm_back(
         y_ref[...].astype(f32), g_ref[1:2, :], db_ref[...].astype(f32) + dbq_ref[...]
     )
     grad_ref[...] = gy1_ref[...] + part
-    dg_ref[...] = dg
     out_ref[...] = (y1_ref[...] + nn(oa_ref[...], w[0])).astype(bf16)
 
 
@@ -895,11 +903,10 @@
     return [jnp.stack([part[k] for part in parts]) for k in range(2)]
 
 
-def spread_second(held):
-    return [
-        jnp.concatenate([held[0], swapped(held[0], "blk", 2)]),
-        jnp.concatenate([held[1], swapped(held[1], "blk", 4)]),
-    ]
+def spread_second(held, *gate):
+    got = swapped(held[0], "blk", 2), swapped(held[1], "blk", 4)
+    held = after(held, *gate)
+    return [jnp.concatenate([held[k], got[k]]) for k in range(2)]
 
 
 def spread_third(near):
@@ -944,25 +951,22 @@
     return total
 
 
-def collect_blocks(parts):
-    if len(parts) == 1:
-        return lax.psum_scatter(parts[0], "blk", scatter_dimension=0, tiled=True)
+def blocks_in_chip(parts, gate):
     keep, send = parts
     got = swapped(send, "blk", 1)
-    chips = [added(keep[k], got[k]) for k in range(4)]
-    total = chips[0].astype(f32)
+    keep = after(keep, gate)
+    return [added(keep[k], got[k]) for k in range(4)]
+
+
+def blocks_over_chips(chips, gate):
+    total = after(chips[0], gate).astype(f32)
     for k in range(1, 4):
         total = total + swapped(chips[k], "blk", 2 * k).astype(f32)
-    return total.astype(bf16)
-
-
-def summed_everywhere(value):
-    for axis in ("blk", "page"):
-        flip = 1
-        while flip < lax.axis_size(axis):
-            value = value + swapped(value, axis, flip)
-            flip *= 2
-    return value
+    return total
+
+
+def scattered_blocks(part):
+    return lax.psum_scatter(part, "blk", scatter_dimension=0, tiled=True)
 
 
 def on_device(
@@ -1008,15 +1012,13 @@
     def flat_share(value):
         return value.astype(bf16).reshape(share, D)
 
-    gain_pages = jnp.concatenate(from_pages(norm_gains.astype(bf16)))[None]
-    gain_rows = jnp.pad(gain_pages, ((0, 15), (0, D - pages * gain_width)))
+    gain_rows = jnp.pad(norm_gains.astype(bf16)[None], ((0, 15), (0, D - gain_width)))
     slot_own = jnp.concatenate([query_tokens[0], query_cot[0], gain_rows], axis=0)
     slots_joined = lax.all_gather(slot_own, "blk", axis=0)
     slot_arrays = [slots_joined]
-    gain_parts = slots_joined[:, 2 * q_rows, : pages * gain_width]
-    gain_parts = gain_parts.reshape(blk_count, pages, gain_width)
-    gains = jnp.take(gain_parts, jnp.arange(pages) ^ page_here, axis=1)
-    gains = gains.transpose(1, 0, 2).reshape(8, D).astype(f32)
+    gain_parts = jnp.stack(from_pages(slots_joined[:, 2 * q_rows, :gain_width].reshape(-1)))
+    gains = jnp.take(gain_parts, jnp.arange(pages) ^ page_here, axis=0)
+    gains = gains.reshape(8, D).astype(f32)
     if staged:
         a_z = spread_first([flat_share(attn_self), flat_share(attn_swin)])
         a_near = spread_second(a_z)
@@ -1036,18 +1038,8 @@
             jnp.concatenate([other, mine], axis=1),
         ).reshape(share, D)
         d_z = spread_first(after([up_share, flat_share(mlp_down)], c_z))
-        c_near = spread_second(after(c_z, a_far))
+        c_near = spread_second(after(c_z, a_far, gains))
         c_far = spread_third(c_near)
-        c_near_core, c_far_core = spread_core(c_near), spread_core(c_far)
-        w_qv, w_vq = [
-            Stored(lane_arrays(c_near, c_far, c_near_core, c_far_core, k), (k,)) for k in range(2)
-        ]
-        d_near = spread_second(after(d_z, c_far))
-        d_far = spread_third(d_near)
-        d_near_core, d_far_core = spread_core(d_near), spread_core(d_far)
-        w_up, w_down = [
-            Stored(lane_arrays(d_near, d_far, d_near_core, d_far_core, k), (k,)) for k in range(2)
-        ]
     else:
         up_share = (
             mlp_up.astype(bf16).reshape(share // 4, 4, D).transpose(1, 0, 2).reshape(share, D)
@@ -1078,6 +1070,9 @@
     vis_in = window_order(both[0], half)
     vis_cot = window_order(both[1], half)
 
+    where_self = where_swin = where_cross = where_vq = where
+    if staged:
+        where_self = after(where, vis_in, vis_cot)
     b_all, q_self, kv_self, lse_self, o_self, y1, c_own = call(
         self_forward_kernel,
         [
@@ -1089,13 +1084,21 @@
             sds((q_rows, D), f32),
             sds((q_rows, D), bf16),
         ],
-        [where, gains],
+        [where_self, gains],
         slots=(slot_arrays, 0, q_rows),
         scratch=[pltpu.VMEM((q_rows, slots), f32)],
         loads=[(w_self, 1), (w_self, 2), (w_self, 0), (w_self, 3)],
         flops=15e-6 * 1.1e15,
         name="self_forward",
     )
+    if staged:
+        c_far = after(c_far, c_own)
+        c_near_core, c_far_core = spread_core(c_near), spread_core(c_far)
+        w_qv, w_vq = [
+            Stored(lane_arrays(c_near, c_far, c_near_core, c_far_core, k), (k,)) for k in range(2)
+        ]
+        where_swin = after(where, c_far)
+        d_z = after(d_z, c_far)
     c_all = lax.all_gather(c_own, "blk", axis=0, tiled=True)
 
     def swin_forward(*refs):
@@ -1111,13 +1114,17 @@
             sds((tokens, D), f32),
             sds((tokens, D), bf16),
         ],
-        [where, vis_in, gains],
+        [where_swin, vis_in, gains],
         scratch=[pltpu.VMEM((cols_all // rows_here, rows_here**2, rows_here**2), f32)],
         loads=[(w_swin, k) for k in range(4)],
         flops=11e-6 * 1.1e15,
         name="swin_forward",
     )
 
+    if staged:
+        d_near = spread_second(d_z, e_low)
+        d_far = spread_third(d_near)
+        where_cross = after(where, d_near)
     qa, kvb, doa, kva, qb, stats = call(
         cross_forward_kernel,
         [
@@ -1128,16 +1135,23 @@
             sds((tokens, D), bf16),
             sds((3, 16, slots), f32),
         ],
-        [where, c_all, e_low],
+        [where_cross, c_all, e_low],
         slots=(slot_arrays, 1, q_rows),
         loads=[(w_qv, 1), (w_qv, 2), (w_vq, 0), (w_qv, 0), (w_vq, 1), (w_vq, 2), (w_qv, 3)],
         flops=18e-6 * 1.1e15,
         name="cross_forward",
     )
+    if staged:
+        d_far = after(d_far, qb)
+        d_near_core, d_far_core = spread_core(d_near), spread_core(d_far)
+        w_up, w_down = [
+            Stored(lane_arrays(d_near, d_far, d_near_core, d_far_core, k), (k,)) for k in range(2)
+        ]
+        where_vq = after(where, d_far)
     lse_vq, o_vq = call(
         vq_forward_kernel,
         [sds((tokens, 128), f32), sds((tokens, D), bf16)],
-        [where, qb, kvb],
+        [where_vq, qb, kvb],
         flops=11e-6 * 1.1e15,
         name="vq_forward",
     )
@@ -1168,12 +1182,38 @@
         name="mlp",
     )
 
+    def back_to_grid(value):
+        grid = grid_order(value, rows_here, cols_all, half)
+        returned = lax.ppermute(grid[half:], "blk", up_one)
+        return jnp.concatenate([returned, grid[:half]], axis=0)[None]
+
+    def flat(value):
+        return value.astype(f32).reshape(-1)
+
+    def gains_over_pages(db_all):
+        gain_sum = db_all[q_rows, : pages * gain_width].reshape(pages, gain_width).astype(f32)
+        kept = jnp.take(gain_sum, page_here, axis=0)
+        for k in range(1, pages):
+            kept = kept + swapped(jnp.take(gain_sum, page_here ^ k, axis=0), "page", k)
+        return kept
+
+    def late_sums(db_all, mlp_sum):
+        up_sum = mlp_sum[0].reshape(2, 2, share // 4, D)
+        mine = jnp.where(core_here == 0, up_sum[:, 0], up_sum[:, 1])
+        other = swapped(jnp.where(core_here == 0, up_sum[:, 1], up_sum[:, 0]), "blk", 1)
+        joined_up = jnp.where(
+            core_here == 0,
+            jnp.concatenate([mine, other], axis=0),
+            jnp.concatenate([other, mine], axis=0),
+        )
+        return gains_over_pages(db_all), flat(joined_up.transpose(1, 0, 2))
+
     up_entries = [(h_low, 0, du_low, k, "tn") for k in range(4)]
     down_entries = [(act_low, k, vis_cot, 0, "tn") for k in range(4)]
     where_vq_back = where
     if staged:
         m_keep, m_send = weight_grad_call(
-            where, [((0,), "up", up_entries), ((1,), "rows", down_entries)], "mlp_grads"
+            after(where, lse_qv, centre_qv), [((0,), "up", up_entries), ((1,), "rows", down_entries)], "mlp_grads"
         )
         where_vq_back = after(where, m_keep)
 
@@ -1184,16 +1224,25 @@
         flops=16e-6 * 1.1e15,
         name="vq_backward",
     )
+    where_swin_back = where_self_back = where_qv_back = where
+    if staged:
+        visual_out = back_to_grid(after(v3, m_keep))
+        where_qv_back = after(where, visual_out)
+        m_one = collect_first(m_keep, m_send, dqb)
+        where_qv_back = after(where, visual_out, m_one)
     dqat, dkva, *merged_parts = call(
         qv_backward_kernel,
         [sds((D, slots), bf16), sds((tokens, 2 * D), bf16)] + [sds((slots, 2 * D), bf16)],
-        [where, qa, kva, doa, lse_qv, centre_qv, dkvbt],
+        [where_qv_back, qa, kva, doa, lse_qv, centre_qv, dkvbt],
         scratch=[pltpu.VMEM((slots, 2 * D), bf16)],
         loads=[(w_qv, 0), (w_vq, 1), (w_vq, 2)],
         flops=23e-6 * 1.1e15,
         name="qv_backward",
     )
-    merged = collect_blocks(merged_parts)
+    merged = scattered_blocks(merged_parts[0])
+    if staged:
+        m_two = collect_second(m_one, dqat)
+        where_swin_back = after(where, m_two)
     dc, oa_low = merged[:, :D], merged[:, D:]
 
     def swin_backward(*refs):
@@ -1207,7 +1256,7 @@
             sds((tokens, D), f32),
             sds((2, D), f32),
         ],
-        [where, vis_in, v1, g2, gains, dkva, dqb, qkv_swin, lse_swin],
+        [where_swin_back, vis_in, v1, g2, gains, dkva, dqb, qkv_swin, lse_swin],
         scratch=[
             pltpu.VMEM((cols_all // rows_here, rows_here**2, rows_here**2), f32),
             pltpu.VMEM((tokens, D), bf16),
@@ -1232,11 +1281,14 @@
         (oa_low, 0, query_cot[0], 0, "tn"),
     ]
     if staged:
+        m_three = collect_third(m_two, dz_swin)
         p_keep, p_send = weight_grad_call(
-            where, [((0,), "rows", vq_entries), ((1,), "rows", swin_entries)], "patch_grads"
+            after(where, m_three), [((0,), "rows", vq_entries), ((1,), "rows", swin_entries)], "patch_grads"
         )
-
-    gy1, dz_self, dq_self, dkvt_self, dbq, dg4, *db_parts = call(
+        p_one = collect_first(p_keep, p_send)
+        where_self_back = after(where, p_one)
+
+    gy1, dz_self, dq_self, dkvt_self, dbq, dg_slots, *db_parts = call(
         self_backward_kernel,
         [
             sds((q_rows, D), f32),
@@ -1244,10 +1296,11 @@
             sds((q_rows, D), bf16),
             sds((2 * D, slots), bf16),
             sds((q_rows, D), f32),
-            sds((1, D), f32),
+            sds((2, D), f32),
         ]
         + ([sds((4, q_rows, D), bf16)] * 2 if staged else [sds((slots, D), bf16)]),
-        [where, dc, y1, query_cot[0], gains, q_self, kv_self, lse_self],
+        [where_self_back, dc, y1, query_cot[0], gains, q_self, kv_self, lse_self],
+        slots=(slot_arrays, 0, q_rows),
         scratch=[
             pltpu.VMEM((q_rows, slots), f32),
             pltpu.VMEM((q_rows, D), bf16),
@@ -1264,56 +1317,58 @@
         (b_all, 0, dkvt_self, 1, "tt"),
         (o_self, 0, dz_self, 0, "tn"),
     ]
-    db = collect_blocks(db_parts)
+    gain_block = jnp.concatenate(
+        [dg_visual[0:1], dg_slots[0:1], dg_visual[1:2], dg_slots[1:2], dg5, jnp.zeros((3, D), f32)],
+        axis=0,
+    )
+    gain_block = gain_block.astype(bf16).reshape(pages, blk_count, gain_width).transpose(1, 0, 2)
+    gain_block = gain_block.reshape(blk_count, 1, pages * gain_width)
+    gain_block = jnp.pad(gain_block, ((0, 0), (0, 15), (0, D - pages * gain_width)))
+    if staged:
+        order = (jnp.arange(8).reshape(4, 2) * 1).transpose(1, 0) ^ blk_here
+        db_parts = [
+            jnp.concatenate([db_parts[core], gain_block[order[core]]], axis=1) for core in range(2)
+        ]
+    else:
+        whole_part = db_parts[0].reshape(blk_count, q_rows, D)
+        whole_part = jnp.concatenate([whole_part, gain_block], axis=1)
+        db_all = scattered_blocks(whole_part.reshape(blk_count * (q_rows + 16), D)).astype(f32)
     where_end = where
     if staged:
+        p_two = collect_second(p_one, gy1)
+        mlp_sum = collect_last(m_three, gy1)
         z_keep, z_send = weight_grad_call(
-            where, [((0,), "rows", qv_entries), ((1,), "rows", self_entries)], "slot_grads"
+            after(where, p_two, mlp_sum), [((0,), "rows", qv_entries), ((1,), "rows", self_entries)], "slot_grads"
         )
-        m_one = collect_first(m_keep, m_send, dqb)
-        m_two = collect_second(m_one, dz_swin)
-        m_three = collect_third(m_two, gy1)
-        mlp_sum = collect_last(m_three, z_keep)
-        p_one = collect_first(p_keep, p_send, gy1)
-        p_two = collect_second(p_one, z_keep)
-        p_three = collect_third(p_two)
+        db_chips = blocks_in_chip(db_parts, z_keep)
         z_one = collect_first(z_keep, z_send)
-        where_end = after(where, z_keep)
-    query_grad, dg2, query_out = call(
+        db_all = blocks_over_chips(db_chips, z_one)
+        p_three = collect_third(p_two, z_keep)
+        z_two = collect_second(after(z_one, p_three, db_all))
+        patch_sum = collect_last(p_three)
+        z_two, db_all, mlp_sum = after((z_two, db_all, mlp_sum), patch_sum)
+        z_three = collect_third(z_two)
+        gain_grad, up_grad = late_sums(db_all, mlp_sum)
+        z_three = after(z_three, gain_grad, up_grad)
+        visual_grad = back_to_grid(after(visual_grad, z_three))
+        where_end = after(where, z_three, visual_grad)
+    db = db_all[:q_rows]
+    query_grad, query_out = call(
         query_end_kernel,
-        [sds((q_rows, D), f32), sds((1, D), f32), sds((q_rows, D), bf16)],
+        [sds((q_rows, D), f32), sds((q_rows, D), bf16)],
         [where_end, db, dbq, query_tokens[0], gy1, gains, y1, oa_low],
         loads=[(w_qv, 3)],
         name="query_end",
     )
 
-    gain_block = jnp.concatenate(
-        [dg_visual[0:1], dg2, dg_visual[1:2], dg4, dg5, jnp.zeros((3, D), f32)], axis=0
-    )
-    gain_sum = summed_everywhere(gain_block)
-    gain_grad = lax.dynamic_slice_in_dim(
-        gain_sum.reshape(-1), (page_here * blk_count + blk_here) * gain_width, gain_width, 0
-    )
-
-    def flat(value):
-        return value.astype(f32).reshape(-1)
-
     if staged:
-        patch_sum = collect_last(p_three)
-        slot_sum = collect_last(collect_third(collect_second(z_one)))
-        up_sum = mlp_sum[0].reshape(2, 2, share // 4, D)
-        up_mine = jnp.where(core_here == 0, up_sum[:, 0], up_sum[:, 1])
-        up_other = swapped(jnp.where(core_here == 0, up_sum[:, 1], up_sum[:, 0]), "blk", 1)
-        up_grad = jnp.where(
-            core_here == 0,
-            jnp.concatenate([up_mine, up_other], axis=0),
-            jnp.concatenate([up_other, up_mine], axis=0),
-        )
-        up_grad = flat(up_grad.transpose(1, 0, 2))
+        slot_sum = collect_last(z_three)
         swin_grad, self_grad = flat(patch_sum[1]), flat(slot_sum[1])
         qv_grad, vq_grad = flat(slot_sum[0]), flat(patch_sum[0])
         down_grad = flat(mlp_sum[1])
     else:
+        visual_out, visual_grad = back_to_grid(v3), back_to_grid(visual_grad)
+        gain_grad = gains_over_pages(db_all)
 
         def outer(left, right):
             return tn(left, right).astype(bf16)
@@ -1376,15 +1431,10 @@
         qv_grad, vq_grad = flat(cross_sum[:share]), flat(cross_sum[share:])
         swin_grad, self_grad = flat(last_sum[:share]), flat(last_sum[share:])
 
-    def back_to_grid(value):
-        grid = grid_order(value, rows_here, cols_all, half)
-        returned = lax.ppermute(grid[half:], "blk", up_one)
-        return jnp.concatenate([returned, grid[:half]], axis=0)[None]
-
     return (
-        back_to_grid(v3),
+        visual_out,
         query_out[None],
-        back_to_grid(visual_grad),
+        visual_grad,
         query_grad[None],
         swin_grad,
         self_grad,

time: 607 us -> 558 us (0.919)
  waiting for transfers between devices: 238 us -> 157 us
  starting transfers between devices: 70.6 us -> 87.4 us
  other arithmetic: 43.8 us -> 52.7 us
    ppermute x71 -> x69, waiting for transfers between devices: 235 us -> 155 us  [swapped(): return lax.ppermute(value, axis, [(i, i ^ flip) for i in range(count)])]
    ppermute x71 -> x69, starting transfers between devices: 68.3 us -> 85.7 us  [swapped(): return lax.ppermute(value, axis, [(i, i ^ flip) for i in range(count)])]
    unnamed x56 -> x71, local copies, waits for them, and re-layouts: 7.04 us -> 14.3 us
  transfers between devices with their start and end apart: 78 -> 76, of which waited for: 33 -> 26; matrix products, arithmetic and copies ran while one was open for 12% -> 12% of each run, Pallas kernels for 32% -> 30%
where the time goes in v3:
time: 558 us; the launch traced here: 548 us
  Pallas kernels  195 us (35%)
  waiting for transfers between devices  157 us (28%)
  starting transfers between devices  87.4 us (16%)
  other arithmetic  52.7 us (9%)
  local copies, waits for them, and re-layouts  39.6 us (7%)
  between operations  15.9 us (3%)
    ppermute x69, waiting for transfers between devices, swapped(): return lax.ppermute(value, axis, [(i, i ^ flip) for i in range(count)])  155 us
    pallas_call x10, Pallas kernels, call(): pl.pallas_call(body, grid=(1,), out_shape=shapes, in_specs=specs + [pl.Bl...  155 us
    ppermute x69, starting transfers between devices, swapped(): return lax.ppermute(value, axis, [(i, i ^ flip) for i in range(count)])  85.7 us
    pallas_call x3, Pallas kernels, weight_grad_call(): pl.pallas_call(body, grid=(1,), out_shape=shapes, in_specs=[pl.BlockSpec(...  40.4 us
    convert_element_type x16, other arithmetic, added(): return (left.astype(f32) + right.astype(f32)).astype(bf16)  28.2 us
    unnamed x71, local copies, waits for them, and re-layouts  14.3 us
  transfers between devices with their start and end apart: 76, of which 26 were waited for; matrix products, arithmetic and copies ran while one was open for 12% of the time, Pallas kernels for 30%

profile of v3, /device:TPU:0, one launch (start us, length us, event | category | flops | bytes accessed | tf_op | source)
XLA Modules:
  0.0 547.9 jit_solution(651669278512697873)
XLA Ops:
  17.7 9.7 %collective-permute-done = bf16[2,96,768]{2,1,0:T(8,128)(2,1)S(1)} collective-permute-done((bf16[2,96,768]{2,1,0:T(8,128)(2,1)}, bf16[2,96,768]{2,1,0:T(8,128)(2,1)S(1)}, u32[]{:S(2)}, u32[]{:S(2)}) %collective-permute-start) | collective-permute-done | bytes 294944 | tf_op jit(solution)/shard_map/ppermute | solution.py:893
  27.4 10.9 %collective-permute-done.1 = bf16[2,96,768]{2,1,0:T(8,128)(2,1)S(1)} collective-permute-done((bf16[2,96,768]{2,1,0:T(8,128)(2,1)}, bf16[2,96,768]{2,1,0:T(8,128)(2,1)S(1)}, u32[]{:S(2)}, u32[]{:S(2)}) %collective-permute-start.1) | collective-permute-done | bytes 294944 | tf_op jit(solution)/shard_map/ppermute | solution.py:893
  52.8 18.2 %collective-permute-done.4 = bf16[2,96,768]{2,1,0:T(8,128)(2,1)S(1)} collective-permute-done((bf16[2,96,768]{2,1,0:T(8,128)(2,1)S(1)}, bf16[2,96,768]{2,1,0:T(8,128)(2,1)S(1)}, u32[]{:S(2)}, u32[]{:S(2)}) %collective-permute-start.4) | collective-permute-done | bytes 294944 | tf_op jit(solution)/shard_map/ppermute | solution.py:893
  133.8 16.1 %self_forward.1 = (bf16[1024,768]{1,0:T(8,128)(2,1)}, bf16[128,768]{1,0:T(8,128)(2,1)}, bf16[1024,1536]{1,0:T(8,128)(2,1)}, f32[128,128]{1,0:T(8,128)}, bf16[128...) custom-call(s32[5]{0:T(128)} %stack.110.refs_0_, ...), custom_call_target="tpu_custom_call" | custom-call | flops 16499999744 | bytes 10510356 | tf_op jit(solution)/shard_map/self_forward/pallas_call | solution.py:232
  152.6 8.0 %collective-permute-done.16.refs_8_.refs_6_.refs_12_.refs_14_ = bf16[8,96,768]{2,1,0:T(8,128)(2,1)} collective-permute-done((bf16[8,96,768]{2,1,0:T(8,128)(2,1)}, bf16[8,96,768]{2,1,0:T(8,128)(2,1)}, u32[]{:S(2)}, u32[]{:S(2)}) %collective-permute-start.16) | collective-permute-done | bytes 1179680 | tf_op jit(solution)/shard_map/ppermute | solution.py:893
  164.4 14.8 %collective-permute-done.28 = bf16[4,96,768]{2,1,0:T(8,128)(2,1)S(1)} collective-permute-done((bf16[4,96,768]{2,1,0:T(8,128)(2,1)S(1)}, bf16[4,96,768]{2,1,0:T(8,128)(2,1)S(1)}, u32[]{:S(2)}, u32[]{:S(2)}) %collective-permute-start.28) | collective-permute-done | bytes 589856 | tf_op jit(solution)/shard_map/ppermute | solution.py:893
  179.8 11.5 %swin_forward.1 = (bf16[288,768]{1,0:T(8,128)(2,1)}, bf16[288,2304]{1,0:T(8,128)(2,1)}, f32[288,128]{1,0:T(8,128)}, bf16[288,768]{1,0:T(8,128)(2,1)}, f32[288,768]{1,0:T(8,128)}, /*index=5*/bf16[288,768]{1,0:T(8,128)(2,1)}) custom-call(s32[5]{0:T(128)} %stack.110.refs_0_, bf16[288,768]{1,0:T(8,128)(2,1)} %reshape.236.refs_1_, ...), custom_call_target="tpu_custom_call" | custom-call | flops 12099999744 | bytes 8871956 | tf_op jit(solution)/shard_map/swin_forward/pallas_call | solution.py:232
  198.9 21.1 %cross_forward.1 = (bf16[1024,768]{1,0:T(8,128)(2,1)}, bf16[1024,1536]{1,0:T(8,128)(2,1)}, bf16[1024,768]{1,0:T(8,128)(2,1)}, bf16[288,1536]{1,0:T(8,128)(2,1)},...) custom-call(s32[5]{0:T(128)} %stack.110.refs_0_, bf16[1024,768]{1,0:T(8,128)(2,1)} %all-gather.6.cloned.1.call-done.refs_1_.refs_3_, ...), custom_call_target="tpu_custom_call" | custom-call | flops 19800000512 | bytes 18087956 | tf_op jit(solution)/shard_map/cross_forward/pallas_call | solution.py:232
  221.8 11.7 %vq_forward.1 = (f32[288,128]{1,0:T(8,128)}, bf16[288,768]{1,0:T(8,128)(2,1)}) custom-call(s32[5]{0:T(128)} %stack.110.refs_0_, bf16[288,768]{1,0:T(8,128)(2,1)} %get-tuple-element.154.refs_1_, bf16[1024,1536]{1,0:T(8,128)(2,1)} %get-tuple-element.158.refs_2_), custom_call_target="tpu_custom_call" | custom-call | flops 12099999744 | bytes 4177940 | tf_op jit(solution)/shard_map/vq_forward/pallas_call | solution.py:232
  235.7 14.7 %mlp.1 = (bf16[288,768]{1,0:T(8,128)(2,1)}, bf16[288,768]{1,0:T(8,128)(2,1)}, bf16[288,3072]{1,0:T(8,128)(2,1)}, bf16[288,3072]{1,0:T(8,128)(2,1)}, f32[288,768]...) custom-call(s32[5]{0:T(128)} %stack.110.refs_0_, ...), custom_call_target="tpu_custom_call" | custom-call | flops 15399999488 | bytes 18607124 | tf_op jit(solution)/shard_map/mlp/pallas_call | solution.py:232
  253.8 11.6 %mlp_grads.1 = (bf16[2,16,96,768]{3,2,1,0:T(8,128)(2,1)}, bf16[2,16,96,768]{3,2,1,0:T(8,128)(2,1)}) custom-call(s32[5]{0:T(128)} %stack.110.refs_0_, bf16[288,768]{1,0:T(8,128)(2,1)} %get-tuple-element.163.refs_1_, bf16[288,3072]{1,0:T(8,128)(2,1)} %get-tuple-element.164.refs_2_, bf16[288,3072]{1,0:T(8,128)(2,1)} %get-tuple-element.165.refs_3_, ...), custom_call_target="tpu_custom_call" | custom-call | flops 14080000000 | bytes 13860864 | tf_op jit(solution)/shard_map/mlp_grads/pallas_call | solution.py:855
  266.6 16.0 %vq_backward.1 = (bf16[288,768]{1,0:T(8,128)(2,1)}, bf16[1536,1024]{1,0:T(8,128)(2,1)}) custom-call(s32[5]{0:T(128)} %stack.110.refs_0_, bf16[288,768]{1,0:T(8,128)(2,1)} %get-tuple-element.154.refs_1_, bf16[1024,1536]{1,0:T(8,128)(2,1)} %get-tuple-element.158.refs_2_, bf16[288,768]{1,0:T(8,128)(2,1)} %get-tuple-element.169.refs_3_, ...), custom_call_target="tpu_custom_call" | custom-call | flops 17600000000 | bytes 7766036 | tf_op jit(solution)/shard_map/vq_backward/pallas_call | solution.py:232
  289.3 22.7 %qv_backward.1 = (bf16[768,1024]{1,0:T(8,128)(2,1)}, bf16[288,1536]{1,0:T(8,128)(2,1)}, bf16[1024,1536]{1,0:T(8,128)(2,1)}) custom-call(s32[5]{0:T(128)} %stack.110.refs_0_, bf16[1024,768]{1,0:T(8,128)(2,1)} %get-tuple-element.175.refs_1_, bf16[288,1536]{1,0:T(8,128)(2,1)} %get-tuple-element.176.refs_2_, bf16[1024,768]{1,0:T(8,128)(2,1)} %get-tuple-element.177.refs_3_, ...), custom_call_target="tpu_custom_call" | custom-call | flops 25300000768 | bytes 16449556 | tf_op jit(solution)/shard_map/qv_backward/pallas_call | solution.py:232
  321.4 20.1 %swin_backward.1 = (bf16[288,768]{1,0:T(8,128)(2,1)}, bf16[288,2304]{1,0:T(8,128)(2,1)}, f32[288,768]{1,0:T(8,128)}, f32[2,768]{1,0:T(2,128)}) custom-call(s32[5]{0:T(128)} %stack.110.refs_0_, bf16[288,768]{1,0:T(8,128)(2,1)} %reshape.236.refs_1_, f32[288,768]{1,0:T(8,128)} %get-tuple-element.144.refs_1_.refs_2_, f32[288,768]{1,0:T(8,128)} %get-tuple-element.183.refs_3_, ...), custom_call_target="tpu_custom_call" | custom-call | flops 22000001024 | bytes 15955988 | tf_op jit(solution)/shard_map/swin_backward/pallas_call | solution.py:232
  343.5 14.0 %patch_grads.1 = (bf16[2,16,96,768]{3,2,1,0:T(8,128)(2,1)}, bf16[2,16,96,768]{3,2,1,0:T(8,128)(2,1)}) custom-call(s32[5]{0:T(128)} %stack.110.refs_0_, bf16[288,768]{1,0:T(8,128)(2,1)} %get-tuple-element.150.refs_2_.refs_1_.refs_3_, bf16[288,768]{1,0:T(8,128)(2,1)} %get-tuple-element.171.refs_6_.refs_2_, ...), custom_call_target="tpu_custom_call" | custom-call | flops 14080000000 | bytes 18579456 | tf_op jit(solution)/shard_map/patch_grads/pallas_call | solution.py:855
  372.4 16.9 %self_backward.1 = (f32[128,768]{1,0:T(8,128)}, bf16[128,768]{1,0:T(8,128)(2,1)}, bf16[128,768]{1,0:T(8,128)(2,1)}, bf16[1536,1024]{1,0:T(8,128)(2,1)}, f32[128,...) custom-call(s32[5]{0:T(128)} %stack.110.refs_0_, ...), custom_call_target="tpu_custom_call" | custom-call | flops 16499999744 | bytes 14841876 | tf_op jit(solution)/shard_map/self_backward/pallas_call | solution.py:232
  391.7 6.6 %collective-permute-done.46 = bf16[8,96,768]{2,1,0:T(8,128)(2,1)S(1)} collective-permute-done((bf16[8,96,768]{2,1,0:T(8,128)(2,1)S(1)}, bf16[8,96,768]{2,1,0:T(8,128)(2,1)S(1)}, u32[]{:S(2)}, u32[]{:S(2)}) %collective-permute-start.46) | collective-permute-done | bytes 1179680 | tf_op jit(solution)/shard_map/ppermute | solution.py:893
  400.5 14.8 %slot_grads.1 = (bf16[2,16,96,768]{3,2,1,0:T(8,128)(2,1)}, bf16[2,16,96,768]{3,2,1,0:T(8,128)(2,1)}) custom-call(s32[5]{0:T(128)} %stack.110.refs_0_, bf16[1024,768]{1,0:T(8,128)(2,1)} %all-gather.6.cloned.1.call-done.refs_1_.refs_3_, bf16[768,1024]{1,0:T(8,128)(2,1)} %get-tuple-element.179.refs_2_, ...), custom_call_target="tpu_custom_call" | custom-call | flops 14080000000 | bytes 19808256 | tf_op jit(solution)/shard_map/slot_grads/pallas_call | solution.py:855
  428.4 6.2 %collective-permute-done.51 = bf16[4,96,768]{2,1,0:T(8,128)(2,1)} collective-permute-done((bf16[4,96,768]{2,1,0:T(8,128)(2,1)}, bf16[4,96,768]{2,1,0:T(8,128)(2,1)}, u32[]{:S(2)}, u32[]{:S(2)}) %collective-permute-start.51) | collective-permute-done | bytes 589856 | tf_op jit(solution)/shard_map/ppermute | solution.py:893
  453.3 7.7 %collective-permute-done.61 = bf16[2,96,768]{2,1,0:T(8,128)(2,1)S(1)} collective-permute-done((bf16[2,96,768]{2,1,0:T(8,128)(2,1)}, bf16[2,96,768]{2,1,0:T(8,128)(2,1)S(1)}, u32[]{:S(2)}, u32[]{:S(2)}) %collective-permute-start.61) | collective-permute-done | bytes 294944 | tf_op jit(solution)/shard_map/ppermute | solution.py:893
  460.9 16.0 %collective-permute-done.60 = bf16[2,96,768]{2,1,0:T(8,128)(2,1)} collective-permute-done((bf16[2,96,768]{2,1,0:T(8,128)(2,1)}, bf16[2,96,768]{2,1,0:T(8,128)(2,1)}, u32[]{:S(2)}, u32[]{:S(2)}) %collective-permute-start.60) | collective-permute-done | bytes 294944 | tf_op jit(solution)/shard_map/ppermute | solution.py:893
  500.0 6.2 %collective-permute-done.63 = bf16[4,96,768]{2,1,0:T(8,128)(2,1)} collective-permute-done((bf16[4,96,768]{2,1,0:T(8,128)(2,1)}, bf16[4,96,768]{2,1,0:T(8,128)(2,1)}, u32[]{:S(2)}, u32[]{:S(2)}) %collective-permute-start.63) | collective-permute-done | bytes 589856 | tf_op jit(solution)/shard_map/ppermute | solution.py:893
  517.6 6.3 %collective-permute-done.69 = bf16[2,96,768]{2,1,0:T(8,128)(2,1)S(1)} collective-permute-done((bf16[2,96,768]{2,1,0:T(8,128)(2,1)}, bf16[2,96,768]{2,1,0:T(8,128)(2,1)S(1)}, u32[]{:S(2)}, u32[]{:S(2)}) %collective-permute-start.69) | collective-permute-done | bytes 294944 | tf_op jit(solution)/shard_map/ppermute | solution.py:893
  524.0 9.6 %collective-permute-done.70 = bf16[2,96,768]{2,1,0:T(8,128)(2,1)} collective-permute-done((bf16[2,96,768]{2,1,0:T(8,128)(2,1)}, bf16[2,96,768]{2,1,0:T(8,128)(2,1)}, u32[]{:S(2)}, u32[]{:S(2)}) %collective-permute-start.70) | collective-permute-done | bytes 294944 | tf_op jit(solution)/shard_map/ppermute | solution.py:893
  (381 shorter events, 220.5 us)
Async XLA Ops:
  7.2 74.7 %all-gather.8.cloned.1.call-start = ((), (), s32[]{:S(2)}) async-start(), calls=%async_computation.3 | async-start | bytes 3760128 | tf_op jit(solution)/shard_map/all_gather | solution.py:1017
  9.8 188.1 %all-gather.6.cloned.1.call-start = ((), (), s32[]{:S(2)}) async-start(), calls=%async_computation.1 | async-start | bytes 1769472 | tf_op jit(solution)/shard_map/all_gather | solution.py:1102
  45.8 28.0 %collective-permute-start.8 = (bf16[4,96,768]{2,1,0:T(8,128)(2,1)S(1)}, bf16[4,96,768]{2,1,0:T(8,128)(2,1)S(1)}, u32[]{:S(2)}, u32[]{:S(2)}) collective-permute-start(bf16[4,96,768]{2,1,0:T(8,128)(2,1)S(1)} %pad_maximum_fusion.3), channel_id=1, source_target_pairs={{0,4},{1,5},{2,6},{3,7},{4,0},{5,1},{6,2},{7,3},{8,12},{9,13},{10,... | collective-permute-start | bytes 1769480 | tf_op jit(solution)/shard_map/ppermute | solution.py:893
  75.3 28.7 %collective-permute-start.9 = (bf16[8,96,768]{2,1,0:T(8,128)(2,1)}, bf16[8,96,768]{2,1,0:T(8,128)(2,1)}, u32[]{:S(2)}, u32[]{:S(2)}) collective-permute-start(bf16[8,96,768]{2,1,0:T(8,128)(2,1)} %copy-done.12), channel_id=1, source_target_pairs={{0,2},{1,3},{2,0},{3,1},{4,6},{5,7},{6,4},{7,5},{8,10},{9,11},{10,... | collective-permute-start | bytes 3538952 | tf_op jit(solution)/shard_map/ppermute | solution.py:893
  91.8 37.7 %collective-permute-start.18 = (bf16[8,96,768]{2,1,0:T(8,128)(2,1)}, bf16[8,96,768]{2,1,0:T(8,128)(2,1)}, u32[]{:S(2)}, u32[]{:S(2)}) collective-permute-start(bf16[8,96,768]{2,1,0:T(8,128)(2,1)} %constant_dynamic-update-slice_fusion.2.refs_2_.refs_8_), channel_id=1, source_target_pairs={{0,1},{1,0},{2,3},{3,2},{4,5},{5,4},{6,7},{7,6},{8,9},{9,8},{10,11... | collective-permute-start | bytes 3538952 | tf_op jit(solution)/shard_map/ppermute | solution.py:893
  91.9 72.1 %collective-permute-start.20 = (bf16[8,96,768]{2,1,0:T(8,128)(2,1)}, bf16[8,96,768]{2,1,0:T(8,128)(2,1)}, u32[]{:S(2)}, u32[]{:S(2)}) collective-permute-start(bf16[8,96,768]{2,1,0:T(8,128)(2,1)} %copy-done.12), channel_id=1, source_target_pairs={{0,1},{1,0},{2,3},{3,2},{4,5},{5,4},{6,7},{7,6},{8,9},{9,8},{10,11... | collective-permute-start | bytes 3538952 | tf_op jit(solution)/shard_map/ppermute | solution.py:893
  97.8 35.4 %collective-permute-start.19 = (bf16[8,96,768]{2,1,0:T(8,128)(2,1)}, bf16[8,96,768]{2,1,0:T(8,128)(2,1)}, u32[]{:S(2)}, u32[]{:S(2)}) collective-permute-start(bf16[8,96,768]{2,1,0:T(8,128)(2,1)} %collective-permute-done.7.refs_3_.refs_9_), channel_id=1, source_target_pairs={{0,1},{1,0},{2,3},{3,2},{4,5},{5,4},{6,7},{7,6},{8,9},{9,8},{10,11... | collective-permute-start | bytes 3538952 | tf_op jit(solution)/shard_map/ppermute | solution.py:893
  119.3 31.0 %collective-permute-start.24 = (bf16[2,96,768]{2,1,0:T(8,128)(2,1)S(1)}, bf16[2,96,768]{2,1,0:T(8,128)(2,1)}, u32[]{:S(2)}, u32[]{:S(2)}) collective-permute-start(bf16[2,96,768]{2,1,0:T(8,128)(2,1)S(1)} %copy-done.20), channel_id=1, source_target_pairs={{0,16},{8,24},{16,0},{24,8},{1,17},{9,25},{17,1},{25,9},{2,18},{10... | collective-permute-start | bytes 884744 | tf_op jit(solution)/shard_map/ppermute | solution.py:893
  129.6 31.0 %collective-permute-start.16 = (bf16[8,96,768]{2,1,0:T(8,128)(2,1)}, bf16[8,96,768]{2,1,0:T(8,128)(2,1)}, u32[]{:S(2)}, u32[]{:S(2)}) collective-permute-start(bf16[8,96,768]{2,1,0:T(8,128)(2,1)} %constant_dynamic-update-slice_fusion.8.refs_7_.refs_5_.refs_11_.refs_13_), channel_id=1, source_target_pairs={{0,2},{1,3},{2,0},{3,1},{4,6},{5,7},{6,4},{7,5},{8,10},{9,11},{10,... | collective-permute-start | bytes 3538952 | tf_op jit(solution)/shard_map/ppermute | solution.py:893
  133.3 29.1 %collective-permute-start.14 = (bf16[8,96,768]{2,1,0:T(8,128)(2,1)S(1)}, bf16[8,96,768]{2,1,0:T(8,128)(2,1)S(1)}, u32[]{:S(2)}, u32[]{:S(2)}) collective-permute-start(bf16[8,96,768]{2,1,0:T(8,128)(2,1)S(1)} %constant_dynamic-update-slice_fusion.6.refs_3_.refs_7_.refs_9_.refs_8_), channel_id=1, source_target_pairs={{0,4},{1,5},{2,6},{3,7},{4,0},{5,1},{6,2},{7,3},{8,12},{9,13},{10,... | collective-permute-start | bytes 3538952 | tf_op jit(solution)/shard_map/ppermute | solution.py:893
  149.9 100.5 %all-gather.10.cloned.1.call-start = ((), (), s32[]{:S(2)}) async-start(), calls=%async_computation.4 | async-start | bytes 1769472 | tf_op jit(solution)/shard_map/all_gather | solution.py:1159
  163.4 32.9 %collective-permute-start.32 = (bf16[8,96,768]{2,1,0:T(8,128)(2,1)}, bf16[8,96,768]{2,1,0:T(8,128)(2,1)S(1)}, u32[]{:S(2)}, u32[]{:S(2)}) collective-permute-start(bf16[8,96,768]{2,1,0:T(8,128)(2,1)} %constant_dynamic-update-slice_fusion.8.refs_7_.refs_5_.refs_11_.refs_13_), channel_id=1, source_target_pairs={{0,1},{1,0},{2,3},{3,2},{4,5},{5,4},{6,7},{7,6},{8,9},{9,8},{10,11... | collective-permute-start | bytes 3538952 | tf_op jit(solution)/shard_map/ppermute | solution.py:893
  163.4 34.5 %collective-permute-start.30 = (bf16[8,96,768]{2,1,0:T(8,128)(2,1)S(1)}, bf16[8,96,768]{2,1,0:T(8,128)(2,1)S(1)}, u32[]{:S(2)}, u32[]{:S(2)}) collective-permute-start(bf16[8,96,768]{2,1,0:T(8,128)(2,1)S(1)} %constant_dynamic-update-slice_fusion.6.refs_3_.refs_7_.refs_9_.refs_8_), channel_id=1, source_target_pairs={{0,1},{1,0},{2,3},{3,2},{4,5},{5,4},{6,7},{7,6},{8,9},{9,8},{10,11... | collective-permute-start | bytes 3538952 | tf_op jit(solution)/shard_map/ppermute | solution.py:893
  163.9 34.0 %collective-permute-start.31 = (bf16[8,96,768]{2,1,0:T(8,128)(2,1)S(1)}, bf16[8,96,768]{2,1,0:T(8,128)(2,1)}, u32[]{:S(2)}, u32[]{:S(2)}) collective-permute-start(bf16[8,96,768]{2,1,0:T(8,128)(2,1)S(1)} %collective-permute-done.14.refs_4_.refs_8_.refs_10_.refs_9_), channel_id=1, source_target_pairs={{0,1},{1,0},{2,3},{3,2},{4,5},{5,4},{6,7},{7,6},{8,9},{9,8},{10,11... | collective-permute-start | bytes 3538952 | tf_op jit(solution)/shard_map/ppermute | solution.py:893
  164.0 33.9 %collective-permute-start.33 = (bf16[8,96,768]{2,1,0:T(8,128)(2,1)}, bf16[8,96,768]{2,1,0:T(8,128)(2,1)}, u32[]{:S(2)}, u32[]{:S(2)}) collective-permute-start(bf16[8,96,768]{2,1,0:T(8,128)(2,1)} %collective-permute-done.16.refs_8_.refs_6_.refs_12_.refs_14_), channel_id=1, source_target_pairs={{0,1},{1,0},{2,3},{3,2},{4,5},{5,4},{6,7},{7,6},{8,9},{9,8},{10,11... | collective-permute-start | bytes 3538952 | tf_op jit(solution)/shard_map/ppermute | solution.py:893
  193.9 27.3 %collective-permute-start.29 = (bf16[8,96,768]{2,1,0:T(8,128)(2,1)}, bf16[8,96,768]{2,1,0:T(8,128)(2,1)}, u32[]{:S(2)}, u32[]{:S(2)}) collective-permute-start(bf16[8,96,768]{2,1,0:T(8,128)(2,1)} %constant_dynamic-update-slice_fusion.12.refs_13_), channel_id=1, source_target_pairs={{0,2},{1,3},{2,0},{3,1},{4,6},{5,7},{6,4},{7,5},{8,10},{9,11},{10,... | collective-permute-start | bytes 3538952 | tf_op jit(solution)/shard_map/ppermute | solution.py:893
  220.1 143.6 %reduce-scatter.2.cloned.1.call-start = ((), (), s32[]{:S(2)}) async-start(), calls=%async_computation.2 | async-start | bytes 3538944 | tf_op jit(solution)/shard_map/reduce_scatter | solution.py:969
  287.3 29.1 %collective-permute-start.40 = (bf16[8,96,768]{2,1,0:T(8,128)(2,1)}, bf16[8,96,768]{2,1,0:T(8,128)(2,1)}, u32[]{:S(2)}, u32[]{:S(2)}) collective-permute-start(bf16[8,96,768]{2,1,0:T(8,128)(2,1)} %get-tuple-element.269), channel_id=1, source_target_pairs={{0,2},{1,3},{2,0},{3,1},{4,6},{5,7},{6,4},{7,5},{8,10},{9,11},{10,... | collective-permute-start | bytes 3538952 | tf_op jit(solution)/shard_map/ppermute | solution.py:893
  287.8 31.0 %collective-permute-start.41 = (bf16[8,96,768]{2,1,0:T(8,128)(2,1)S(1)}, bf16[8,96,768]{2,1,0:T(8,128)(2,1)}, u32[]{:S(2)}, u32[]{:S(2)}) collective-permute-start(bf16[8,96,768]{2,1,0:T(8,128)(2,1)S(1)} %get-tuple-element.270), channel_id=1, source_target_pairs={{0,4},{1,5},{2,6},{3,7},{4,0},{5,1},{6,2},{7,3},{8,12},{9,13},{10,... | collective-permute-start | bytes 3538952 | tf_op jit(solution)/shard_map/ppermute | solution.py:893
  359.2 30.1 %collective-permute-start.49 = (bf16[2,96,768]{2,1,0:T(8,128)(2,1)}, bf16[2,96,768]{2,1,0:T(8,128)(2,1)S(1)}, u32[]{:S(2)}, u32[]{:S(2)}) collective-permute-start(bf16[2,96,768]{2,1,0:T(8,128)(2,1)} %pad_maximum_fusion.17), channel_id=1, source_target_pairs={{0,24},{8,16},{16,8},{24,0},{1,25},{9,17},{17,9},{25,1},{2,26},{10... | collective-permute-start | bytes 884744 | tf_op jit(solution)/shard_map/ppermute | solution.py:893
  370.2 28.1 %collective-permute-start.46 = (bf16[8,96,768]{2,1,0:T(8,128)(2,1)S(1)}, bf16[8,96,768]{2,1,0:T(8,128)(2,1)S(1)}, u32[]{:S(2)}, u32[]{:S(2)}) collective-permute-start(bf16[8,96,768]{2,1,0:T(8,128)(2,1)S(1)} %get-tuple-element.265), channel_id=1, source_target_pairs={{0,4},{1,5},{2,6},{3,7},{4,0},{5,1},{6,2},{7,3},{8,12},{9,13},{10,... | collective-permute-start | bytes 3538952 | tf_op jit(solution)/shard_map/ppermute | solution.py:893
  370.7 28.7 %collective-permute-start.45 = (bf16[8,96,768]{2,1,0:T(8,128)(2,1)S(1)}, bf16[8,96,768]{2,1,0:T(8,128)(2,1)S(1)}, u32[]{:S(2)}, u32[]{:S(2)}) collective-permute-start(bf16[8,96,768]{2,1,0:T(8,128)(2,1)S(1)} %get-tuple-element.266), channel_id=1, source_target_pairs={{0,2},{1,3},{2,0},{3,1},{4,6},{5,7},{6,4},{7,5},{8,10},{9,11},{10,... | collective-permute-start | bytes 3538952 | tf_op jit(solution)/shard_map/ppermute | solution.py:893
  446.7 32.2 %collective-permute-start.58 = (bf16[8,96,768]{2,1,0:T(8,128)(2,1)}, bf16[8,96,768]{2,1,0:T(8,128)(2,1)}, u32[]{:S(2)}, u32[]{:S(2)}) collective-permute-start(bf16[8,96,768]{2,1,0:T(8,128)(2,1)} %get-tuple-element.229), channel_id=1, source_target_pairs={{0,4},{1,5},{2,6},{3,7},{4,0},{5,1},{6,2},{7,3},{8,12},{9,13},{10,... | collective-permute-start | bytes 3538952 | tf_op jit(solution)/shard_map/ppermute | solution.py:893
  447.3 33.9 %collective-permute-start.57 = (bf16[8,96,768]{2,1,0:T(8,128)(2,1)}, bf16[8,96,768]{2,1,0:T(8,128)(2,1)}, u32[]{:S(2)}, u32[]{:S(2)}) collective-permute-start(bf16[8,96,768]{2,1,0:T(8,128)(2,1)} %get-tuple-element.227), channel_id=1, source_target_pairs={{0,2},{1,3},{2,0},{3,1},{4,6},{5,7},{6,4},{7,5},{8,10},{9,11},{10,... | collective-permute-start | bytes 3538952 | tf_op jit(solution)/shard_map/ppermute | solution.py:893
  (84 other events, 1104.9 us)
Sparse Core Ops, SparseCore 0:
  10.5 35.8 all-gather.7
  150.1 28.7 all-gather.5
  220.2 25.6 all-gather.9
  312.1 47.0 reduce-scatter.1

commit v4 on v3

--- a/solution.py
+++ b/solution.py
@@ -905,7 +905,7 @@
 
 def spread_second(held, *gate):
     got = swapped(held[0], "blk", 2), swapped(held[1], "blk", 4)
-    held = after(held, *gate)
+    held, got = after((held, got), *gate)
     return [jnp.concatenate([held[k], got[k]]) for k in range(2)]
 
 
@@ -1072,7 +1072,7 @@
 
     where_self = where_swin = where_cross = where_vq = where
     if staged:
-        where_self = after(where, vis_in, vis_cot)
+        where_self = after(where, vis_in, vis_cot, a_near_core, a_far_core)
     b_all, q_self, kv_self, lse_self, o_self, y1, c_own = call(
         self_forward_kernel,
         [
@@ -1092,12 +1092,13 @@
         name="self_forward",
     )
     if staged:
-        c_far = after(c_far, c_own)
-        c_near_core, c_far_core = spread_core(c_near), spread_core(c_far)
+        c_near_core = spread_core(c_near)
+        c_far, c_near_core = after((c_far, c_near_core), c_own)
+        c_far_core = spread_core(c_far)
         w_qv, w_vq = [
             Stored(lane_arrays(c_near, c_far, c_near_core, c_far_core, k), (k,)) for k in range(2)
         ]
-        where_swin = after(where, c_far)
+        where_swin = after(where, c_far, c_near_core)
         d_z = after(d_z, c_far)
     c_all = lax.all_gather(c_own, "blk", axis=0, tiled=True)
 
@@ -1182,9 +1183,10 @@
         name="mlp",
     )
 
-    def back_to_grid(value):
+    def back_to_grid(value, *gate):
         grid = grid_order(value, rows_here, cols_all, half)
         returned = lax.ppermute(grid[half:], "blk", up_one)
+        returned, grid = after((returned, grid), *gate)
         return jnp.concatenate([returned, grid[:half]], axis=0)[None]
 
     def flat(value):
@@ -1197,7 +1199,16 @@
             kept = kept + swapped(jnp.take(gain_sum, page_here ^ k, axis=0), "page", k)
         return kept
 
-    def late_sums(db_all, mlp_sum):
+    def with_gains(held, db_all):
+        gain_sum = db_all[q_rows, : pages * gain_width].reshape(pages, gain_width)
+        joined = []
+        for k in range(pages):
+            row = jnp.take(gain_sum, page_here ^ k, axis=0)[None, None]
+            row = jnp.pad(row, ((0, 1), (0, 7), (0, D - gain_width)))
+            joined.append(jnp.concatenate([held[k], row], axis=1))
+        return joined
+
+    def up_over_core(mlp_sum):
         up_sum = mlp_sum[0].reshape(2, 2, share // 4, D)
         mine = jnp.where(core_here == 0, up_sum[:, 0], up_sum[:, 1])
         other = swapped(jnp.where(core_here == 0, up_sum[:, 1], up_sum[:, 0]), "blk", 1)
@@ -1206,7 +1217,7 @@
             jnp.concatenate([mine, other], axis=0),
             jnp.concatenate([other, mine], axis=0),
         )
-        return gains_over_pages(db_all), flat(joined_up.transpose(1, 0, 2))
+        return flat(joined_up.transpose(1, 0, 2))
 
     up_entries = [(h_low, 0, du_low, k, "tn") for k in range(4)]
     down_entries = [(act_low, k, vis_cot, 0, "tn") for k in range(4)]
@@ -1288,7 +1299,7 @@
         p_one = collect_first(p_keep, p_send)
         where_self_back = after(where, p_one)
 
-    gy1, dz_self, dq_self, dkvt_self, dbq, dg_slots, *db_parts = call(
+    gy1, dz_self, dq_self, dkvt_self, dbq, dg_slots, db_part = call(
         self_backward_kernel,
         [
             sds((q_rows, D), f32),
@@ -1298,7 +1309,7 @@
             sds((q_rows, D), f32),
             sds((2, D), f32),
         ]
-        + ([sds((4, q_rows, D), bf16)] * 2 if staged else [sds((slots, D), bf16)]),
+        + [sds((slots, D), bf16)],
         [where_self_back, dc, y1, query_cot[0], gains, q_self, kv_self, lse_self],
         slots=(slot_arrays, 0, q_rows),
         scratch=[
@@ -1324,15 +1335,8 @@
     gain_block = gain_block.astype(bf16).reshape(pages, blk_count, gain_width).transpose(1, 0, 2)
     gain_block = gain_block.reshape(blk_count, 1, pages * gain_width)
     gain_block = jnp.pad(gain_block, ((0, 0), (0, 15), (0, D - pages * gain_width)))
-    if staged:
-        order = (jnp.arange(8).reshape(4, 2) * 1).transpose(1, 0) ^ blk_here
-        db_parts = [
-            jnp.concatenate([db_parts[core], gain_block[order[core]]], axis=1) for core in range(2)
-        ]
-    else:
-        whole_part = db_parts[0].reshape(blk_count, q_rows, D)
-        whole_part = jnp.concatenate([whole_part, gain_block], axis=1)
-        db_all = scattered_blocks(whole_part.reshape(blk_count * (q_rows + 16), D)).astype(f32)
+    whole_part = jnp.concatenate([db_part.reshape(blk_count, q_rows, D), gain_block], axis=1)
+    db_all = scattered_blocks(whole_part.reshape(blk_count * (q_rows + 16), D))
     where_end = where
     if staged:
         p_two = collect_second(p_one, gy1)
@@ -1340,18 +1344,17 @@
         z_keep, z_send = weight_grad_call(
             after(where, p_two, mlp_sum), [((0,), "rows", qv_entries), ((1,), "rows", self_entries)], "slot_grads"
         )
-        db_chips = blocks_in_chip(db_parts, z_keep)
+        visual_grad = back_to_grid(visual_grad, z_keep)
+        z_keep, z_send = after((z_keep, z_send), visual_grad)
         z_one = collect_first(z_keep, z_send)
-        db_all = blocks_over_chips(db_chips, z_one)
-        p_three = collect_third(p_two, z_keep)
-        z_two = collect_second(after(z_one, p_three, db_all))
-        patch_sum = collect_last(p_three)
-        z_two, db_all, mlp_sum = after((z_two, db_all, mlp_sum), patch_sum)
-        z_three = collect_third(z_two)
-        gain_grad, up_grad = late_sums(db_all, mlp_sum)
-        z_three = after(z_three, gain_grad, up_grad)
-        visual_grad = back_to_grid(after(visual_grad, z_three))
-        where_end = after(where, z_three, visual_grad)
+        p_three = collect_third(p_two, z_one)
+        z_two = collect_second(after(z_one, p_three))
+        patch_sum = collect_last(after(p_three, z_one))
+        db_all = after(db_all, patch_sum)
+        up_grad = up_over_core(mlp_sum)
+        z_two = after(z_two, patch_sum, up_grad)
+        z_three = with_gains(collect_third(z_two), db_all)
+        where_end = after(where, z_three)
     db = db_all[:q_rows]
     query_grad, query_out = call(
         query_end_kernel,
@@ -1363,6 +1366,7 @@
 
     if staged:
         slot_sum = collect_last(z_three)
+        gain_grad, slot_sum = slot_sum[0, share, :gain_width], slot_sum[:, :share]
         swin_grad, self_grad = flat(patch_sum[1]), flat(slot_sum[1])
         qv_grad, vq_grad = flat(slot_sum[0]), flat(patch_sum[0])
         down_grad = flat(mlp_sum[1])

time: 558 us -> 533 us (0.955)
  starting transfers between devices: 87.4 us -> 75.5 us
    ppermute x69 -> x62, starting transfers between devices: 85.7 us -> 72.4 us  [swapped(): return lax.ppermute(value, axis, [(i, i ^ flip) for i in range(count)])]
    unnamed x71 -> x65, local copies, waits for them, and re-layouts: 14.3 us -> 8.1 us
    ppermute x69 -> x62, waiting for transfers between devices: 155 us -> 150 us  [swapped(): return lax.ppermute(value, axis, [(i, i ^ flip) for i in range(count)])]
    convert_element_type x16 -> x15, other arithmetic: 28.2 us -> 27.5 us  [added(): return (left.astype(f32) + right.astype(f32)).astype(bf16)]
  transfers between devices with their start and end apart: 76 -> 70, of which waited for: 26 -> 32; matrix products, arithmetic and copies ran while one was open for 12% -> 12% of each run, Pallas kernels for 30% -> 35%
where the time goes in v4:
time: 533 us; the launch traced here: 525 us
  Pallas kernels  195 us (37%)
  waiting for transfers between devices  155 us (29%)
  starting transfers between devices  75.5 us (14%)
  other arithmetic  49.2 us (9%)
  local copies, waits for them, and re-layouts  34.7 us (7%)
  between operations  15.9 us (3%)
    pallas_call x10, Pallas kernels, call(): pl.pallas_call(body, grid=(1,), out_shape=shapes, in_specs=specs + [pl.Bl...  155 us
    ppermute x62, waiting for transfers between devices, swapped(): return lax.ppermute(value, axis, [(i, i ^ flip) for i in range(count)])  150 us
    ppermute x62, starting transfers between devices, swapped(): return lax.ppermute(value, axis, [(i, i ^ flip) for i in range(count)])  72.4 us
    pallas_call x3, Pallas kernels, weight_grad_call(): pl.pallas_call(body, grid=(1,), out_shape=shapes, in_specs=[pl.BlockSpec(...  40.4 us
    convert_element_type x15, other arithmetic, added(): return (left.astype(f32) + right.astype(f32)).astype(bf16)  27.5 us
  transfers between devices with their start and end apart: 70, of which 32 were waited for; matrix products, arithmetic and copies ran while one was open for 12% of the time, Pallas kernels for 35%

profile of v4, /device:TPU:0, one launch (start us, length us, event | category | flops | bytes accessed | tf_op | source)
XLA Modules:
  0.0 525.5 jit_solution(15734661611872385310)
XLA Ops:
  16.4 9.6 %collective-permute-done = bf16[2,96,768]{2,1,0:T(8,128)(2,1)S(1)} collective-permute-done((bf16[2,96,768]{2,1,0:T(8,128)(2,1)S(1)}, bf16[2,96,768]{2,1,0:T(8,128)(2,1)S(1)}, u32[]{:S(2)}, u32[]{:S(2)}) %collective-permute-start) | collective-permute-done | bytes 294944 | tf_op jit(solution)/shard_map/ppermute | solution.py:893
  26.0 10.9 %collective-permute-done.1 = bf16[2,96,768]{2,1,0:T(8,128)(2,1)S(1)} collective-permute-done((bf16[2,96,768]{2,1,0:T(8,128)(2,1)S(1)}, bf16[2,96,768]{2,1,0:T(8,128)(2,1)S(1)}, u32[]{:S(2)}, u32[]{:S(2)}) %collective-permute-start.1) | collective-permute-done | bytes 294944 | tf_op jit(solution)/shard_map/ppermute | solution.py:893
  64.0 7.7 %collective-permute-done.4 = bf16[2,96,768]{2,1,0:T(8,128)(2,1)S(1)} collective-permute-done((bf16[2,96,768]{2,1,0:T(8,128)(2,1)}, bf16[2,96,768]{2,1,0:T(8,128)(2,1)S(1)}, u32[]{:S(2)}, u32[]{:S(2)}) %collective-permute-start.4) | collective-permute-done | bytes 294944 | tf_op jit(solution)/shard_map/ppermute | solution.py:893
  79.8 6.4 %collective-permute-done.9.refs_4_.refs_18_ = bf16[8,96,768]{2,1,0:T(8,128)(2,1)} collective-permute-done((bf16[8,96,768]{2,1,0:T(8,128)(2,1)}, bf16[8,96,768]{2,1,0:T(8,128)(2,1)}, u32[]{:S(2)}, u32[]{:S(2)}) %collective-permute-start.9) | collective-permute-done | bytes 1179680 | tf_op jit(solution)/shard_map/ppermute | solution.py:893
  108.4 7.9 %collective-permute-done.13 = bf16[4,96,768]{2,1,0:T(8,128)(2,1)} collective-permute-done((bf16[4,96,768]{2,1,0:T(8,128)(2,1)S(1)}, bf16[4,96,768]{2,1,0:T(8,128)(2,1)}, u32[]{:S(2)}, u32[]{:S(2)}) %collective-permute-start.13) | collective-permute-done | bytes 589856 | tf_op jit(solution)/shard_map/ppermute | solution.py:893
  121.7 16.1 %self_forward.1 = (bf16[1024,768]{1,0:T(8,128)(2,1)}, bf16[128,768]{1,0:T(8,128)(2,1)}, bf16[1024,1536]{1,0:T(8,128)(2,1)}, f32[128,128]{1,0:T(8,128)}, bf16[128...) custom-call(s32[5]{0:T(128)} %stack.110.refs_0_, ...), custom_call_target="tpu_custom_call" | custom-call | flops 16499999744 | bytes 10510356 | tf_op jit(solution)/shard_map/self_forward/pallas_call | solution.py:232
  142.9 6.6 %collective-permute-done.27 = bf16[2,96,768]{2,1,0:T(8,128)(2,1)S(1)} collective-permute-done((bf16[2,96,768]{2,1,0:T(8,128)(2,1)}, bf16[2,96,768]{2,1,0:T(8,128)(2,1)S(1)}, u32[]{:S(2)}, u32[]{:S(2)}) %collective-permute-start.27) | collective-permute-done | bytes 294944 | tf_op jit(solution)/shard_map/ppermute | solution.py:893
  152.6 11.6 %swin_forward.1 = (bf16[288,768]{1,0:T(8,128)(2,1)}, bf16[288,2304]{1,0:T(8,128)(2,1)}, f32[288,128]{1,0:T(8,128)}, bf16[288,768]{1,0:T(8,128)(2,1)}, f32[288,768]{1,0:T(8,128)}, /*index=5*/bf16[288,768]{1,0:T(8,128)(2,1)}) custom-call(s32[5]{0:T(128)} %stack.110.refs_0_, bf16[288,768]{1,0:T(8,128)(2,1)} %reshape.163.refs_1_, ...), custom_call_target="tpu_custom_call" | custom-call | flops 12099999744 | bytes 8871956 | tf_op jit(solution)/shard_map/swin_forward/pallas_call | solution.py:232
  164.2 6.4 %collective-permute-done.28 = bf16[4,96,768]{2,1,0:T(8,128)(2,1)S(1)} collective-permute-done((bf16[4,96,768]{2,1,0:T(8,128)(2,1)S(1)}, bf16[4,96,768]{2,1,0:T(8,128)(2,1)S(1)}, u32[]{:S(2)}, u32[]{:S(2)}) %collective-permute-start.28) | collective-permute-done | bytes 589856 | tf_op jit(solution)/shard_map/ppermute | solution.py:893
  175.1 21.1 %cross_forward.1 = (bf16[1024,768]{1,0:T(8,128)(2,1)}, bf16[1024,1536]{1,0:T(8,128)(2,1)}, bf16[1024,768]{1,0:T(8,128)(2,1)}, bf16[288,1536]{1,0:T(8,128)(2,1)},...) custom-call(s32[5]{0:T(128)} %stack.110.refs_0_, bf16[1024,768]{1,0:T(8,128)(2,1)} %all-gather.6.cloned.1.call-done.refs_1_.refs_3_, ...), custom_call_target="tpu_custom_call" | custom-call | flops 19800000512 | bytes 18087956 | tf_op jit(solution)/shard_map/cross_forward/pallas_call | solution.py:232
  199.7 11.7 %vq_forward.1 = (f32[288,128]{1,0:T(8,128)}, bf16[288,768]{1,0:T(8,128)(2,1)}) custom-call(s32[5]{0:T(128)} %stack.110.refs_0_, bf16[288,768]{1,0:T(8,128)(2,1)} %get-tuple-element.171.refs_1_, bf16[1024,1536]{1,0:T(8,128)(2,1)} %get-tuple-element.175.refs_2_), custom_call_target="tpu_custom_call" | custom-call | flops 12099999744 | bytes 4177940 | tf_op jit(solution)/shard_map/vq_forward/pallas_call | solution.py:232
  213.6 14.7 %mlp.1 = (bf16[288,768]{1,0:T(8,128)(2,1)}, bf16[288,768]{1,0:T(8,128)(2,1)}, bf16[288,3072]{1,0:T(8,128)(2,1)}, bf16[288,3072]{1,0:T(8,128)(2,1)}, f32[288,768]...) custom-call(s32[5]{0:T(128)} %stack.110.refs_0_, ...), custom_call_target="tpu_custom_call" | custom-call | flops 15399999488 | bytes 18607124 | tf_op jit(solution)/shard_map/mlp/pallas_call | solution.py:232
  231.6 11.6 %mlp_grads.1 = (bf16[2,16,96,768]{3,2,1,0:T(8,128)(2,1)}, bf16[2,16,96,768]{3,2,1,0:T(8,128)(2,1)}) custom-call(s32[5]{0:T(128)} %stack.110.refs_0_, bf16[288,768]{1,0:T(8,128)(2,1)} %get-tuple-element.180.refs_1_, bf16[288,3072]{1,0:T(8,128)(2,1)} %get-tuple-element.181.refs_2_, bf16[288,3072]{1,0:T(8,128)(2,1)} %get-tuple-element.182.refs_3_, ...), custom_call_target="tpu_custom_call" | custom-call | flops 14080000000 | bytes 13860864 | tf_op jit(solution)/shard_map/mlp_grads/pallas_call | solution.py:855
  244.4 16.0 %vq_backward.1 = (bf16[288,768]{1,0:T(8,128)(2,1)}, bf16[1536,1024]{1,0:T(8,128)(2,1)}) custom-call(s32[5]{0:T(128)} %stack.110.refs_0_, bf16[288,768]{1,0:T(8,128)(2,1)} %get-tuple-element.171.refs_1_, bf16[1024,1536]{1,0:T(8,128)(2,1)} %get-tuple-element.175.refs_2_, bf16[288,768]{1,0:T(8,128)(2,1)} %get-tuple-element.188.refs_3_, ...), custom_call_target="tpu_custom_call" | custom-call | flops 17600000000 | bytes 7766036 | tf_op jit(solution)/shard_map/vq_backward/pallas_call | solution.py:232
  267.3 22.6 %qv_backward.1 = (bf16[768,1024]{1,0:T(8,128)(2,1)}, bf16[288,1536]{1,0:T(8,128)(2,1)}, bf16[1024,1536]{1,0:T(8,128)(2,1)}) custom-call(s32[5]{0:T(128)} %stack.110.refs_0_, bf16[1024,768]{1,0:T(8,128)(2,1)} %get-tuple-element.194.refs_1_, bf16[288,1536]{1,0:T(8,128)(2,1)} %get-tuple-element.195.refs_2_, bf16[1024,768]{1,0:T(8,128)(2,1)} %get-tuple-element.196.refs_3_, ...), custom_call_target="tpu_custom_call" | custom-call | flops 25300000768 | bytes 16449556 | tf_op jit(solution)/shard_map/qv_backward/pallas_call | solution.py:232
  299.6 20.2 %swin_backward.1 = (bf16[288,768]{1,0:T(8,128)(2,1)}, bf16[288,2304]{1,0:T(8,128)(2,1)}, f32[288,768]{1,0:T(8,128)}, f32[2,768]{1,0:T(2,128)}) custom-call(s32[5]{0:T(128)} %stack.110.refs_0_, bf16[288,768]{1,0:T(8,128)(2,1)} %reshape.163.refs_1_, f32[288,768]{1,0:T(8,128)} %get-tuple-element.159.refs_1_.refs_2_, f32[288,768]{1,0:T(8,128)} %get-tuple-element.202.refs_3_, ...), custom_call_target="tpu_custom_call" | custom-call | flops 22000001024 | bytes 15955988 | tf_op jit(solution)/shard_map/swin_backward/pallas_call | solution.py:232
  322.5 14.0 %patch_grads.1 = (bf16[2,16,96,768]{3,2,1,0:T(8,128)(2,1)}, bf16[2,16,96,768]{3,2,1,0:T(8,128)(2,1)}) custom-call(s32[5]{0:T(128)} %stack.110.refs_0_, bf16[288,768]{1,0:T(8,128)(2,1)} %get-tuple-element.165.refs_2_.refs_1_.refs_3_, bf16[288,768]{1,0:T(8,128)(2,1)} %get-tuple-element.190.refs_6_.refs_2_, ...), custom_call_target="tpu_custom_call" | custom-call | flops 14080000000 | bytes 18579456 | tf_op jit(solution)/shard_map/patch_grads/pallas_call | solution.py:855
  355.7 16.8 %self_backward.1 = (f32[128,768]{1,0:T(8,128)}, bf16[128,768]{1,0:T(8,128)(2,1)}, bf16[128,768]{1,0:T(8,128)(2,1)}, bf16[1536,1024]{1,0:T(8,128)(2,1)}, f32[128,...) custom-call(s32[5]{0:T(128)} %stack.110.refs_0_, bf16[128,768]{1,0:T(8,128)(2,1)} %get-tuple-element.338.refs_1_, ...), custom_call_target="tpu_custom_call" | custom-call | flops 16499999744 | bytes 14841876 | tf_op jit(solution)/shard_map/self_backward/pallas_call | solution.py:232
  372.7 9.7 %collective-permute-done.45 = bf16[8,96,768]{2,1,0:T(8,128)(2,1)} collective-permute-done((bf16[8,96,768]{2,1,0:T(8,128)(2,1)S(1)}, bf16[8,96,768]{2,1,0:T(8,128)(2,1)}, u32[]{:S(2)}, u32[]{:S(2)}) %collective-permute-start.45) | collective-permute-done | bytes 1179680 | tf_op jit(solution)/shard_map/ppermute | solution.py:893
  387.8 14.8 %slot_grads.1 = (bf16[2,16,96,768]{3,2,1,0:T(8,128)(2,1)}, bf16[2,16,96,768]{3,2,1,0:T(8,128)(2,1)}) custom-call(s32[5]{0:T(128)} %stack.110.refs_0_, bf16[1024,768]{1,0:T(8,128)(2,1)} %all-gather.6.cloned.1.call-done.refs_1_.refs_3_, bf16[768,1024]{1,0:T(8,128)(2,1)} %get-tuple-element.198.refs_2_, ...), custom_call_target="tpu_custom_call" | custom-call | flops 14080000000 | bytes 19808256 | tf_op jit(solution)/shard_map/slot_grads/pallas_call | solution.py:855
  435.6 10.1 %collective-permute-done.56 = bf16[2,96,768]{2,1,0:T(8,128)(2,1)S(1)} collective-permute-done((bf16[2,96,768]{2,1,0:T(8,128)(2,1)}, bf16[2,96,768]{2,1,0:T(8,128)(2,1)S(1)}, u32[]{:S(2)}, u32[]{:S(2)}) %collective-permute-start.56) | collective-permute-done | bytes 294944 | tf_op jit(solution)/shard_map/ppermute | solution.py:893
  445.7 10.0 %collective-permute-done.57 = bf16[2,96,768]{2,1,0:T(8,128)(2,1)S(1)} collective-permute-done((bf16[2,96,768]{2,1,0:T(8,128)(2,1)}, bf16[2,96,768]{2,1,0:T(8,128)(2,1)S(1)}, u32[]{:S(2)}, u32[]{:S(2)}) %collective-permute-start.57) | collective-permute-done | bytes 294944 | tf_op jit(solution)/shard_map/ppermute | solution.py:893
  472.6 10.8 %collective-permute-done.60 = bf16[4,96,768]{2,1,0:T(8,128)(2,1)S(1)} collective-permute-done((bf16[4,96,768]{2,1,0:T(8,128)(2,1)}, bf16[4,96,768]{2,1,0:T(8,128)(2,1)S(1)}, u32[]{:S(2)}, u32[]{:S(2)}) %collective-permute-start.60) | collective-permute-done | bytes 589856 | tf_op jit(solution)/shard_map/ppermute | solution.py:893
  499.5 17.0 %collective-permute-done.63 = bf16[2,104,768]{2,1,0:T(8,128)(2,1)S(1)} collective-permute-done((bf16[2,104,768]{2,1,0:T(8,128)(2,1)S(1)}, bf16[2,104,768]{2,1,0:T(8,128)(2,1)S(1)}, u32[]{:S(2)}, u32[]{:S(2)}) %collective-permute-start.63) | collective-permute-done | bytes 319520 | tf_op jit(solution)/shard_map/ppermute | solution.py:893
  (358 shorter events, 205.2 us)
Async XLA Ops:
  7.2 65.7 %all-gather.8.cloned.1.call-start = ((), (), s32[]{:S(2)}) async-start(), calls=%async_computation.5 | async-start | bytes 3760128 | tf_op jit(solution)/shard_map/all_gather | solution.py:1017
  9.8 164.3 %all-gather.6.cloned.1.call-start = ((), (), s32[]{:S(2)}) async-start(), calls=%async_computation.2 | async-start | bytes 1769472 | tf_op jit(solution)/shard_map/all_gather | solution.py:1103
  59.2 27.0 %collective-permute-start.9 = (bf16[8,96,768]{2,1,0:T(8,128)(2,1)}, bf16[8,96,768]{2,1,0:T(8,128)(2,1)}, u32[]{:S(2)}, u32[]{:S(2)}) collective-permute-start(bf16[8,96,768]{2,1,0:T(8,128)(2,1)} %constant_dynamic-update-slice_fusion.4.refs_3_.refs_17_), channel_id=1, source_target_pairs={{0,2},{1,3},{2,0},{3,1},{4,6},{5,7},{6,4},{7,5},{8,10},{9,11},{10,... | collective-permute-start | bytes 3538952 | tf_op jit(solution)/shard_map/ppermute | solution.py:893
  63.3 26.9 %collective-permute-start.8 = (bf16[8,96,768]{2,1,0:T(8,128)(2,1)}, bf16[8,96,768]{2,1,0:T(8,128)(2,1)}, u32[]{:S(2)}, u32[]{:S(2)}) collective-permute-start(bf16[8,96,768]{2,1,0:T(8,128)(2,1)} %constant_dynamic-update-slice_fusion.2.refs_2_.refs_8_), channel_id=1, source_target_pairs={{0,4},{1,5},{2,6},{3,7},{4,0},{5,1},{6,2},{7,3},{8,12},{9,13},{10,... | collective-permute-start | bytes 3538952 | tf_op jit(solution)/shard_map/ppermute | solution.py:893
  72.0 28.7 %collective-permute-start.21 = (bf16[8,96,768]{2,1,0:T(8,128)(2,1)}, bf16[8,96,768]{2,1,0:T(8,128)(2,1)}, u32[]{:S(2)}, u32[]{:S(2)}) collective-permute-start(bf16[8,96,768]{2,1,0:T(8,128)(2,1)} %constant_dynamic-update-slice_fusion.4.refs_3_.refs_17_), channel_id=1, source_target_pairs={{0,1},{1,0},{2,3},{3,2},{4,5},{5,4},{6,7},{7,6},{8,9},{9,8},{10,11... | collective-permute-start | bytes 3538952 | tf_op jit(solution)/shard_map/ppermute | solution.py:893
  106.7 31.5 %collective-permute-start.26 = (bf16[2,96,768]{2,1,0:T(8,128)(2,1)}, bf16[2,96,768]{2,1,0:T(8,128)(2,1)}, u32[]{:S(2)}, u32[]{:S(2)}) collective-permute-start(bf16[2,96,768]{2,1,0:T(8,128)(2,1)} %pad_maximum_fusion.13), channel_id=1, source_target_pairs={{0,16},{8,24},{16,0},{24,8},{1,17},{9,25},{17,1},{25,9},{2,18},{10... | collective-permute-start | bytes 884744 | tf_op jit(solution)/shard_map/ppermute | solution.py:893
  117.6 32.1 %collective-permute-start.16 = (bf16[8,96,768]{2,1,0:T(8,128)(2,1)S(1)}, bf16[8,96,768]{2,1,0:T(8,128)(2,1)}, u32[]{:S(2)}, u32[]{:S(2)}) collective-permute-start(bf16[8,96,768]{2,1,0:T(8,128)(2,1)S(1)} %constant_dynamic-update-slice_fusion.8.refs_7_.refs_5_.refs_11_.refs_13_), channel_id=1, source_target_pairs={{0,2},{1,3},{2,0},{3,1},{4,6},{5,7},{6,4},{7,5},{8,10},{9,11},{10,... | collective-permute-start | bytes 3538952 | tf_op jit(solution)/shard_map/ppermute | solution.py:893
  119.3 30.5 %collective-permute-start.18 = (bf16[8,96,768]{2,1,0:T(8,128)(2,1)S(1)}, bf16[8,96,768]{2,1,0:T(8,128)(2,1)}, u32[]{:S(2)}, u32[]{:S(2)}) collective-permute-start(bf16[8,96,768]{2,1,0:T(8,128)(2,1)S(1)} %constant_dynamic-update-slice_fusion.8.refs_7_.refs_5_.refs_11_.refs_13_), channel_id=1, source_target_pairs={{0,1},{1,0},{2,3},{3,2},{4,5},{5,4},{6,7},{7,6},{8,9},{9,8},{10,11... | collective-permute-start | bytes 3538952 | tf_op jit(solution)/shard_map/ppermute | solution.py:893
  120.4 30.2 %collective-permute-start.15 = (bf16[8,96,768]{2,1,0:T(8,128)(2,1)S(1)}, bf16[8,96,768]{2,1,0:T(8,128)(2,1)}, u32[]{:S(2)}, u32[]{:S(2)}) collective-permute-start(bf16[8,96,768]{2,1,0:T(8,128)(2,1)S(1)} %constant_dynamic-update-slice_fusion.6.refs_3_.refs_7_.refs_9_.refs_8_), channel_id=1, source_target_pairs={{0,4},{1,5},{2,6},{3,7},{4,0},{5,1},{6,2},{7,3},{8,12},{9,13},{10,... | collective-permute-start | bytes 3538952 | tf_op jit(solution)/shard_map/ppermute | solution.py:893
  121.5 29.2 %collective-permute-start.17 = (bf16[8,96,768]{2,1,0:T(8,128)(2,1)S(1)}, bf16[8,96,768]{2,1,0:T(8,128)(2,1)}, u32[]{:S(2)}, u32[]{:S(2)}) collective-permute-start(bf16[8,96,768]{2,1,0:T(8,128)(2,1)S(1)} %constant_dynamic-update-slice_fusion.6.refs_3_.refs_7_.refs_9_.refs_8_), channel_id=1, source_target_pairs={{0,1},{1,0},{2,3},{3,2},{4,5},{5,4},{6,7},{7,6},{8,9},{9,8},{10,11... | collective-permute-start | bytes 3538952 | tf_op jit(solution)/shard_map/ppermute | solution.py:893
  137.8 90.5 %all-gather.10.cloned.1.call-start = ((), (), s32[]{:S(2)}) async-start(), calls=%async_computation.6 | async-start | bytes 1769472 | tf_op jit(solution)/shard_map/all_gather | solution.py:1160
  170.9 27.0 %collective-permute-start.31 = (bf16[8,96,768]{2,1,0:T(8,128)(2,1)S(1)}, bf16[8,96,768]{2,1,0:T(8,128)(2,1)}, u32[]{:S(2)}, u32[]{:S(2)}) collective-permute-start(bf16[8,96,768]{2,1,0:T(8,128)(2,1)S(1)} %constant_dynamic-update-slice_fusion.12.refs_13_), channel_id=1, source_target_pairs={{0,2},{1,3},{2,0},{3,1},{4,6},{5,7},{6,4},{7,5},{8,10},{9,11},{10,... | collective-permute-start | bytes 3538952 | tf_op jit(solution)/shard_map/ppermute | solution.py:893
  196.2 151.0 %reduce-scatter.3.cloned.1.call-start = ((), (), s32[]{:S(2)}) async-start(), calls=%async_computation.3 | async-start | bytes 3538944 | tf_op jit(solution)/shard_map/reduce_scatter | solution.py:969
  265.2 32.3 %collective-permute-start.41 = (bf16[8,96,768]{2,1,0:T(8,128)(2,1)S(1)}, bf16[8,96,768]{2,1,0:T(8,128)(2,1)}, u32[]{:S(2)}, u32[]{:S(2)}) collective-permute-start(bf16[8,96,768]{2,1,0:T(8,128)(2,1)S(1)} %get-tuple-element.287), channel_id=1, source_target_pairs={{0,4},{1,5},{2,6},{3,7},{4,0},{5,1},{6,2},{7,3},{8,12},{9,13},{10,... | collective-permute-start | bytes 3538952 | tf_op jit(solution)/shard_map/ppermute | solution.py:893
  266.7 28.1 %collective-permute-start.40 = (bf16[8,96,768]{2,1,0:T(8,128)(2,1)}, bf16[8,96,768]{2,1,0:T(8,128)(2,1)}, u32[]{:S(2)}, u32[]{:S(2)}) collective-permute-start(bf16[8,96,768]{2,1,0:T(8,128)(2,1)} %get-tuple-element.288), channel_id=1, source_target_pairs={{0,2},{1,3},{2,0},{3,1},{4,6},{5,7},{6,4},{7,5},{8,10},{9,11},{10,... | collective-permute-start | bytes 3538952 | tf_op jit(solution)/shard_map/ppermute | solution.py:893
  289.9 179.6 %reduce-scatter.5.cloned.1.call-start = ((), (), s32[]{:S(2)}) async-start(), calls=%async_computation.4 | async-start | bytes 1990656 | tf_op jit(solution)/shard_map/reduce_scatter | solution.py:969
  339.6 32.8 %collective-permute-start.49 = (bf16[2,96,768]{2,1,0:T(8,128)(2,1)S(1)}, bf16[2,96,768]{2,1,0:T(8,128)(2,1)S(1)}, u32[]{:S(2)}, u32[]{:S(2)}) collective-permute-start(bf16[2,96,768]{2,1,0:T(8,128)(2,1)S(1)} %copy-done.19), channel_id=1, source_target_pairs={{0,24},{8,16},{16,8},{24,0},{1,25},{9,17},{17,9},{25,1},{2,26},{10... | collective-permute-start | bytes 884744 | tf_op jit(solution)/shard_map/ppermute | solution.py:893
  341.6 30.9 %collective-permute-start.48 = (bf16[2,96,768]{2,1,0:T(8,128)(2,1)}, bf16[2,96,768]{2,1,0:T(8,128)(2,1)S(1)}, u32[]{:S(2)}, u32[]{:S(2)}) collective-permute-start(bf16[2,96,768]{2,1,0:T(8,128)(2,1)} %pad_maximum_fusion.16), channel_id=1, source_target_pairs={{0,16},{8,24},{16,0},{24,8},{1,17},{9,25},{17,1},{25,9},{2,18},{10... | collective-permute-start | bytes 884744 | tf_op jit(solution)/shard_map/ppermute | solution.py:893
  353.4 29.0 %collective-permute-start.45 = (bf16[8,96,768]{2,1,0:T(8,128)(2,1)S(1)}, bf16[8,96,768]{2,1,0:T(8,128)(2,1)}, u32[]{:S(2)}, u32[]{:S(2)}) collective-permute-start(bf16[8,96,768]{2,1,0:T(8,128)(2,1)S(1)} %get-tuple-element.284), channel_id=1, source_target_pairs={{0,2},{1,3},{2,0},{3,1},{4,6},{5,7},{6,4},{7,5},{8,10},{9,11},{10,... | collective-permute-start | bytes 3538952 | tf_op jit(solution)/shard_map/ppermute | solution.py:893
  354.3 31.2 %collective-permute-start.46 = (bf16[8,96,768]{2,1,0:T(8,128)(2,1)S(1)}, bf16[8,96,768]{2,1,0:T(8,128)(2,1)}, u32[]{:S(2)}, u32[]{:S(2)}) collective-permute-start(bf16[8,96,768]{2,1,0:T(8,128)(2,1)S(1)} %get-tuple-element.283), channel_id=1, source_target_pairs={{0,4},{1,5},{2,6},{3,7},{4,0},{5,1},{6,2},{7,3},{8,12},{9,13},{10,... | collective-permute-start | bytes 3538952 | tf_op jit(solution)/shard_map/ppermute | solution.py:893
  372.5 30.2 %collective-permute-start.50 = (f32[6,24,768]{2,1,0:T(8,128)S(1)}, f32[6,24,768]{2,1,0:T(8,128)S(1)}, u32[]{:S(2)}, u32[]{:S(2)}) collective-permute-start(f32[6,24,768]{2,1,0:T(8,128)S(1)} %fusion.24), channel_id=1, source_target_pairs={{0,1},{1,2},{2,3},{3,4},{4,5},{5,6},{6,7},{7,0},{8,9},{9,10},{10,1... | collective-permute-start | bytes 1327112 | tf_op jit(solution)/shard_map/ppermute | solution.py:1188
  428.9 34.8 %collective-permute-start.55 = (bf16[8,96,768]{2,1,0:T(8,128)(2,1)}, bf16[8,96,768]{2,1,0:T(8,128)(2,1)}, u32[]{:S(2)}, u32[]{:S(2)}) collective-permute-start(bf16[8,96,768]{2,1,0:T(8,128)(2,1)} %get-tuple-element.246), channel_id=1, source_target_pairs={{0,4},{1,5},{2,6},{3,7},{4,0},{5,1},{6,2},{7,3},{8,12},{9,13},{10,... | collective-permute-start | bytes 3538952 | tf_op jit(solution)/shard_map/ppermute | solution.py:893
  429.2 36.8 %collective-permute-start.54 = (bf16[8,96,768]{2,1,0:T(8,128)(2,1)}, bf16[8,96,768]{2,1,0:T(8,128)(2,1)}, u32[]{:S(2)}, u32[]{:S(2)}) collective-permute-start(bf16[8,96,768]{2,1,0:T(8,128)(2,1)} %get-tuple-element.244), channel_id=1, source_target_pairs={{0,2},{1,3},{2,0},{3,1},{4,6},{5,7},{6,4},{7,5},{8,10},{9,11},{10,... | collective-permute-start | bytes 3538952 | tf_op jit(solution)/shard_map/ppermute | solution.py:893
  488.9 27.6 %collective-permute-start.63 = (bf16[2,104,768]{2,1,0:T(8,128)(2,1)S(1)}, bf16[2,104,768]{2,1,0:T(8,128)(2,1)S(1)}, u32[]{:S(2)}, u32[]{:S(2)}) collective-permute-start(bf16[2,104,768]{2,1,0:T(8,128)(2,1)S(1)} %fusion.31), channel_id=1, source_target_pairs={{0,16},{8,24},{16,0},{24,8},{1,17},{9,25},{17,1},{25,9},{2,18},{10... | collective-permute-start | bytes 958472 | tf_op jit(solution)/shard_map/ppermute | solution.py:893
  (75 other events, 966.0 us)
Sparse Core Ops, SparseCore 0:
  10.5 42.6 all-gather.7
  137.9 29.6 all-gather.5
  196.4 27.3 all-gather.9
  290.0 50.0 reduce-scatter.2
  407.5 47.5 reduce-scatter.4

commit v5 on v4

--- a/solution.py
+++ b/solution.py
@@ -776,7 +776,8 @@
     def body(*refs):
         where_ref = refs[0]
         ins = refs[1 : 1 + count]
-        *outs, held, sems = refs[1 + count :]
+        *outs, held, sems, flipped = refs[1 + count :]
+        turned = None
         keep, send = outs[0], outs[-1]
         page, blk = where_ref[3], where_ref[4]
 
@@ -831,7 +832,10 @@
             lhs = ins[left][:, left_at * D : (left_at + 1) * D]
             if form == "tt":
                 rhs = ins[right][right_at * D : (right_at + 1) * D, :]
-                product = nt(lhs.astype(f32).T.astype(bf16), rhs)
+                if turned != (left, left_at):
+                    turned = (left, left_at)
+                    flipped[...] = lhs.T
+                product = nt(flipped[...], rhs)
             else:
                 product = tn(lhs, ins[right][:, right_at * D : (right_at + 1) * D])
             held[slot] = product.astype(bf16)
@@ -851,6 +855,7 @@
     shapes = [sds((2, 16, rows, D), bf16)] * 2
     if shards:
         shapes = [sds((shards, len(weights) * 4 * D // shards, D), bf16)]
+    turned_rows = max([128] + [arrays[item[3]].shape[0] for item in items if item[7] == "tt"])
     moved = 2 * len(items) * D * D + sum(v.size * 2 for v in arrays)
     return pl.pallas_call(
         body,
@@ -861,7 +866,11 @@
             pl.BlockSpec(v.shape, lambda i: (0, 0), pipeline_mode=pl.Buffered(1)) for v in arrays
         ],
         out_specs=[pl.BlockSpec(memory_space=pl.ANY)] * len(shapes),
-        scratch_shapes=[pltpu.VMEM((2, D, D), bf16), pltpu.SemaphoreType.DMA((2,))],
+        scratch_shapes=[
+            pltpu.VMEM((2, D, D), bf16),
+            pltpu.SemaphoreType.DMA((2,)),
+            pltpu.VMEM((D, turned_rows), bf16),
+        ],
         compiler_params=pltpu.CompilerParams(
             vmem_limit_bytes=VMEM_LIMIT, dimension_semantics=("arbitrary",)
         ),
@@ -1009,6 +1018,14 @@
         ]
     ).astype(jnp.int32)
 
+    down_one = [(i, (i - 1) % blk_count) for i in range(blk_count)]
+    up_one = [(i, (i + 1) % blk_count) for i in range(blk_count)]
+    both = jnp.concatenate([visual, visual_cot], axis=0)
+    lent = lax.ppermute(both[:, :half], "blk", down_one)
+    both = jnp.concatenate([both[:, half:], lent], axis=1)
+    vis_in = window_order(both[0], half)
+    vis_cot = window_order(both[1], half)
+
     def flat_share(value):
         return value.astype(bf16).reshape(share, D)
 
@@ -1021,6 +1038,7 @@
     gains = gains.reshape(8, D).astype(f32)
     if staged:
         a_z = spread_first([flat_share(attn_self), flat_share(attn_swin)])
+        a_z = after(a_z, vis_in, vis_cot)
         a_near = spread_second(a_z)
         c_z = spread_first(after([flat_share(attn_qv), flat_share(attn_vq)], a_z))
         a_far = spread_third(a_near)
@@ -1059,16 +1077,6 @@
         ]
         up_all = joined[:, 5 * share : 6 * share].reshape(shards, 4, share // 4, D)
         w_up = Stored([up_all.transpose(1, 0, 2, 3).reshape(4, D, D)])
-
-    down_one = [(i, (i - 1) % blk_count) for i in range(blk_count)]
-    up_one = [(i, (i + 1) % blk_count) for i in range(blk_count)]
-    both = jnp.concatenate([visual, visual_cot], axis=0)
-    if staged:
-        both = after(both, a_near)
-    lent = lax.ppermute(both[:, :half], "blk", down_one)
-    both = jnp.concatenate([both[:, half:], lent], axis=1)
-    vis_in = window_order(both[0], half)
-    vis_cot = window_order(both[1], half)
 
     where_self = where_swin = where_cross = where_vq = where
     if staged:

time: 533 us -> 530 us (level)
  transfers between devices with their start and end apart: 70 -> 70, of which waited for: 32 -> 26; matrix products, arithmetic and copies ran while one was open for 12% -> 11% of each run, Pallas kernels for 35% -> 35%
where the time goes in v5:
time: 530 us; the launch traced here: 523 us
  Pallas kernels  195 us (37%)
  waiting for transfers between devices  155 us (29%)
  starting transfers between devices  77.6 us (15%)
  other arithmetic  46.6 us (9%)
  local copies, waits for them, and re-layouts  33 us (6%)
  between operations  15.9 us (3%)
    ppermute x62, waiting for transfers between devices, swapped(): return lax.ppermute(value, axis, [(i, i ^ flip) for i in range(count)])  155 us
    pallas_call x10, Pallas kernels, call(): pl.pallas_call(body, grid=(1,), out_shape=shapes, in_specs=specs + [pl.Bl...  155 us
    ppermute x62, starting transfers between devices, swapped(): return lax.ppermute(value, axis, [(i, i ^ flip) for i in range(count)])  74.4 us
    pallas_call x3, Pallas kernels, weight_grad_call(): pl.pallas_call(body, grid=(1,), out_shape=shapes, in_specs=[pl.BlockSpec(...  40.3 us
    convert_element_type x15, other arithmetic, added(): return (left.astype(f32) + right.astype(f32)).astype(bf16)  27.5 us
  transfers between devices with their start and end apart: 70, of which 26 were waited for; matrix products, arithmetic and copies ran while one was open for 11% of the time, Pallas kernels for 35%

profile of v5, /device:TPU:0, one launch (start us, length us, event | category | flops | bytes accessed | tf_op | source)
XLA Modules:
  0.0 522.9 jit_solution(3643696582797166573)
XLA Ops:
  17.5 8.4 %collective-permute-done = bf16[2,96,768]{2,1,0:T(8,128)(2,1)S(1)} collective-permute-done((bf16[2,96,768]{2,1,0:T(8,128)(2,1)S(1)}, bf16[2,96,768]{2,1,0:T(8,128)(2,1)S(1)}, u32[]{:S(2)}, u32[]{:S(2)}) %collective-permute-start) | collective-permute-done | bytes 294944 | tf_op jit(solution)/shard_map/ppermute | solution.py:902
  26.0 10.9 %collective-permute-done.1 = bf16[2,96,768]{2,1,0:T(8,128)(2,1)S(1)} collective-permute-done((bf16[2,96,768]{2,1,0:T(8,128)(2,1)S(1)}, bf16[2,96,768]{2,1,0:T(8,128)(2,1)S(1)}, u32[]{:S(2)}, u32[]{:S(2)}) %collective-permute-start.1) | collective-permute-done | bytes 294944 | tf_op jit(solution)/shard_map/ppermute | solution.py:902
  49.9 9.4 %collective-permute-done.7 = bf16[4,96,768]{2,1,0:T(8,128)(2,1)S(1)} collective-permute-done((bf16[4,96,768]{2,1,0:T(8,128)(2,1)S(1)}, bf16[4,96,768]{2,1,0:T(8,128)(2,1)S(1)}, u32[]{:S(2)}, u32[]{:S(2)}) %collective-permute-start.7) | collective-permute-done | bytes 589856 | tf_op jit(solution)/shard_map/ppermute | solution.py:902
  75.0 6.1 %collective-permute-start.11 = (bf16[1536]{0:T(1024)(128)(2,1)S(1)}, bf16[1536]{0:T(1024)(128)(2,1)S(1)}, u32[]{:S(2)}, u32[]{:S(2)}) collective-permute-start(bf16[1536]{0:T(1024)(128)(2,1)S(1)} %reshape_squeeze.24), channel_id=1, source_target_pairs={{0,8},{8,0},{16,24},{24,16},{1,9},{9,1},{17,25},{25,17},{2,10},{10... | collective-permute-start | bytes 9224 | tf_op jit(solution)/shard_map/ppermute | solution.py:902
  82.2 6.7 %collective-permute-done.10.refs_4_.refs_18_ = bf16[8,96,768]{2,1,0:T(8,128)(2,1)} collective-permute-done((bf16[8,96,768]{2,1,0:T(8,128)(2,1)}, bf16[8,96,768]{2,1,0:T(8,128)(2,1)}, u32[]{:S(2)}, u32[]{:S(2)}) %collective-permute-start.10) | collective-permute-done | bytes 1179680 | tf_op jit(solution)/shard_map/ppermute | solution.py:902
  105.8 8.1 %collective-permute-done.14 = bf16[4,96,768]{2,1,0:T(8,128)(2,1)S(1)} collective-permute-done((bf16[4,96,768]{2,1,0:T(8,128)(2,1)S(1)}, bf16[4,96,768]{2,1,0:T(8,128)(2,1)S(1)}, u32[]{:S(2)}, u32[]{:S(2)}) %collective-permute-start.14) | collective-permute-done | bytes 589856 | tf_op jit(solution)/shard_map/ppermute | solution.py:902
  119.2 16.1 %self_forward.1 = (bf16[1024,768]{1,0:T(8,128)(2,1)}, bf16[128,768]{1,0:T(8,128)(2,1)}, bf16[1024,1536]{1,0:T(8,128)(2,1)}, f32[128,128]{1,0:T(8,128)}, bf16[128...) custom-call(s32[5]{0:T(128)} %stack.110.refs_0_, ...), custom_call_target="tpu_custom_call" | custom-call | flops 16499999744 | bytes 10510356 | tf_op jit(solution)/shard_map/self_forward/pallas_call | solution.py:232
  139.7 7.2 %collective-permute-done.27 = bf16[2,96,768]{2,1,0:T(8,128)(2,1)S(1)} collective-permute-done((bf16[2,96,768]{2,1,0:T(8,128)(2,1)S(1)}, bf16[2,96,768]{2,1,0:T(8,128)(2,1)S(1)}, u32[]{:S(2)}, u32[]{:S(2)}) %collective-permute-start.27) | collective-permute-done | bytes 294944 | tf_op jit(solution)/shard_map/ppermute | solution.py:902
  149.7 11.6 %swin_forward.1 = (bf16[288,768]{1,0:T(8,128)(2,1)}, bf16[288,2304]{1,0:T(8,128)(2,1)}, f32[288,128]{1,0:T(8,128)}, bf16[288,768]{1,0:T(8,128)(2,1)}, f32[288,768]{1,0:T(8,128)}, /*index=5*/bf16[288,768]{1,0:T(8,128)(2,1)}) custom-call(s32[5]{0:T(128)} %stack.110.refs_0_, bf16[288,768]{1,0:T(8,128)(2,1)} %reshape.163.refs_1_, ...), custom_call_target="tpu_custom_call" | custom-call | flops 12099999744 | bytes 8871956 | tf_op jit(solution)/shard_map/swin_forward/pallas_call | solution.py:232
  173.3 21.1 %cross_forward.1 = (bf16[1024,768]{1,0:T(8,128)(2,1)}, bf16[1024,1536]{1,0:T(8,128)(2,1)}, bf16[1024,768]{1,0:T(8,128)(2,1)}, bf16[288,1536]{1,0:T(8,128)(2,1)},...) custom-call(s32[5]{0:T(128)} %stack.110.refs_0_, bf16[1024,768]{1,0:T(8,128)(2,1)} %all-gather.6.cloned.1.call-done.refs_1_.refs_3_, ...), custom_call_target="tpu_custom_call" | custom-call | flops 19800000512 | bytes 18087956 | tf_op jit(solution)/shard_map/cross_forward/pallas_call | solution.py:232
  198.3 11.7 %vq_forward.1 = (f32[288,128]{1,0:T(8,128)}, bf16[288,768]{1,0:T(8,128)(2,1)}) custom-call(s32[5]{0:T(128)} %stack.110.refs_0_, bf16[288,768]{1,0:T(8,128)(2,1)} %get-tuple-element.173.refs_1_, bf16[1024,1536]{1,0:T(8,128)(2,1)} %get-tuple-element.177.refs_2_), custom_call_target="tpu_custom_call" | custom-call | flops 12099999744 | bytes 4177940 | tf_op jit(solution)/shard_map/vq_forward/pallas_call | solution.py:232
  212.1 14.7 %mlp.1 = (bf16[288,768]{1,0:T(8,128)(2,1)}, bf16[288,768]{1,0:T(8,128)(2,1)}, bf16[288,3072]{1,0:T(8,128)(2,1)}, bf16[288,3072]{1,0:T(8,128)(2,1)}, f32[288,768]...) custom-call(s32[5]{0:T(128)} %stack.110.refs_0_, ...), custom_call_target="tpu_custom_call" | custom-call | flops 15399999488 | bytes 18607124 | tf_op jit(solution)/shard_map/mlp/pallas_call | solution.py:232
  230.2 11.6 %mlp_grads.1 = (bf16[2,16,96,768]{3,2,1,0:T(8,128)(2,1)}, bf16[2,16,96,768]{3,2,1,0:T(8,128)(2,1)}) custom-call(s32[5]{0:T(128)} %stack.110.refs_0_, bf16[288,768]{1,0:T(8,128)(2,1)} %get-tuple-element.182.refs_1_, bf16[288,3072]{1,0:T(8,128)(2,1)} %get-tuple-element.183.refs_2_, bf16[288,3072]{1,0:T(8,128)(2,1)} %get-tuple-element.184.refs_3_, ...), custom_call_target="tpu_custom_call" | custom-call | flops 14080000000 | bytes 13860864 | tf_op jit(solution)/shard_map/mlp_grads/pallas_call | solution.py:860
  243.0 16.0 %vq_backward.1 = (bf16[288,768]{1,0:T(8,128)(2,1)}, bf16[1536,1024]{1,0:T(8,128)(2,1)}) custom-call(s32[5]{0:T(128)} %stack.110.refs_0_, bf16[288,768]{1,0:T(8,128)(2,1)} %get-tuple-element.173.refs_1_, bf16[1024,1536]{1,0:T(8,128)(2,1)} %get-tuple-element.177.refs_2_, bf16[288,768]{1,0:T(8,128)(2,1)} %get-tuple-element.190.refs_3_, ...), custom_call_target="tpu_custom_call" | custom-call | flops 17600000000 | bytes 7766036 | tf_op jit(solution)/shard_map/vq_backward/pallas_call | solution.py:232
  265.8 22.6 %qv_backward.1 = (bf16[768,1024]{1,0:T(8,128)(2,1)}, bf16[288,1536]{1,0:T(8,128)(2,1)}, bf16[1024,1536]{1,0:T(8,128)(2,1)}) custom-call(s32[5]{0:T(128)} %stack.110.refs_0_, bf16[1024,768]{1,0:T(8,128)(2,1)} %get-tuple-element.196.refs_1_, bf16[288,1536]{1,0:T(8,128)(2,1)} %get-tuple-element.197.refs_2_, bf16[1024,768]{1,0:T(8,128)(2,1)} %get-tuple-element.198.refs_3_, ...), custom_call_target="tpu_custom_call" | custom-call | flops 25300000768 | bytes 16449556 | tf_op jit(solution)/shard_map/qv_backward/pallas_call | solution.py:232
  299.5 20.1 %swin_backward.1 = (bf16[288,768]{1,0:T(8,128)(2,1)}, bf16[288,2304]{1,0:T(8,128)(2,1)}, f32[288,768]{1,0:T(8,128)}, f32[2,768]{1,0:T(2,128)}) custom-call(s32[5]{0:T(128)} %stack.110.refs_0_, bf16[288,768]{1,0:T(8,128)(2,1)} %reshape.163.refs_1_, f32[288,768]{1,0:T(8,128)} %get-tuple-element.161.refs_1_.refs_2_, f32[288,768]{1,0:T(8,128)} %get-tuple-element.204.refs_3_, ...), custom_call_target="tpu_custom_call" | custom-call | flops 22000001024 | bytes 15955988 | tf_op jit(solution)/shard_map/swin_backward/pallas_call | solution.py:232
  322.3 14.0 %patch_grads.1 = (bf16[2,16,96,768]{3,2,1,0:T(8,128)(2,1)}, bf16[2,16,96,768]{3,2,1,0:T(8,128)(2,1)}) custom-call(s32[5]{0:T(128)} %stack.110.refs_0_, bf16[288,768]{1,0:T(8,128)(2,1)} %get-tuple-element.167.refs_2_.refs_1_.refs_3_, bf16[288,768]{1,0:T(8,128)(2,1)} %get-tuple-element.192.refs_6_.refs_2_, ...), custom_call_target="tpu_custom_call" | custom-call | flops 14080000000 | bytes 18579456 | tf_op jit(solution)/shard_map/patch_grads/pallas_call | solution.py:860
  353.2 16.8 %self_backward.1 = (f32[128,768]{1,0:T(8,128)}, bf16[128,768]{1,0:T(8,128)(2,1)}, bf16[128,768]{1,0:T(8,128)(2,1)}, bf16[1536,1024]{1,0:T(8,128)(2,1)}, f32[128,...) custom-call(s32[5]{0:T(128)} %stack.110.refs_0_, bf16[128,768]{1,0:T(8,128)(2,1)} %get-tuple-element.340.refs_1_, ...), custom_call_target="tpu_custom_call" | custom-call | flops 16499999744 | bytes 14841876 | tf_op jit(solution)/shard_map/self_backward/pallas_call | solution.py:232
  370.2 9.9 %collective-permute-done.45 = bf16[8,96,768]{2,1,0:T(8,128)(2,1)} collective-permute-done((bf16[8,96,768]{2,1,0:T(8,128)(2,1)S(1)}, bf16[8,96,768]{2,1,0:T(8,128)(2,1)}, u32[]{:S(2)}, u32[]{:S(2)}) %collective-permute-start.45) | collective-permute-done | bytes 1179680 | tf_op jit(solution)/shard_map/ppermute | solution.py:902
  387.2 14.8 %slot_grads.1 = (bf16[2,16,96,768]{3,2,1,0:T(8,128)(2,1)}, bf16[2,16,96,768]{3,2,1,0:T(8,128)(2,1)}) custom-call(s32[5]{0:T(128)} %stack.110.refs_0_, bf16[1024,768]{1,0:T(8,128)(2,1)} %all-gather.6.cloned.1.call-done.refs_1_.refs_3_, bf16[768,1024]{1,0:T(8,128)(2,1)} %get-tuple-element.200.refs_2_, ...), custom_call_target="tpu_custom_call" | custom-call | flops 14080000000 | bytes 19808256 | tf_op jit(solution)/shard_map/slot_grads/pallas_call | solution.py:860
  434.1 10.1 %collective-permute-done.56 = bf16[2,96,768]{2,1,0:T(8,128)(2,1)S(1)} collective-permute-done((bf16[2,96,768]{2,1,0:T(8,128)(2,1)}, bf16[2,96,768]{2,1,0:T(8,128)(2,1)S(1)}, u32[]{:S(2)}, u32[]{:S(2)}) %collective-permute-start.56) | collective-permute-done | bytes 294944 | tf_op jit(solution)/shard_map/ppermute | solution.py:902
  444.2 10.0 %collective-permute-done.57 = bf16[2,96,768]{2,1,0:T(8,128)(2,1)S(1)} collective-permute-done((bf16[2,96,768]{2,1,0:T(8,128)(2,1)}, bf16[2,96,768]{2,1,0:T(8,128)(2,1)S(1)}, u32[]{:S(2)}, u32[]{:S(2)}) %collective-permute-start.57) | collective-permute-done | bytes 294944 | tf_op jit(solution)/shard_map/ppermute | solution.py:902
  470.9 10.0 %collective-permute-done.60 = bf16[4,96,768]{2,1,0:T(8,128)(2,1)S(1)} collective-permute-done((bf16[4,96,768]{2,1,0:T(8,128)(2,1)}, bf16[4,96,768]{2,1,0:T(8,128)(2,1)S(1)}, u32[]{:S(2)}, u32[]{:S(2)}) %collective-permute-start.60) | collective-permute-done | bytes 589856 | tf_op jit(solution)/shard_map/ppermute | solution.py:902
  496.8 17.1 %collective-permute-done.63 = bf16[2,104,768]{2,1,0:T(8,128)(2,1)S(1)} collective-permute-done((bf16[2,104,768]{2,1,0:T(8,128)(2,1)S(1)}, bf16[2,104,768]{2,1,0:T(8,128)(2,1)S(1)}, u32[]{:S(2)}, u32[]{:S(2)}) %collective-permute-start.63) | collective-permute-done | bytes 319520 | tf_op jit(solution)/shard_map/ppermute | solution.py:902
  (365 shorter events, 201.8 us)
Async XLA Ops:
  7.2 66.9 %all-gather.8.cloned.1.call-start = ((), (), s32[]{:S(2)}) async-start(), calls=%async_computation.5 | async-start | bytes 3760128 | tf_op jit(solution)/shard_map/all_gather | solution.py:1034
  9.8 162.4 %all-gather.6.cloned.1.call-start = ((), (), s32[]{:S(2)}) async-start(), calls=%async_computation.2 | async-start | bytes 1769472 | tf_op jit(solution)/shard_map/all_gather | solution.py:1111
  61.9 27.1 %collective-permute-start.10 = (bf16[8,96,768]{2,1,0:T(8,128)(2,1)}, bf16[8,96,768]{2,1,0:T(8,128)(2,1)}, u32[]{:S(2)}, u32[]{:S(2)}) collective-permute-start(bf16[8,96,768]{2,1,0:T(8,128)(2,1)} %constant_dynamic-update-slice_fusion.6.refs_3_.refs_17_), channel_id=1, source_target_pairs={{0,2},{1,3},{2,0},{3,1},{4,6},{5,7},{6,4},{7,5},{8,10},{9,11},{10,... | collective-permute-start | bytes 3538952 | tf_op jit(solution)/shard_map/ppermute | solution.py:902
  64.2 26.7 %collective-permute-start.9 = (bf16[8,96,768]{2,1,0:T(8,128)(2,1)}, bf16[8,96,768]{2,1,0:T(8,128)(2,1)}, u32[]{:S(2)}, u32[]{:S(2)}) collective-permute-start(bf16[8,96,768]{2,1,0:T(8,128)(2,1)} %constant_dynamic-update-slice_fusion.4.refs_2_.refs_8_), channel_id=1, source_target_pairs={{0,4},{1,5},{2,6},{3,7},{4,0},{5,1},{6,2},{7,3},{8,12},{9,13},{10,... | collective-permute-start | bytes 3538952 | tf_op jit(solution)/shard_map/ppermute | solution.py:902
  68.2 30.7 %collective-permute-start.21 = (bf16[8,96,768]{2,1,0:T(8,128)(2,1)}, bf16[8,96,768]{2,1,0:T(8,128)(2,1)}, u32[]{:S(2)}, u32[]{:S(2)}) collective-permute-start(bf16[8,96,768]{2,1,0:T(8,128)(2,1)} %constant_dynamic-update-slice_fusion.6.refs_3_.refs_17_), channel_id=1, source_target_pairs={{0,1},{1,0},{2,3},{3,2},{4,5},{5,4},{6,7},{7,6},{8,9},{9,8},{10,11... | collective-permute-start | bytes 3538952 | tf_op jit(solution)/shard_map/ppermute | solution.py:902
  102.5 33.3 %collective-permute-start.26 = (bf16[2,96,768]{2,1,0:T(8,128)(2,1)S(1)}, bf16[2,96,768]{2,1,0:T(8,128)(2,1)}, u32[]{:S(2)}, u32[]{:S(2)}) collective-permute-start(bf16[2,96,768]{2,1,0:T(8,128)(2,1)S(1)} %pad_maximum_fusion.12), channel_id=1, source_target_pairs={{0,16},{8,24},{16,0},{24,8},{1,17},{9,25},{17,1},{25,9},{2,18},{10... | collective-permute-start | bytes 884744 | tf_op jit(solution)/shard_map/ppermute | solution.py:902
  116.0 31.1 %collective-permute-start.17 = (bf16[8,96,768]{2,1,0:T(8,128)(2,1)}, bf16[8,96,768]{2,1,0:T(8,128)(2,1)}, u32[]{:S(2)}, u32[]{:S(2)}) collective-permute-start(bf16[8,96,768]{2,1,0:T(8,128)(2,1)} %constant_dynamic-update-slice_fusion.10.refs_7_.refs_5_.refs_11_.refs_13_), channel_id=1, source_target_pairs={{0,2},{1,3},{2,0},{3,1},{4,6},{5,7},{6,4},{7,5},{8,10},{9,11},{10,... | collective-permute-start | bytes 3538952 | tf_op jit(solution)/shard_map/ppermute | solution.py:902
  117.4 29.7 %collective-permute-start.19 = (bf16[8,96,768]{2,1,0:T(8,128)(2,1)}, bf16[8,96,768]{2,1,0:T(8,128)(2,1)}, u32[]{:S(2)}, u32[]{:S(2)}) collective-permute-start(bf16[8,96,768]{2,1,0:T(8,128)(2,1)} %constant_dynamic-update-slice_fusion.10.refs_7_.refs_5_.refs_11_.refs_13_), channel_id=1, source_target_pairs={{0,1},{1,0},{2,3},{3,2},{4,5},{5,4},{6,7},{7,6},{8,9},{9,8},{10,11... | collective-permute-start | bytes 3538952 | tf_op jit(solution)/shard_map/ppermute | solution.py:902
  117.5 29.6 %collective-permute-start.16 = (bf16[8,96,768]{2,1,0:T(8,128)(2,1)S(1)}, bf16[8,96,768]{2,1,0:T(8,128)(2,1)S(1)}, u32[]{:S(2)}, u32[]{:S(2)}) collective-permute-start(bf16[8,96,768]{2,1,0:T(8,128)(2,1)S(1)} %constant_dynamic-update-slice_fusion.8.refs_3_.refs_7_.refs_9_.refs_8_), channel_id=1, source_target_pairs={{0,4},{1,5},{2,6},{3,7},{4,0},{5,1},{6,2},{7,3},{8,12},{9,13},{10,... | collective-permute-start | bytes 3538952 | tf_op jit(solution)/shard_map/ppermute | solution.py:902
  119.0 28.2 %collective-permute-start.18 = (bf16[8,96,768]{2,1,0:T(8,128)(2,1)S(1)}, bf16[8,96,768]{2,1,0:T(8,128)(2,1)}, u32[]{:S(2)}, u32[]{:S(2)}) collective-permute-start(bf16[8,96,768]{2,1,0:T(8,128)(2,1)S(1)} %constant_dynamic-update-slice_fusion.8.refs_3_.refs_7_.refs_9_.refs_8_), channel_id=1, source_target_pairs={{0,1},{1,0},{2,3},{3,2},{4,5},{5,4},{6,7},{7,6},{8,9},{9,8},{10,11... | collective-permute-start | bytes 3538952 | tf_op jit(solution)/shard_map/ppermute | solution.py:902
  135.4 91.5 %all-gather.10.cloned.1.call-start = ((), (), s32[]{:S(2)}) async-start(), calls=%async_computation.6 | async-start | bytes 1769472 | tf_op jit(solution)/shard_map/all_gather | solution.py:1168
  168.5 27.0 %collective-permute-start.31 = (bf16[8,96,768]{2,1,0:T(8,128)(2,1)S(1)}, bf16[8,96,768]{2,1,0:T(8,128)(2,1)}, u32[]{:S(2)}, u32[]{:S(2)}) collective-permute-start(bf16[8,96,768]{2,1,0:T(8,128)(2,1)S(1)} %constant_dynamic-update-slice_fusion.14.refs_13_), channel_id=1, source_target_pairs={{0,2},{1,3},{2,0},{3,1},{4,6},{5,7},{6,4},{7,5},{8,10},{9,11},{10,... | collective-permute-start | bytes 3538952 | tf_op jit(solution)/shard_map/ppermute | solution.py:902
  170.9 26.9 %collective-permute-start.30 = (bf16[8,96,768]{2,1,0:T(8,128)(2,1)}, bf16[8,96,768]{2,1,0:T(8,128)(2,1)}, u32[]{:S(2)}, u32[]{:S(2)}) collective-permute-start(bf16[8,96,768]{2,1,0:T(8,128)(2,1)} %constant_dynamic-update-slice_fusion.12.refs_9_), channel_id=1, source_target_pairs={{0,4},{1,5},{2,6},{3,7},{4,0},{5,1},{6,2},{7,3},{8,12},{9,13},{10,... | collective-permute-start | bytes 3538952 | tf_op jit(solution)/shard_map/ppermute | solution.py:902
  194.4 150.5 %reduce-scatter.3.cloned.1.call-start = ((), (), s32[]{:S(2)}) async-start(), calls=%async_computation.3 | async-start | bytes 3538944 | tf_op jit(solution)/shard_map/reduce_scatter | solution.py:978
  263.8 32.6 %collective-permute-start.41 = (bf16[8,96,768]{2,1,0:T(8,128)(2,1)S(1)}, bf16[8,96,768]{2,1,0:T(8,128)(2,1)}, u32[]{:S(2)}, u32[]{:S(2)}) collective-permute-start(bf16[8,96,768]{2,1,0:T(8,128)(2,1)S(1)} %get-tuple-element.289), channel_id=1, source_target_pairs={{0,4},{1,5},{2,6},{3,7},{4,0},{5,1},{6,2},{7,3},{8,12},{9,13},{10,... | collective-permute-start | bytes 3538952 | tf_op jit(solution)/shard_map/ppermute | solution.py:902
  265.1 28.2 %collective-permute-start.40 = (bf16[8,96,768]{2,1,0:T(8,128)(2,1)}, bf16[8,96,768]{2,1,0:T(8,128)(2,1)}, u32[]{:S(2)}, u32[]{:S(2)}) collective-permute-start(bf16[8,96,768]{2,1,0:T(8,128)(2,1)} %get-tuple-element.290), channel_id=1, source_target_pairs={{0,2},{1,3},{2,0},{3,1},{4,6},{5,7},{6,4},{7,5},{8,10},{9,11},{10,... | collective-permute-start | bytes 3538952 | tf_op jit(solution)/shard_map/ppermute | solution.py:902
  288.4 178.6 %reduce-scatter.5.cloned.1.call-start = ((), (), s32[]{:S(2)}) async-start(), calls=%async_computation.4 | async-start | bytes 1990656 | tf_op jit(solution)/shard_map/reduce_scatter | solution.py:978
  339.4 30.6 %collective-permute-start.49 = (bf16[2,96,768]{2,1,0:T(8,128)(2,1)S(1)}, bf16[2,96,768]{2,1,0:T(8,128)(2,1)S(1)}, u32[]{:S(2)}, u32[]{:S(2)}) collective-permute-start(bf16[2,96,768]{2,1,0:T(8,128)(2,1)S(1)} %copy-done.20), channel_id=1, source_target_pairs={{0,24},{8,16},{16,8},{24,0},{1,25},{9,17},{17,9},{25,1},{2,26},{10... | collective-permute-start | bytes 884744 | tf_op jit(solution)/shard_map/ppermute | solution.py:902
  342.4 27.7 %collective-permute-start.48 = (bf16[2,96,768]{2,1,0:T(8,128)(2,1)}, bf16[2,96,768]{2,1,0:T(8,128)(2,1)S(1)}, u32[]{:S(2)}, u32[]{:S(2)}) collective-permute-start(bf16[2,96,768]{2,1,0:T(8,128)(2,1)} %pad_maximum_fusion.15), channel_id=1, source_target_pairs={{0,16},{8,24},{16,0},{24,8},{1,17},{9,25},{17,1},{25,9},{2,18},{10... | collective-permute-start | bytes 884744 | tf_op jit(solution)/shard_map/ppermute | solution.py:902
  351.0 29.0 %collective-permute-start.45 = (bf16[8,96,768]{2,1,0:T(8,128)(2,1)S(1)}, bf16[8,96,768]{2,1,0:T(8,128)(2,1)}, u32[]{:S(2)}, u32[]{:S(2)}) collective-permute-start(bf16[8,96,768]{2,1,0:T(8,128)(2,1)S(1)} %get-tuple-element.286), channel_id=1, source_target_pairs={{0,2},{1,3},{2,0},{3,1},{4,6},{5,7},{6,4},{7,5},{8,10},{9,11},{10,... | collective-permute-start | bytes 3538952 | tf_op jit(solution)/shard_map/ppermute | solution.py:902
  352.5 32.4 %collective-permute-start.46 = (bf16[8,96,768]{2,1,0:T(8,128)(2,1)S(1)}, bf16[8,96,768]{2,1,0:T(8,128)(2,1)}, u32[]{:S(2)}, u32[]{:S(2)}) collective-permute-start(bf16[8,96,768]{2,1,0:T(8,128)(2,1)S(1)} %get-tuple-element.285), channel_id=1, source_target_pairs={{0,4},{1,5},{2,6},{3,7},{4,0},{5,1},{6,2},{7,3},{8,12},{9,13},{10,... | collective-permute-start | bytes 3538952 | tf_op jit(solution)/shard_map/ppermute | solution.py:902
  370.0 32.0 %collective-permute-start.50 = (f32[6,24,768]{2,1,0:T(8,128)S(1)}, f32[6,24,768]{2,1,0:T(8,128)S(1)}, u32[]{:S(2)}, u32[]{:S(2)}) collective-permute-start(f32[6,24,768]{2,1,0:T(8,128)S(1)} %fusion.24), channel_id=1, source_target_pairs={{0,1},{1,2},{2,3},{3,4},{4,5},{5,6},{6,7},{7,0},{8,9},{9,10},{10,1... | collective-permute-start | bytes 1327112 | tf_op jit(solution)/shard_map/ppermute | solution.py:1196
  426.3 34.8 %collective-permute-start.55 = (bf16[8,96,768]{2,1,0:T(8,128)(2,1)}, bf16[8,96,768]{2,1,0:T(8,128)(2,1)}, u32[]{:S(2)}, u32[]{:S(2)}) collective-permute-start(bf16[8,96,768]{2,1,0:T(8,128)(2,1)} %get-tuple-element.248), channel_id=1, source_target_pairs={{0,4},{1,5},{2,6},{3,7},{4,0},{5,1},{6,2},{7,3},{8,12},{9,13},{10,... | collective-permute-start | bytes 3538952 | tf_op jit(solution)/shard_map/ppermute | solution.py:902
  427.7 35.7 %collective-permute-start.54 = (bf16[8,96,768]{2,1,0:T(8,128)(2,1)}, bf16[8,96,768]{2,1,0:T(8,128)(2,1)}, u32[]{:S(2)}, u32[]{:S(2)}) collective-permute-start(bf16[8,96,768]{2,1,0:T(8,128)(2,1)} %get-tuple-element.246), channel_id=1, source_target_pairs={{0,2},{1,3},{2,0},{3,1},{4,6},{5,7},{6,4},{7,5},{8,10},{9,11},{10,... | collective-permute-start | bytes 3538952 | tf_op jit(solution)/shard_map/ppermute | solution.py:902
  (78 other events, 995.0 us)
Sparse Core Ops, SparseCore 0:
  10.5 43.7 all-gather.7
  135.5 30.0 all-gather.5
  194.5 27.9 all-gather.9
  288.5 49.2 reduce-scatter.2
  406.8 45.7 reduce-scatter.4

commit v6 on v5

--- a/solution.py
+++ b/solution.py
@@ -1193,8 +1193,9 @@
 
     def back_to_grid(value, *gate):
         grid = grid_order(value, rows_here, cols_all, half)
-        returned = lax.ppermute(grid[half:], "blk", up_one)
+        returned = lax.ppermute(grid[half:].astype(bf16), "blk", up_one)
         returned, grid = after((returned, grid), *gate)
+        returned = returned.astype(grid.dtype)
         return jnp.concatenate([returned, grid[:half]], axis=0)[None]
 
     def flat(value):

time: 530 us -> 526 us (level)
  transfers between devices with their start and end apart: 70 -> 70, of which waited for: 26 -> 25; matrix products, arithmetic and copies ran while one was open for 11% -> 11% of each run, Pallas kernels for 35% -> 35%
where the time goes in v6:
time: 526 us; the launch traced here: 519 us
  Pallas kernels  195 us (37%)
  waiting for transfers between devices  151 us (29%)
  starting transfers between devices  79.4 us (15%)
  other arithmetic  45.5 us (9%)
  local copies, waits for them, and re-layouts  32.6 us (6%)
  between operations  15.9 us (3%)
    pallas_call x10, Pallas kernels, call(): pl.pallas_call(body, grid=(1,), out_shape=shapes, in_specs=specs + [pl.Bl...  155 us
    ppermute x62, waiting for transfers between devices, swapped(): return lax.ppermute(value, axis, [(i, i ^ flip) for i in range(count)])  151 us
    ppermute x62, starting transfers between devices, swapped(): return lax.ppermute(value, axis, [(i, i ^ flip) for i in range(count)])  76.2 us
    pallas_call x3, Pallas kernels, weight_grad_call(): pl.pallas_call(body, grid=(1,), out_shape=shapes, in_specs=[pl.BlockSpec(...  40.3 us
    convert_element_type x15, other arithmetic, added(): return (left.astype(f32) + right.astype(f32)).astype(bf16)  27.5 us
  transfers between devices with their start and end apart: 70, of which 25 were waited for; matrix products, arithmetic and copies ran while one was open for 11% of the time, Pallas kernels for 35%

profile of v6, /device:TPU:0, one launch (start us, length us, event | category | flops | bytes accessed | tf_op | source)
XLA Modules:
  0.0 519.2 jit_solution(13907854083836491024)
XLA Ops:
  17.5 8.4 %collective-permute-done = bf16[2,96,768]{2,1,0:T(8,128)(2,1)S(1)} collective-permute-done((bf16[2,96,768]{2,1,0:T(8,128)(2,1)S(1)}, bf16[2,96,768]{2,1,0:T(8,128)(2,1)S(1)}, u32[]{:S(2)}, u32[]{:S(2)}) %collective-permute-start) | collective-permute-done | bytes 294944 | tf_op jit(solution)/shard_map/ppermute | solution.py:902
  26.0 10.9 %collective-permute-done.1 = bf16[2,96,768]{2,1,0:T(8,128)(2,1)S(1)} collective-permute-done((bf16[2,96,768]{2,1,0:T(8,128)(2,1)S(1)}, bf16[2,96,768]{2,1,0:T(8,128)(2,1)S(1)}, u32[]{:S(2)}, u32[]{:S(2)}) %collective-permute-start.1) | collective-permute-done | bytes 294944 | tf_op jit(solution)/shard_map/ppermute | solution.py:902
  49.9 9.4 %collective-permute-done.7 = bf16[4,96,768]{2,1,0:T(8,128)(2,1)S(1)} collective-permute-done((bf16[4,96,768]{2,1,0:T(8,128)(2,1)S(1)}, bf16[4,96,768]{2,1,0:T(8,128)(2,1)S(1)}, u32[]{:S(2)}, u32[]{:S(2)}) %collective-permute-start.7) | collective-permute-done | bytes 589856 | tf_op jit(solution)/shard_map/ppermute | solution.py:902
  75.0 6.1 %collective-permute-start.11 = (bf16[1536]{0:T(1024)(128)(2,1)S(1)}, bf16[1536]{0:T(1024)(128)(2,1)S(1)}, u32[]{:S(2)}, u32[]{:S(2)}) collective-permute-start(bf16[1536]{0:T(1024)(128)(2,1)S(1)} %reshape_squeeze.24), channel_id=1, source_target_pairs={{0,8},{8,0},{16,24},{24,16},{1,9},{9,1},{17,25},{25,17},{2,10},{10... | collective-permute-start | bytes 9224 | tf_op jit(solution)/shard_map/ppermute | solution.py:902
  82.2 6.7 %collective-permute-done.10.refs_4_.refs_18_ = bf16[8,96,768]{2,1,0:T(8,128)(2,1)} collective-permute-done((bf16[8,96,768]{2,1,0:T(8,128)(2,1)}, bf16[8,96,768]{2,1,0:T(8,128)(2,1)}, u32[]{:S(2)}, u32[]{:S(2)}) %collective-permute-start.10) | collective-permute-done | bytes 1179680 | tf_op jit(solution)/shard_map/ppermute | solution.py:902
  105.8 8.1 %collective-permute-done.14 = bf16[4,96,768]{2,1,0:T(8,128)(2,1)S(1)} collective-permute-done((bf16[4,96,768]{2,1,0:T(8,128)(2,1)S(1)}, bf16[4,96,768]{2,1,0:T(8,128)(2,1)S(1)}, u32[]{:S(2)}, u32[]{:S(2)}) %collective-permute-start.14) | collective-permute-done | bytes 589856 | tf_op jit(solution)/shard_map/ppermute | solution.py:902
  119.2 16.1 %self_forward.1 = (bf16[1024,768]{1,0:T(8,128)(2,1)}, bf16[128,768]{1,0:T(8,128)(2,1)}, bf16[1024,1536]{1,0:T(8,128)(2,1)}, f32[128,128]{1,0:T(8,128)}, bf16[128...) custom-call(s32[5]{0:T(128)} %stack.110.refs_0_, ...), custom_call_target="tpu_custom_call" | custom-call | flops 16499999744 | bytes 10510356 | tf_op jit(solution)/shard_map/self_forward/pallas_call | solution.py:232
  139.7 7.2 %collective-permute-done.27 = bf16[2,96,768]{2,1,0:T(8,128)(2,1)S(1)} collective-permute-done((bf16[2,96,768]{2,1,0:T(8,128)(2,1)S(1)}, bf16[2,96,768]{2,1,0:T(8,128)(2,1)S(1)}, u32[]{:S(2)}, u32[]{:S(2)}) %collective-permute-start.27) | collective-permute-done | bytes 294944 | tf_op jit(solution)/shard_map/ppermute | solution.py:902
  149.7 11.6 %swin_forward.1 = (bf16[288,768]{1,0:T(8,128)(2,1)}, bf16[288,2304]{1,0:T(8,128)(2,1)}, f32[288,128]{1,0:T(8,128)}, bf16[288,768]{1,0:T(8,128)(2,1)}, f32[288,768]{1,0:T(8,128)}, /*index=5*/bf16[288,768]{1,0:T(8,128)(2,1)}) custom-call(s32[5]{0:T(128)} %stack.110.refs_0_, bf16[288,768]{1,0:T(8,128)(2,1)} %reshape.163.refs_1_, ...), custom_call_target="tpu_custom_call" | custom-call | flops 12099999744 | bytes 8871956 | tf_op jit(solution)/shard_map/swin_forward/pallas_call | solution.py:232
  173.3 21.1 %cross_forward.1 = (bf16[1024,768]{1,0:T(8,128)(2,1)}, bf16[1024,1536]{1,0:T(8,128)(2,1)}, bf16[1024,768]{1,0:T(8,128)(2,1)}, bf16[288,1536]{1,0:T(8,128)(2,1)},...) custom-call(s32[5]{0:T(128)} %stack.110.refs_0_, bf16[1024,768]{1,0:T(8,128)(2,1)} %all-gather.6.cloned.1.call-done.refs_1_.refs_3_, ...), custom_call_target="tpu_custom_call" | custom-call | flops 19800000512 | bytes 18087956 | tf_op jit(solution)/shard_map/cross_forward/pallas_call | solution.py:232
  198.3 11.7 %vq_forward.1 = (f32[288,128]{1,0:T(8,128)}, bf16[288,768]{1,0:T(8,128)(2,1)}) custom-call(s32[5]{0:T(128)} %stack.110.refs_0_, bf16[288,768]{1,0:T(8,128)(2,1)} %get-tuple-element.173.refs_1_, bf16[1024,1536]{1,0:T(8,128)(2,1)} %get-tuple-element.177.refs_2_), custom_call_target="tpu_custom_call" | custom-call | flops 12099999744 | bytes 4177940 | tf_op jit(solution)/shard_map/vq_forward/pallas_call | solution.py:232
  212.1 14.7 %mlp.1 = (bf16[288,768]{1,0:T(8,128)(2,1)}, bf16[288,768]{1,0:T(8,128)(2,1)}, bf16[288,3072]{1,0:T(8,128)(2,1)}, bf16[288,3072]{1,0:T(8,128)(2,1)}, f32[288,768]...) custom-call(s32[5]{0:T(128)} %stack.110.refs_0_, ...), custom_call_target="tpu_custom_call" | custom-call | flops 15399999488 | bytes 18607124 | tf_op jit(solution)/shard_map/mlp/pallas_call | solution.py:232
  230.2 11.6 %mlp_grads.1 = (bf16[2,16,96,768]{3,2,1,0:T(8,128)(2,1)}, bf16[2,16,96,768]{3,2,1,0:T(8,128)(2,1)}) custom-call(s32[5]{0:T(128)} %stack.110.refs_0_, bf16[288,768]{1,0:T(8,128)(2,1)} %get-tuple-element.182.refs_1_, bf16[288,3072]{1,0:T(8,128)(2,1)} %get-tuple-element.183.refs_2_, bf16[288,3072]{1,0:T(8,128)(2,1)} %get-tuple-element.184.refs_3_, ...), custom_call_target="tpu_custom_call" | custom-call | flops 14080000000 | bytes 13860864 | tf_op jit(solution)/shard_map/mlp_grads/pallas_call | solution.py:860
  243.0 16.0 %vq_backward.1 = (bf16[288,768]{1,0:T(8,128)(2,1)}, bf16[1536,1024]{1,0:T(8,128)(2,1)}) custom-call(s32[5]{0:T(128)} %stack.110.refs_0_, bf16[288,768]{1,0:T(8,128)(2,1)} %get-tuple-element.173.refs_1_, bf16[1024,1536]{1,0:T(8,128)(2,1)} %get-tuple-element.177.refs_2_, bf16[288,768]{1,0:T(8,128)(2,1)} %get-tuple-element.190.refs_3_, ...), custom_call_target="tpu_custom_call" | custom-call | flops 17600000000 | bytes 7766036 | tf_op jit(solution)/shard_map/vq_backward/pallas_call | solution.py:232
  265.8 22.6 %qv_backward.1 = (bf16[768,1024]{1,0:T(8,128)(2,1)}, bf16[288,1536]{1,0:T(8,128)(2,1)}, bf16[1024,1536]{1,0:T(8,128)(2,1)}) custom-call(s32[5]{0:T(128)} %stack.110.refs_0_, bf16[1024,768]{1,0:T(8,128)(2,1)} %get-tuple-element.196.refs_1_, bf16[288,1536]{1,0:T(8,128)(2,1)} %get-tuple-element.197.refs_2_, bf16[1024,768]{1,0:T(8,128)(2,1)} %get-tuple-element.198.refs_3_, ...), custom_call_target="tpu_custom_call" | custom-call | flops 25300000768 | bytes 16449556 | tf_op jit(solution)/shard_map/qv_backward/pallas_call | solution.py:232
  299.5 20.1 %swin_backward.1 = (bf16[288,768]{1,0:T(8,128)(2,1)}, bf16[288,2304]{1,0:T(8,128)(2,1)}, f32[288,768]{1,0:T(8,128)}, f32[2,768]{1,0:T(2,128)}) custom-call(s32[5]{0:T(128)} %stack.110.refs_0_, bf16[288,768]{1,0:T(8,128)(2,1)} %reshape.163.refs_1_, f32[288,768]{1,0:T(8,128)} %get-tuple-element.161.refs_1_.refs_2_, f32[288,768]{1,0:T(8,128)} %get-tuple-element.204.refs_3_, ...), custom_call_target="tpu_custom_call" | custom-call | flops 22000001024 | bytes 15955988 | tf_op jit(solution)/shard_map/swin_backward/pallas_call | solution.py:232
  322.3 14.0 %patch_grads.1 = (bf16[2,16,96,768]{3,2,1,0:T(8,128)(2,1)}, bf16[2,16,96,768]{3,2,1,0:T(8,128)(2,1)}) custom-call(s32[5]{0:T(128)} %stack.110.refs_0_, bf16[288,768]{1,0:T(8,128)(2,1)} %get-tuple-element.167.refs_2_.refs_1_.refs_3_, bf16[288,768]{1,0:T(8,128)(2,1)} %get-tuple-element.192.refs_6_.refs_2_, ...), custom_call_target="tpu_custom_call" | custom-call | flops 14080000000 | bytes 18579456 | tf_op jit(solution)/shard_map/patch_grads/pallas_call | solution.py:860
  353.2 16.8 %self_backward.1 = (f32[128,768]{1,0:T(8,128)}, bf16[128,768]{1,0:T(8,128)(2,1)}, bf16[128,768]{1,0:T(8,128)(2,1)}, bf16[1536,1024]{1,0:T(8,128)(2,1)}, f32[128,...) custom-call(s32[5]{0:T(128)} %stack.110.refs_0_, bf16[128,768]{1,0:T(8,128)(2,1)} %get-tuple-element.340.refs_1_, ...), custom_call_target="tpu_custom_call" | custom-call | flops 16499999744 | bytes 14841876 | tf_op jit(solution)/shard_map/self_backward/pallas_call | solution.py:232
  370.3 9.9 %collective-permute-done.45 = bf16[8,96,768]{2,1,0:T(8,128)(2,1)} collective-permute-done((bf16[8,96,768]{2,1,0:T(8,128)(2,1)S(1)}, bf16[8,96,768]{2,1,0:T(8,128)(2,1)}, u32[]{:S(2)}, u32[]{:S(2)}) %collective-permute-start.45) | collective-permute-done | bytes 1179680 | tf_op jit(solution)/shard_map/ppermute | solution.py:902
  384.9 14.8 %slot_grads.1 = (bf16[2,16,96,768]{3,2,1,0:T(8,128)(2,1)}, bf16[2,16,96,768]{3,2,1,0:T(8,128)(2,1)}) custom-call(s32[5]{0:T(128)} %stack.110.refs_0_, bf16[1024,768]{1,0:T(8,128)(2,1)} %all-gather.6.cloned.1.call-done.refs_1_.refs_3_, bf16[768,1024]{1,0:T(8,128)(2,1)} %get-tuple-element.200.refs_2_, ...), custom_call_target="tpu_custom_call" | custom-call | flops 14080000000 | bytes 19808256 | tf_op jit(solution)/shard_map/slot_grads/pallas_call | solution.py:860
  430.8 10.1 %collective-permute-done.56 = bf16[2,96,768]{2,1,0:T(8,128)(2,1)S(1)} collective-permute-done((bf16[2,96,768]{2,1,0:T(8,128)(2,1)}, bf16[2,96,768]{2,1,0:T(8,128)(2,1)S(1)}, u32[]{:S(2)}, u32[]{:S(2)}) %collective-permute-start.56) | collective-permute-done | bytes 294944 | tf_op jit(solution)/shard_map/ppermute | solution.py:902
  440.9 10.0 %collective-permute-done.57 = bf16[2,96,768]{2,1,0:T(8,128)(2,1)S(1)} collective-permute-done((bf16[2,96,768]{2,1,0:T(8,128)(2,1)}, bf16[2,96,768]{2,1,0:T(8,128)(2,1)S(1)}, u32[]{:S(2)}, u32[]{:S(2)}) %collective-permute-start.57) | collective-permute-done | bytes 294944 | tf_op jit(solution)/shard_map/ppermute | solution.py:902
  467.1 9.3 %collective-permute-done.60 = bf16[4,96,768]{2,1,0:T(8,128)(2,1)S(1)} collective-permute-done((bf16[4,96,768]{2,1,0:T(8,128)(2,1)}, bf16[4,96,768]{2,1,0:T(8,128)(2,1)S(1)}, u32[]{:S(2)}, u32[]{:S(2)}) %collective-permute-start.60) | collective-permute-done | bytes 589856 | tf_op jit(solution)/shard_map/ppermute | solution.py:902
  492.8 17.4 %collective-permute-done.63 = bf16[2,104,768]{2,1,0:T(8,128)(2,1)S(1)} collective-permute-done((bf16[2,104,768]{2,1,0:T(8,128)(2,1)S(1)}, bf16[2,104,768]{2,1,0:T(8,128)(2,1)S(1)}, u32[]{:S(2)}, u32[]{:S(2)}) %collective-permute-start.63) | collective-permute-done | bytes 319520 | tf_op jit(solution)/shard_map/ppermute | solution.py:902
  (366 shorter events, 198.6 us)
Async XLA Ops:
  7.2 66.9 %all-gather.8.cloned.1.call-start = ((), (), s32[]{:S(2)}) async-start(), calls=%async_computation.5 | async-start | bytes 3760128 | tf_op jit(solution)/shard_map/all_gather | solution.py:1034
  9.8 162.4 %all-gather.6.cloned.1.call-start = ((), (), s32[]{:S(2)}) async-start(), calls=%async_computation.2 | async-start | bytes 1769472 | tf_op jit(solution)/shard_map/all_gather | solution.py:1111
  61.9 27.1 %collective-permute-start.10 = (bf16[8,96,768]{2,1,0:T(8,128)(2,1)}, bf16[8,96,768]{2,1,0:T(8,128)(2,1)}, u32[]{:S(2)}, u32[]{:S(2)}) collective-permute-start(bf16[8,96,768]{2,1,0:T(8,128)(2,1)} %constant_dynamic-update-slice_fusion.6.refs_3_.refs_17_), channel_id=1, source_target_pairs={{0,2},{1,3},{2,0},{3,1},{4,6},{5,7},{6,4},{7,5},{8,10},{9,11},{10,... | collective-permute-start | bytes 3538952 | tf_op jit(solution)/shard_map/ppermute | solution.py:902
  68.2 30.7 %collective-permute-start.21 = (bf16[8,96,768]{2,1,0:T(8,128)(2,1)}, bf16[8,96,768]{2,1,0:T(8,128)(2,1)}, u32[]{:S(2)}, u32[]{:S(2)}) collective-permute-start(bf16[8,96,768]{2,1,0:T(8,128)(2,1)} %constant_dynamic-update-slice_fusion.6.refs_3_.refs_17_), channel_id=1, source_target_pairs={{0,1},{1,0},{2,3},{3,2},{4,5},{5,4},{6,7},{7,6},{8,9},{9,8},{10,11... | collective-permute-start | bytes 3538952 | tf_op jit(solution)/shard_map/ppermute | solution.py:902
  102.5 33.3 %collective-permute-start.26 = (bf16[2,96,768]{2,1,0:T(8,128)(2,1)S(1)}, bf16[2,96,768]{2,1,0:T(8,128)(2,1)}, u32[]{:S(2)}, u32[]{:S(2)}) collective-permute-start(bf16[2,96,768]{2,1,0:T(8,128)(2,1)S(1)} %pad_maximum_fusion.12), channel_id=1, source_target_pairs={{0,16},{8,24},{16,0},{24,8},{1,17},{9,25},{17,1},{25,9},{2,18},{10... | collective-permute-start | bytes 884744 | tf_op jit(solution)/shard_map/ppermute | solution.py:902
  116.0 31.1 %collective-permute-start.17 = (bf16[8,96,768]{2,1,0:T(8,128)(2,1)}, bf16[8,96,768]{2,1,0:T(8,128)(2,1)}, u32[]{:S(2)}, u32[]{:S(2)}) collective-permute-start(bf16[8,96,768]{2,1,0:T(8,128)(2,1)} %constant_dynamic-update-slice_fusion.10.refs_7_.refs_5_.refs_11_.refs_13_), channel_id=1, source_target_pairs={{0,2},{1,3},{2,0},{3,1},{4,6},{5,7},{6,4},{7,5},{8,10},{9,11},{10,... | collective-permute-start | bytes 3538952 | tf_op jit(solution)/shard_map/ppermute | solution.py:902
  117.4 29.7 %collective-permute-start.19 = (bf16[8,96,768]{2,1,0:T(8,128)(2,1)}, bf16[8,96,768]{2,1,0:T(8,128)(2,1)}, u32[]{:S(2)}, u32[]{:S(2)}) collective-permute-start(bf16[8,96,768]{2,1,0:T(8,128)(2,1)} %constant_dynamic-update-slice_fusion.10.refs_7_.refs_5_.refs_11_.refs_13_), channel_id=1, source_target_pairs={{0,1},{1,0},{2,3},{3,2},{4,5},{5,4},{6,7},{7,6},{8,9},{9,8},{10,11... | collective-permute-start | bytes 3538952 | tf_op jit(solution)/shard_map/ppermute | solution.py:902
  117.5 29.6 %collective-permute-start.16 = (bf16[8,96,768]{2,1,0:T(8,128)(2,1)S(1)}, bf16[8,96,768]{2,1,0:T(8,128)(2,1)S(1)}, u32[]{:S(2)}, u32[]{:S(2)}) collective-permute-start(bf16[8,96,768]{2,1,0:T(8,128)(2,1)S(1)} %constant_dynamic-update-slice_fusion.8.refs_3_.refs_7_.refs_9_.refs_8_), channel_id=1, source_target_pairs={{0,4},{1,5},{2,6},{3,7},{4,0},{5,1},{6,2},{7,3},{8,12},{9,13},{10,... | collective-permute-start | bytes 3538952 | tf_op jit(solution)/shard_map/ppermute | solution.py:902
  119.0 28.2 %collective-permute-start.18 = (bf16[8,96,768]{2,1,0:T(8,128)(2,1)S(1)}, bf16[8,96,768]{2,1,0:T(8,128)(2,1)}, u32[]{:S(2)}, u32[]{:S(2)}) collective-permute-start(bf16[8,96,768]{2,1,0:T(8,128)(2,1)S(1)} %constant_dynamic-update-slice_fusion.8.refs_3_.refs_7_.refs_9_.refs_8_), channel_id=1, source_target_pairs={{0,1},{1,0},{2,3},{3,2},{4,5},{5,4},{6,7},{7,6},{8,9},{9,8},{10,11... | collective-permute-start | bytes 3538952 | tf_op jit(solution)/shard_map/ppermute | solution.py:902
  135.4 91.5 %all-gather.10.cloned.1.call-start = ((), (), s32[]{:S(2)}) async-start(), calls=%async_computation.6 | async-start | bytes 1769472 | tf_op jit(solution)/shard_map/all_gather | solution.py:1168
  168.5 27.0 %collective-permute-start.31 = (bf16[8,96,768]{2,1,0:T(8,128)(2,1)S(1)}, bf16[8,96,768]{2,1,0:T(8,128)(2,1)}, u32[]{:S(2)}, u32[]{:S(2)}) collective-permute-start(bf16[8,96,768]{2,1,0:T(8,128)(2,1)S(1)} %constant_dynamic-update-slice_fusion.14.refs_13_), channel_id=1, source_target_pairs={{0,2},{1,3},{2,0},{3,1},{4,6},{5,7},{6,4},{7,5},{8,10},{9,11},{10,... | collective-permute-start | bytes 3538952 | tf_op jit(solution)/shard_map/ppermute | solution.py:902
  170.9 26.9 %collective-permute-start.30 = (bf16[8,96,768]{2,1,0:T(8,128)(2,1)}, bf16[8,96,768]{2,1,0:T(8,128)(2,1)}, u32[]{:S(2)}, u32[]{:S(2)}) collective-permute-start(bf16[8,96,768]{2,1,0:T(8,128)(2,1)} %constant_dynamic-update-slice_fusion.12.refs_9_), channel_id=1, source_target_pairs={{0,4},{1,5},{2,6},{3,7},{4,0},{5,1},{6,2},{7,3},{8,12},{9,13},{10,... | collective-permute-start | bytes 3538952 | tf_op jit(solution)/shard_map/ppermute | solution.py:902
  194.4 150.5 %reduce-scatter.3.cloned.1.call-start = ((), (), s32[]{:S(2)}) async-start(), calls=%async_computation.3 | async-start | bytes 3538944 | tf_op jit(solution)/shard_map/reduce_scatter | solution.py:978
  263.8 32.6 %collective-permute-start.41 = (bf16[8,96,768]{2,1,0:T(8,128)(2,1)S(1)}, bf16[8,96,768]{2,1,0:T(8,128)(2,1)}, u32[]{:S(2)}, u32[]{:S(2)}) collective-permute-start(bf16[8,96,768]{2,1,0:T(8,128)(2,1)S(1)} %get-tuple-element.289), channel_id=1, source_target_pairs={{0,4},{1,5},{2,6},{3,7},{4,0},{5,1},{6,2},{7,3},{8,12},{9,13},{10,... | collective-permute-start | bytes 3538952 | tf_op jit(solution)/shard_map/ppermute | solution.py:902
  265.1 28.2 %collective-permute-start.40 = (bf16[8,96,768]{2,1,0:T(8,128)(2,1)}, bf16[8,96,768]{2,1,0:T(8,128)(2,1)}, u32[]{:S(2)}, u32[]{:S(2)}) collective-permute-start(bf16[8,96,768]{2,1,0:T(8,128)(2,1)} %get-tuple-element.290), channel_id=1, source_target_pairs={{0,2},{1,3},{2,0},{3,1},{4,6},{5,7},{6,4},{7,5},{8,10},{9,11},{10,... | collective-permute-start | bytes 3538952 | tf_op jit(solution)/shard_map/ppermute | solution.py:902
  288.4 174.9 %reduce-scatter.5.cloned.1.call-start = ((), (), s32[]{:S(2)}) async-start(), calls=%async_computation.4 | async-start | bytes 1990656 | tf_op jit(solution)/shard_map/reduce_scatter | solution.py:978
  339.4 30.6 %collective-permute-start.49 = (bf16[2,96,768]{2,1,0:T(8,128)(2,1)S(1)}, bf16[2,96,768]{2,1,0:T(8,128)(2,1)S(1)}, u32[]{:S(2)}, u32[]{:S(2)}) collective-permute-start(bf16[2,96,768]{2,1,0:T(8,128)(2,1)S(1)} %copy-done.20), channel_id=1, source_target_pairs={{0,24},{8,16},{16,8},{24,0},{1,25},{9,17},{17,9},{25,1},{2,26},{10... | collective-permute-start | bytes 884744 | tf_op jit(solution)/shard_map/ppermute | solution.py:902
  342.4 27.7 %collective-permute-start.48 = (bf16[2,96,768]{2,1,0:T(8,128)(2,1)S(1)}, bf16[2,96,768]{2,1,0:T(8,128)(2,1)S(1)}, u32[]{:S(2)}, u32[]{:S(2)}) collective-permute-start(bf16[2,96,768]{2,1,0:T(8,128)(2,1)S(1)} %copy-done.19), channel_id=1, source_target_pairs={{0,16},{8,24},{16,0},{24,8},{1,17},{9,25},{17,1},{25,9},{2,18},{10... | collective-permute-start | bytes 884744 | tf_op jit(solution)/shard_map/ppermute | solution.py:902
  351.1 29.0 %collective-permute-start.45 = (bf16[8,96,768]{2,1,0:T(8,128)(2,1)S(1)}, bf16[8,96,768]{2,1,0:T(8,128)(2,1)}, u32[]{:S(2)}, u32[]{:S(2)}) collective-permute-start(bf16[8,96,768]{2,1,0:T(8,128)(2,1)S(1)} %get-tuple-element.286), channel_id=1, source_target_pairs={{0,2},{1,3},{2,0},{3,1},{4,6},{5,7},{6,4},{7,5},{8,10},{9,11},{10,... | collective-permute-start | bytes 3538952 | tf_op jit(solution)/shard_map/ppermute | solution.py:902
  352.5 30.0 %collective-permute-start.46 = (bf16[8,96,768]{2,1,0:T(8,128)(2,1)S(1)}, bf16[8,96,768]{2,1,0:T(8,128)(2,1)}, u32[]{:S(2)}, u32[]{:S(2)}) collective-permute-start(bf16[8,96,768]{2,1,0:T(8,128)(2,1)S(1)} %get-tuple-element.285), channel_id=1, source_target_pairs={{0,4},{1,5},{2,6},{3,7},{4,0},{5,1},{6,2},{7,3},{8,12},{9,13},{10,... | collective-permute-start | bytes 3538952 | tf_op jit(solution)/shard_map/ppermute | solution.py:902
  370.0 29.6 %collective-permute-start.50 = (bf16[6,24,768]{2,1,0:T(8,128)(2,1)S(1)}, bf16[6,24,768]{2,1,0:T(8,128)(2,1)S(1)}, u32[]{:S(2)}, u32[]{:S(2)}) collective-permute-start(bf16[6,24,768]{2,1,0:T(8,128)(2,1)S(1)} %fusion.25), channel_id=1, source_target_pairs={{0,1},{1,2},{2,3},{3,4},{4,5},{5,6},{6,7},{7,0},{8,9},{9,10},{10,1... | collective-permute-start | bytes 663560 | tf_op jit(solution)/shard_map/ppermute | solution.py:1196
  422.7 34.3 %collective-permute-start.55 = (bf16[8,96,768]{2,1,0:T(8,128)(2,1)}, bf16[8,96,768]{2,1,0:T(8,128)(2,1)}, u32[]{:S(2)}, u32[]{:S(2)}) collective-permute-start(bf16[8,96,768]{2,1,0:T(8,128)(2,1)} %get-tuple-element.248), channel_id=1, source_target_pairs={{0,4},{1,5},{2,6},{3,7},{4,0},{5,1},{6,2},{7,3},{8,12},{9,13},{10,... | collective-permute-start | bytes 3538952 | tf_op jit(solution)/shard_map/ppermute | solution.py:902
  423.6 35.8 %collective-permute-start.54 = (bf16[8,96,768]{2,1,0:T(8,128)(2,1)}, bf16[8,96,768]{2,1,0:T(8,128)(2,1)}, u32[]{:S(2)}, u32[]{:S(2)}) collective-permute-start(bf16[8,96,768]{2,1,0:T(8,128)(2,1)} %get-tuple-element.246), channel_id=1, source_target_pairs={{0,2},{1,3},{2,0},{3,1},{4,6},{5,7},{6,4},{7,5},{8,10},{9,11},{10,... | collective-permute-start | bytes 3538952 | tf_op jit(solution)/shard_map/ppermute | solution.py:902
  481.9 28.3 %collective-permute-start.63 = (bf16[2,104,768]{2,1,0:T(8,128)(2,1)S(1)}, bf16[2,104,768]{2,1,0:T(8,128)(2,1)S(1)}, u32[]{:S(2)}, u32[]{:S(2)}) collective-permute-start(bf16[2,104,768]{2,1,0:T(8,128)(2,1)S(1)} %fusion.32), channel_id=1, source_target_pairs={{0,16},{8,24},{16,0},{24,8},{1,17},{9,25},{17,1},{25,9},{2,18},{10... | collective-permute-start | bytes 958472 | tf_op jit(solution)/shard_map/ppermute | solution.py:902
  (78 other events, 992.9 us)
Sparse Core Ops, SparseCore 0:
  10.5 43.7 all-gather.7
  135.5 30.0 all-gather.5
  194.5 27.9 all-gather.9
  288.5 49.2 reduce-scatter.2
  403.0 46.1 reduce-scatter.4

commit v7 on v6

--- a/solution.py
+++ b/solution.py
@@ -1343,9 +1343,9 @@
     )
     gain_block = gain_block.astype(bf16).reshape(pages, blk_count, gain_width).transpose(1, 0, 2)
     gain_block = gain_block.reshape(blk_count, 1, pages * gain_width)
-    gain_block = jnp.pad(gain_block, ((0, 0), (0, 15), (0, D - pages * gain_width)))
+    gain_block = jnp.pad(gain_block, ((0, 0), (0, 7), (0, D - pages * gain_width)))
     whole_part = jnp.concatenate([db_part.reshape(blk_count, q_rows, D), gain_block], axis=1)
-    db_all = scattered_blocks(whole_part.reshape(blk_count * (q_rows + 16), D))
+    db_all = scattered_blocks(whole_part.reshape(blk_count * (q_rows + 8), D))
     where_end = where
     if staged:
         p_two = collect_second(p_one, gy1)

time: 526 us -> 526 us (level)
  no operation moved by 1% of the time
where the time goes in v7:
time: 526 us; the launch traced here: 519 us
  Pallas kernels  195 us (37%)
  waiting for transfers between devices  150 us (29%)
  starting transfers between devices  79.4 us (15%)
  other arithmetic  45.5 us (9%)
  local copies, waits for them, and re-layouts  32.6 us (6%)
  between operations  15.9 us (3%)
    pallas_call x10, Pallas kernels, call(): pl.pallas_call(body, grid=(1,), out_shape=shapes, in_specs=specs + [pl.Bl...  155 us
    ppermute x62, waiting for transfers between devices, swapped(): return lax.ppermute(value, axis, [(i, i ^ flip) for i in range(count)])  150 us
    ppermute x62, starting transfers between devices, swapped(): return lax.ppermute(value, axis, [(i, i ^ flip) for i in range(count)])  76.2 us
    pallas_call x3, Pallas kernels, weight_grad_call(): pl.pallas_call(body, grid=(1,), out_shape=shapes, in_specs=[pl.BlockSpec(...  40.3 us
    convert_element_type x15, other arithmetic, added(): return (left.astype(f32) + right.astype(f32)).astype(bf16)  27.5 us
  transfers between devices with their start and end apart: 70, of which 25 were waited for; matrix products, arithmetic and copies ran while one was open for 11% of the time, Pallas kernels for 35%

profile of v7, /device:TPU:0, one launch (start us, length us, event | category | flops | bytes accessed | tf_op | source)
XLA Modules:
  0.0 518.5 jit_solution(12760520378966164918)
XLA Ops:
  17.5 8.4 %collective-permute-done = bf16[2,96,768]{2,1,0:T(8,128)(2,1)S(1)} collective-permute-done((bf16[2,96,768]{2,1,0:T(8,128)(2,1)S(1)}, bf16[2,96,768]{2,1,0:T(8,128)(2,1)S(1)}, u32[]{:S(2)}, u32[]{:S(2)}) %collective-permute-start) | collective-permute-done | bytes 294944 | tf_op jit(solution)/shard_map/ppermute | solution.py:902
  26.0 10.9 %collective-permute-done.1 = bf16[2,96,768]{2,1,0:T(8,128)(2,1)S(1)} collective-permute-done((bf16[2,96,768]{2,1,0:T(8,128)(2,1)S(1)}, bf16[2,96,768]{2,1,0:T(8,128)(2,1)S(1)}, u32[]{:S(2)}, u32[]{:S(2)}) %collective-permute-start.1) | collective-permute-done | bytes 294944 | tf_op jit(solution)/shard_map/ppermute | solution.py:902
  49.9 9.4 %collective-permute-done.7 = bf16[4,96,768]{2,1,0:T(8,128)(2,1)S(1)} collective-permute-done((bf16[4,96,768]{2,1,0:T(8,128)(2,1)S(1)}, bf16[4,96,768]{2,1,0:T(8,128)(2,1)S(1)}, u32[]{:S(2)}, u32[]{:S(2)}) %collective-permute-start.7) | collective-permute-done | bytes 589856 | tf_op jit(solution)/shard_map/ppermute | solution.py:902
  75.0 6.1 %collective-permute-start.11 = (bf16[1536]{0:T(1024)(128)(2,1)S(1)}, bf16[1536]{0:T(1024)(128)(2,1)S(1)}, u32[]{:S(2)}, u32[]{:S(2)}) collective-permute-start(bf16[1536]{0:T(1024)(128)(2,1)S(1)} %reshape_squeeze.24), channel_id=1, source_target_pairs={{0,8},{8,0},{16,24},{24,16},{1,9},{9,1},{17,25},{25,17},{2,10},{10... | collective-permute-start | bytes 9224 | tf_op jit(solution)/shard_map/ppermute | solution.py:902
  82.2 6.7 %collective-permute-done.10.refs_4_.refs_18_ = bf16[8,96,768]{2,1,0:T(8,128)(2,1)} collective-permute-done((bf16[8,96,768]{2,1,0:T(8,128)(2,1)}, bf16[8,96,768]{2,1,0:T(8,128)(2,1)}, u32[]{:S(2)}, u32[]{:S(2)}) %collective-permute-start.10) | collective-permute-done | bytes 1179680 | tf_op jit(solution)/shard_map/ppermute | solution.py:902
  105.8 8.1 %collective-permute-done.14 = bf16[4,96,768]{2,1,0:T(8,128)(2,1)S(1)} collective-permute-done((bf16[4,96,768]{2,1,0:T(8,128)(2,1)S(1)}, bf16[4,96,768]{2,1,0:T(8,128)(2,1)S(1)}, u32[]{:S(2)}, u32[]{:S(2)}) %collective-permute-start.14) | collective-permute-done | bytes 589856 | tf_op jit(solution)/shard_map/ppermute | solution.py:902
  119.2 16.1 %self_forward.1 = (bf16[1024,768]{1,0:T(8,128)(2,1)}, bf16[128,768]{1,0:T(8,128)(2,1)}, bf16[1024,1536]{1,0:T(8,128)(2,1)}, f32[128,128]{1,0:T(8,128)}, bf16[128...) custom-call(s32[5]{0:T(128)} %stack.110.refs_0_, ...), custom_call_target="tpu_custom_call" | custom-call | flops 16499999744 | bytes 10510356 | tf_op jit(solution)/shard_map/self_forward/pallas_call | solution.py:232
  139.7 7.2 %collective-permute-done.27 = bf16[2,96,768]{2,1,0:T(8,128)(2,1)S(1)} collective-permute-done((bf16[2,96,768]{2,1,0:T(8,128)(2,1)S(1)}, bf16[2,96,768]{2,1,0:T(8,128)(2,1)S(1)}, u32[]{:S(2)}, u32[]{:S(2)}) %collective-permute-start.27) | collective-permute-done | bytes 294944 | tf_op jit(solution)/shard_map/ppermute | solution.py:902
  149.7 11.6 %swin_forward.1 = (bf16[288,768]{1,0:T(8,128)(2,1)}, bf16[288,2304]{1,0:T(8,128)(2,1)}, f32[288,128]{1,0:T(8,128)}, bf16[288,768]{1,0:T(8,128)(2,1)}, f32[288,768]{1,0:T(8,128)}, /*index=5*/bf16[288,768]{1,0:T(8,128)(2,1)}) custom-call(s32[5]{0:T(128)} %stack.110.refs_0_, bf16[288,768]{1,0:T(8,128)(2,1)} %reshape.163.refs_1_, ...), custom_call_target="tpu_custom_call" | custom-call | flops 12099999744 | bytes 8871956 | tf_op jit(solution)/shard_map/swin_forward/pallas_call | solution.py:232
  173.3 21.1 %cross_forward.1 = (bf16[1024,768]{1,0:T(8,128)(2,1)}, bf16[1024,1536]{1,0:T(8,128)(2,1)}, bf16[1024,768]{1,0:T(8,128)(2,1)}, bf16[288,1536]{1,0:T(8,128)(2,1)},...) custom-call(s32[5]{0:T(128)} %stack.110.refs_0_, bf16[1024,768]{1,0:T(8,128)(2,1)} %all-gather.6.cloned.1.call-done.refs_1_.refs_3_, ...), custom_call_target="tpu_custom_call" | custom-call | flops 19800000512 | bytes 18087956 | tf_op jit(solution)/shard_map/cross_forward/pallas_call | solution.py:232
  198.3 11.7 %vq_forward.1 = (f32[288,128]{1,0:T(8,128)}, bf16[288,768]{1,0:T(8,128)(2,1)}) custom-call(s32[5]{0:T(128)} %stack.110.refs_0_, bf16[288,768]{1,0:T(8,128)(2,1)} %get-tuple-element.173.refs_1_, bf16[1024,1536]{1,0:T(8,128)(2,1)} %get-tuple-element.177.refs_2_), custom_call_target="tpu_custom_call" | custom-call | flops 12099999744 | bytes 4177940 | tf_op jit(solution)/shard_map/vq_forward/pallas_call | solution.py:232
  212.1 14.7 %mlp.1 = (bf16[288,768]{1,0:T(8,128)(2,1)}, bf16[288,768]{1,0:T(8,128)(2,1)}, bf16[288,3072]{1,0:T(8,128)(2,1)}, bf16[288,3072]{1,0:T(8,128)(2,1)}, f32[288,768]...) custom-call(s32[5]{0:T(128)} %stack.110.refs_0_, ...), custom_call_target="tpu_custom_call" | custom-call | flops 15399999488 | bytes 18607124 | tf_op jit(solution)/shard_map/mlp/pallas_call | solution.py:232
  230.2 11.6 %mlp_grads.1 = (bf16[2,16,96,768]{3,2,1,0:T(8,128)(2,1)}, bf16[2,16,96,768]{3,2,1,0:T(8,128)(2,1)}) custom-call(s32[5]{0:T(128)} %stack.110.refs_0_, bf16[288,768]{1,0:T(8,128)(2,1)} %get-tuple-element.182.refs_1_, bf16[288,3072]{1,0:T(8,128)(2,1)} %get-tuple-element.183.refs_2_, bf16[288,3072]{1,0:T(8,128)(2,1)} %get-tuple-element.184.refs_3_, ...), custom_call_target="tpu_custom_call" | custom-call | flops 14080000000 | bytes 13860864 | tf_op jit(solution)/shard_map/mlp_grads/pallas_call | solution.py:860
  243.0 16.0 %vq_backward.1 = (bf16[288,768]{1,0:T(8,128)(2,1)}, bf16[1536,1024]{1,0:T(8,128)(2,1)}) custom-call(s32[5]{0:T(128)} %stack.110.refs_0_, bf16[288,768]{1,0:T(8,128)(2,1)} %get-tuple-element.173.refs_1_, bf16[1024,1536]{1,0:T(8,128)(2,1)} %get-tuple-element.177.refs_2_, bf16[288,768]{1,0:T(8,128)(2,1)} %get-tuple-element.190.refs_3_, ...), custom_call_target="tpu_custom_call" | custom-call | flops 17600000000 | bytes 7766036 | tf_op jit(solution)/shard_map/vq_backward/pallas_call | solution.py:232
  265.8 22.6 %qv_backward.1 = (bf16[768,1024]{1,0:T(8,128)(2,1)}, bf16[288,1536]{1,0:T(8,128)(2,1)}, bf16[1024,1536]{1,0:T(8,128)(2,1)}) custom-call(s32[5]{0:T(128)} %stack.110.refs_0_, bf16[1024,768]{1,0:T(8,128)(2,1)} %get-tuple-element.196.refs_1_, bf16[288,1536]{1,0:T(8,128)(2,1)} %get-tuple-element.197.refs_2_, bf16[1024,768]{1,0:T(8,128)(2,1)} %get-tuple-element.198.refs_3_, ...), custom_call_target="tpu_custom_call" | custom-call | flops 25300000768 | bytes 16449556 | tf_op jit(solution)/shard_map/qv_backward/pallas_call | solution.py:232
  299.5 20.1 %swin_backward.1 = (bf16[288,768]{1,0:T(8,128)(2,1)}, bf16[288,2304]{1,0:T(8,128)(2,1)}, f32[288,768]{1,0:T(8,128)}, f32[2,768]{1,0:T(2,128)}) custom-call(s32[5]{0:T(128)} %stack.110.refs_0_, bf16[288,768]{1,0:T(8,128)(2,1)} %reshape.163.refs_1_, f32[288,768]{1,0:T(8,128)} %get-tuple-element.161.refs_1_.refs_2_, f32[288,768]{1,0:T(8,128)} %get-tuple-element.204.refs_3_, ...), custom_call_target="tpu_custom_call" | custom-call | flops 22000001024 | bytes 15955988 | tf_op jit(solution)/shard_map/swin_backward/pallas_call | solution.py:232
  322.3 14.0 %patch_grads.1 = (bf16[2,16,96,768]{3,2,1,0:T(8,128)(2,1)}, bf16[2,16,96,768]{3,2,1,0:T(8,128)(2,1)}) custom-call(s32[5]{0:T(128)} %stack.110.refs_0_, bf16[288,768]{1,0:T(8,128)(2,1)} %get-tuple-element.167.refs_2_.refs_1_.refs_3_, bf16[288,768]{1,0:T(8,128)(2,1)} %get-tuple-element.192.refs_6_.refs_2_, ...), custom_call_target="tpu_custom_call" | custom-call | flops 14080000000 | bytes 18579456 | tf_op jit(solution)/shard_map/patch_grads/pallas_call | solution.py:860
  353.2 16.8 %self_backward.1 = (f32[128,768]{1,0:T(8,128)}, bf16[128,768]{1,0:T(8,128)(2,1)}, bf16[128,768]{1,0:T(8,128)(2,1)}, bf16[1536,1024]{1,0:T(8,128)(2,1)}, f32[128,...) custom-call(s32[5]{0:T(128)} %stack.110.refs_0_, bf16[128,768]{1,0:T(8,128)(2,1)} %get-tuple-element.340.refs_1_, ...), custom_call_target="tpu_custom_call" | custom-call | flops 16499999744 | bytes 14841876 | tf_op jit(solution)/shard_map/self_backward/pallas_call | solution.py:232
  370.3 9.9 %collective-permute-done.45 = bf16[8,96,768]{2,1,0:T(8,128)(2,1)} collective-permute-done((bf16[8,96,768]{2,1,0:T(8,128)(2,1)S(1)}, bf16[8,96,768]{2,1,0:T(8,128)(2,1)}, u32[]{:S(2)}, u32[]{:S(2)}) %collective-permute-start.45) | collective-permute-done | bytes 1179680 | tf_op jit(solution)/shard_map/ppermute | solution.py:902
  384.9 14.8 %slot_grads.1 = (bf16[2,16,96,768]{3,2,1,0:T(8,128)(2,1)}, bf16[2,16,96,768]{3,2,1,0:T(8,128)(2,1)}) custom-call(s32[5]{0:T(128)} %stack.110.refs_0_, bf16[1024,768]{1,0:T(8,128)(2,1)} %all-gather.6.cloned.1.call-done.refs_1_.refs_3_, bf16[768,1024]{1,0:T(8,128)(2,1)} %get-tuple-element.200.refs_2_, ...), custom_call_target="tpu_custom_call" | custom-call | flops 14080000000 | bytes 19808256 | tf_op jit(solution)/shard_map/slot_grads/pallas_call | solution.py:860
  430.7 10.1 %collective-permute-done.56 = bf16[2,96,768]{2,1,0:T(8,128)(2,1)S(1)} collective-permute-done((bf16[2,96,768]{2,1,0:T(8,128)(2,1)}, bf16[2,96,768]{2,1,0:T(8,128)(2,1)S(1)}, u32[]{:S(2)}, u32[]{:S(2)}) %collective-permute-start.56) | collective-permute-done | bytes 294944 | tf_op jit(solution)/shard_map/ppermute | solution.py:902
  440.8 10.0 %collective-permute-done.57 = bf16[2,96,768]{2,1,0:T(8,128)(2,1)S(1)} collective-permute-done((bf16[2,96,768]{2,1,0:T(8,128)(2,1)}, bf16[2,96,768]{2,1,0:T(8,128)(2,1)S(1)}, u32[]{:S(2)}, u32[]{:S(2)}) %collective-permute-start.57) | collective-permute-done | bytes 294944 | tf_op jit(solution)/shard_map/ppermute | solution.py:902
  466.6 9.4 %collective-permute-done.60 = bf16[4,96,768]{2,1,0:T(8,128)(2,1)S(1)} collective-permute-done((bf16[4,96,768]{2,1,0:T(8,128)(2,1)}, bf16[4,96,768]{2,1,0:T(8,128)(2,1)S(1)}, u32[]{:S(2)}, u32[]{:S(2)}) %collective-permute-start.60) | collective-permute-done | bytes 589856 | tf_op jit(solution)/shard_map/ppermute | solution.py:902
  492.5 17.1 %collective-permute-done.63 = bf16[2,104,768]{2,1,0:T(8,128)(2,1)S(1)} collective-permute-done((bf16[2,104,768]{2,1,0:T(8,128)(2,1)S(1)}, bf16[2,104,768]{2,1,0:T(8,128)(2,1)S(1)}, u32[]{:S(2)}, u32[]{:S(2)}) %collective-permute-start.63) | collective-permute-done | bytes 319520 | tf_op jit(solution)/shard_map/ppermute | solution.py:902
  (366 shorter events, 198.1 us)
Async XLA Ops:
  7.2 66.9 %all-gather.8.cloned.1.call-start = ((), (), s32[]{:S(2)}) async-start(), calls=%async_computation.5 | async-start | bytes 3760128 | tf_op jit(solution)/shard_map/all_gather | solution.py:1034
  9.8 162.4 %all-gather.6.cloned.1.call-start = ((), (), s32[]{:S(2)}) async-start(), calls=%async_computation.2 | async-start | bytes 1769472 | tf_op jit(solution)/shard_map/all_gather | solution.py:1111
  61.9 27.1 %collective-permute-start.10 = (bf16[8,96,768]{2,1,0:T(8,128)(2,1)}, bf16[8,96,768]{2,1,0:T(8,128)(2,1)}, u32[]{:S(2)}, u32[]{:S(2)}) collective-permute-start(bf16[8,96,768]{2,1,0:T(8,128)(2,1)} %constant_dynamic-update-slice_fusion.6.refs_3_.refs_17_), channel_id=1, source_target_pairs={{0,2},{1,3},{2,0},{3,1},{4,6},{5,7},{6,4},{7,5},{8,10},{9,11},{10,... | collective-permute-start | bytes 3538952 | tf_op jit(solution)/shard_map/ppermute | solution.py:902
  68.2 30.7 %collective-permute-start.21 = (bf16[8,96,768]{2,1,0:T(8,128)(2,1)}, bf16[8,96,768]{2,1,0:T(8,128)(2,1)}, u32[]{:S(2)}, u32[]{:S(2)}) collective-permute-start(bf16[8,96,768]{2,1,0:T(8,128)(2,1)} %constant_dynamic-update-slice_fusion.6.refs_3_.refs_17_), channel_id=1, source_target_pairs={{0,1},{1,0},{2,3},{3,2},{4,5},{5,4},{6,7},{7,6},{8,9},{9,8},{10,11... | collective-permute-start | bytes 3538952 | tf_op jit(solution)/shard_map/ppermute | solution.py:902
  102.5 33.3 %collective-permute-start.26 = (bf16[2,96,768]{2,1,0:T(8,128)(2,1)S(1)}, bf16[2,96,768]{2,1,0:T(8,128)(2,1)}, u32[]{:S(2)}, u32[]{:S(2)}) collective-permute-start(bf16[2,96,768]{2,1,0:T(8,128)(2,1)S(1)} %pad_maximum_fusion.12), channel_id=1, source_target_pairs={{0,16},{8,24},{16,0},{24,8},{1,17},{9,25},{17,1},{25,9},{2,18},{10... | collective-permute-start | bytes 884744 | tf_op jit(solution)/shard_map/ppermute | solution.py:902
  116.0 31.1 %collective-permute-start.17 = (bf16[8,96,768]{2,1,0:T(8,128)(2,1)}, bf16[8,96,768]{2,1,0:T(8,128)(2,1)}, u32[]{:S(2)}, u32[]{:S(2)}) collective-permute-start(bf16[8,96,768]{2,1,0:T(8,128)(2,1)} %constant_dynamic-update-slice_fusion.10.refs_7_.refs_5_.refs_11_.refs_13_), channel_id=1, source_target_pairs={{0,2},{1,3},{2,0},{3,1},{4,6},{5,7},{6,4},{7,5},{8,10},{9,11},{10,... | collective-permute-start | bytes 3538952 | tf_op jit(solution)/shard_map/ppermute | solution.py:902
  117.4 29.7 %collective-permute-start.19 = (bf16[8,96,768]{2,1,0:T(8,128)(2,1)}, bf16[8,96,768]{2,1,0:T(8,128)(2,1)}, u32[]{:S(2)}, u32[]{:S(2)}) collective-permute-start(bf16[8,96,768]{2,1,0:T(8,128)(2,1)} %constant_dynamic-update-slice_fusion.10.refs_7_.refs_5_.refs_11_.refs_13_), channel_id=1, source_target_pairs={{0,1},{1,0},{2,3},{3,2},{4,5},{5,4},{6,7},{7,6},{8,9},{9,8},{10,11... | collective-permute-start | bytes 3538952 | tf_op jit(solution)/shard_map/ppermute | solution.py:902
  117.5 29.6 %collective-permute-start.16 = (bf16[8,96,768]{2,1,0:T(8,128)(2,1)S(1)}, bf16[8,96,768]{2,1,0:T(8,128)(2,1)S(1)}, u32[]{:S(2)}, u32[]{:S(2)}) collective-permute-start(bf16[8,96,768]{2,1,0:T(8,128)(2,1)S(1)} %constant_dynamic-update-slice_fusion.8.refs_3_.refs_7_.refs_9_.refs_8_), channel_id=1, source_target_pairs={{0,4},{1,5},{2,6},{3,7},{4,0},{5,1},{6,2},{7,3},{8,12},{9,13},{10,... | collective-permute-start | bytes 3538952 | tf_op jit(solution)/shard_map/ppermute | solution.py:902
  119.0 28.2 %collective-permute-start.18 = (bf16[8,96,768]{2,1,0:T(8,128)(2,1)S(1)}, bf16[8,96,768]{2,1,0:T(8,128)(2,1)}, u32[]{:S(2)}, u32[]{:S(2)}) collective-permute-start(bf16[8,96,768]{2,1,0:T(8,128)(2,1)S(1)} %constant_dynamic-update-slice_fusion.8.refs_3_.refs_7_.refs_9_.refs_8_), channel_id=1, source_target_pairs={{0,1},{1,0},{2,3},{3,2},{4,5},{5,4},{6,7},{7,6},{8,9},{9,8},{10,11... | collective-permute-start | bytes 3538952 | tf_op jit(solution)/shard_map/ppermute | solution.py:902
  135.4 91.5 %all-gather.10.cloned.1.call-start = ((), (), s32[]{:S(2)}) async-start(), calls=%async_computation.6 | async-start | bytes 1769472 | tf_op jit(solution)/shard_map/all_gather | solution.py:1168
  168.5 27.0 %collective-permute-start.31 = (bf16[8,96,768]{2,1,0:T(8,128)(2,1)S(1)}, bf16[8,96,768]{2,1,0:T(8,128)(2,1)}, u32[]{:S(2)}, u32[]{:S(2)}) collective-permute-start(bf16[8,96,768]{2,1,0:T(8,128)(2,1)S(1)} %constant_dynamic-update-slice_fusion.14.refs_13_), channel_id=1, source_target_pairs={{0,2},{1,3},{2,0},{3,1},{4,6},{5,7},{6,4},{7,5},{8,10},{9,11},{10,... | collective-permute-start | bytes 3538952 | tf_op jit(solution)/shard_map/ppermute | solution.py:902
  170.9 26.9 %collective-permute-start.30 = (bf16[8,96,768]{2,1,0:T(8,128)(2,1)}, bf16[8,96,768]{2,1,0:T(8,128)(2,1)}, u32[]{:S(2)}, u32[]{:S(2)}) collective-permute-start(bf16[8,96,768]{2,1,0:T(8,128)(2,1)} %constant_dynamic-update-slice_fusion.12.refs_9_), channel_id=1, source_target_pairs={{0,4},{1,5},{2,6},{3,7},{4,0},{5,1},{6,2},{7,3},{8,12},{9,13},{10,... | collective-permute-start | bytes 3538952 | tf_op jit(solution)/shard_map/ppermute | solution.py:902
  194.4 150.5 %reduce-scatter.3.cloned.1.call-start = ((), (), s32[]{:S(2)}) async-start(), calls=%async_computation.3 | async-start | bytes 3538944 | tf_op jit(solution)/shard_map/reduce_scatter | solution.py:978
  263.8 32.6 %collective-permute-start.41 = (bf16[8,96,768]{2,1,0:T(8,128)(2,1)S(1)}, bf16[8,96,768]{2,1,0:T(8,128)(2,1)}, u32[]{:S(2)}, u32[]{:S(2)}) collective-permute-start(bf16[8,96,768]{2,1,0:T(8,128)(2,1)S(1)} %get-tuple-element.289), channel_id=1, source_target_pairs={{0,4},{1,5},{2,6},{3,7},{4,0},{5,1},{6,2},{7,3},{8,12},{9,13},{10,... | collective-permute-start | bytes 3538952 | tf_op jit(solution)/shard_map/ppermute | solution.py:902
  265.1 28.2 %collective-permute-start.40 = (bf16[8,96,768]{2,1,0:T(8,128)(2,1)}, bf16[8,96,768]{2,1,0:T(8,128)(2,1)}, u32[]{:S(2)}, u32[]{:S(2)}) collective-permute-start(bf16[8,96,768]{2,1,0:T(8,128)(2,1)} %get-tuple-element.290), channel_id=1, source_target_pairs={{0,2},{1,3},{2,0},{3,1},{4,6},{5,7},{6,4},{7,5},{8,10},{9,11},{10,... | collective-permute-start | bytes 3538952 | tf_op jit(solution)/shard_map/ppermute | solution.py:902
  288.4 174.4 %reduce-scatter.5.cloned.1.call-start = ((), (), s32[]{:S(2)}) async-start(), calls=%async_computation.4 | async-start | bytes 1880064 | tf_op jit(solution)/shard_map/reduce_scatter | solution.py:978
  339.4 30.6 %collective-permute-start.49 = (bf16[2,96,768]{2,1,0:T(8,128)(2,1)S(1)}, bf16[2,96,768]{2,1,0:T(8,128)(2,1)S(1)}, u32[]{:S(2)}, u32[]{:S(2)}) collective-permute-start(bf16[2,96,768]{2,1,0:T(8,128)(2,1)S(1)} %copy-done.20), channel_id=1, source_target_pairs={{0,24},{8,16},{16,8},{24,0},{1,25},{9,17},{17,9},{25,1},{2,26},{10... | collective-permute-start | bytes 884744 | tf_op jit(solution)/shard_map/ppermute | solution.py:902
  342.4 27.7 %collective-permute-start.48 = (bf16[2,96,768]{2,1,0:T(8,128)(2,1)S(1)}, bf16[2,96,768]{2,1,0:T(8,128)(2,1)S(1)}, u32[]{:S(2)}, u32[]{:S(2)}) collective-permute-start(bf16[2,96,768]{2,1,0:T(8,128)(2,1)S(1)} %copy-done.19), channel_id=1, source_target_pairs={{0,16},{8,24},{16,0},{24,8},{1,17},{9,25},{17,1},{25,9},{2,18},{10... | collective-permute-start | bytes 884744 | tf_op jit(solution)/shard_map/ppermute | solution.py:902
  351.1 29.0 %collective-permute-start.45 = (bf16[8,96,768]{2,1,0:T(8,128)(2,1)S(1)}, bf16[8,96,768]{2,1,0:T(8,128)(2,1)}, u32[]{:S(2)}, u32[]{:S(2)}) collective-permute-start(bf16[8,96,768]{2,1,0:T(8,128)(2,1)S(1)} %get-tuple-element.286), channel_id=1, source_target_pairs={{0,2},{1,3},{2,0},{3,1},{4,6},{5,7},{6,4},{7,5},{8,10},{9,11},{10,... | collective-permute-start | bytes 3538952 | tf_op jit(solution)/shard_map/ppermute | solution.py:902
  352.5 30.0 %collective-permute-start.46 = (bf16[8,96,768]{2,1,0:T(8,128)(2,1)S(1)}, bf16[8,96,768]{2,1,0:T(8,128)(2,1)}, u32[]{:S(2)}, u32[]{:S(2)}) collective-permute-start(bf16[8,96,768]{2,1,0:T(8,128)(2,1)S(1)} %get-tuple-element.285), channel_id=1, source_target_pairs={{0,4},{1,5},{2,6},{3,7},{4,0},{5,1},{6,2},{7,3},{8,12},{9,13},{10,... | collective-permute-start | bytes 3538952 | tf_op jit(solution)/shard_map/ppermute | solution.py:902
  370.0 29.6 %collective-permute-start.50 = (bf16[6,24,768]{2,1,0:T(8,128)(2,1)S(1)}, bf16[6,24,768]{2,1,0:T(8,128)(2,1)S(1)}, u32[]{:S(2)}, u32[]{:S(2)}) collective-permute-start(bf16[6,24,768]{2,1,0:T(8,128)(2,1)S(1)} %fusion.25), channel_id=1, source_target_pairs={{0,1},{1,2},{2,3},{3,4},{4,5},{5,6},{6,7},{7,0},{8,9},{9,10},{10,1... | collective-permute-start | bytes 663560 | tf_op jit(solution)/shard_map/ppermute | solution.py:1196
  422.7 33.9 %collective-permute-start.55 = (bf16[8,96,768]{2,1,0:T(8,128)(2,1)}, bf16[8,96,768]{2,1,0:T(8,128)(2,1)}, u32[]{:S(2)}, u32[]{:S(2)}) collective-permute-start(bf16[8,96,768]{2,1,0:T(8,128)(2,1)} %get-tuple-element.248), channel_id=1, source_target_pairs={{0,4},{1,5},{2,6},{3,7},{4,0},{5,1},{6,2},{7,3},{8,12},{9,13},{10,... | collective-permute-start | bytes 3538952 | tf_op jit(solution)/shard_map/ppermute | solution.py:902
  423.5 35.5 %collective-permute-start.54 = (bf16[8,96,768]{2,1,0:T(8,128)(2,1)}, bf16[8,96,768]{2,1,0:T(8,128)(2,1)}, u32[]{:S(2)}, u32[]{:S(2)}) collective-permute-start(bf16[8,96,768]{2,1,0:T(8,128)(2,1)} %get-tuple-element.246), channel_id=1, source_target_pairs={{0,2},{1,3},{2,0},{3,1},{4,6},{5,7},{6,4},{7,5},{8,10},{9,11},{10,... | collective-permute-start | bytes 3538952 | tf_op jit(solution)/shard_map/ppermute | solution.py:902
  481.7 27.9 %collective-permute-start.63 = (bf16[2,104,768]{2,1,0:T(8,128)(2,1)S(1)}, bf16[2,104,768]{2,1,0:T(8,128)(2,1)S(1)}, u32[]{:S(2)}, u32[]{:S(2)}) collective-permute-start(bf16[2,104,768]{2,1,0:T(8,128)(2,1)S(1)} %fusion.32), channel_id=1, source_target_pairs={{0,16},{8,24},{16,0},{24,8},{1,17},{9,25},{17,1},{25,9},{2,18},{10... | collective-permute-start | bytes 958472 | tf_op jit(solution)/shard_map/ppermute | solution.py:902
  (78 other events, 993.1 us)
Sparse Core Ops, SparseCore 0:
  10.5 43.7 all-gather.7
  135.5 30.0 all-gather.5
  194.5 27.9 all-gather.9
  288.5 49.2 reduce-scatter.2
  403.0 45.2 reduce-scatter.4
